TPU v7x, 32 devices: a whole 2x2x4 slice. The times are simulated.
32 devices in a mesh: space: 16 (over z, y, x), wt: 2 (over core).
Axes of the slice: x: 2, y: 2, z: 4, core: 2. Of those that a mesh axis runs over, the one named last changes fastest.
Arguments:
- features: bfloat16 [32, 8, 8, 8, 192], P(('space', 'wt')), may hold values from -6 to 6
- occupancy: int32 [32], P(('space', 'wt')), may hold values from 0 to 1, as said below
- neighbours: int32 [32, 27], P(('space', 'wt')), may hold values from -1 to 31, as said below
- kernel_one: bfloat16 [3, 3, 3, 48, 768], P(None, None, None, None, 'wt'), may hold values from -0.078125 to 0.078125
- kernel_two: bfloat16 [3, 3, 3, 48, 768], P(None, None, None, None, 'wt'), may hold values from -0.078125 to 0.078125
Outputs:
- block_out: float32 [32, 8, 8, 8, 192], P(('space', 'wt'))
Inputs may be any that keep to these rules, and one draw needn't show every extreme that they name: `occupancy`: the first slot of every device's 1 slots is active; the others are active with probability three quarters. `neighbours`: entries are -1 or an active slot; for an active slot s, entry 13 is s itself, and every other entry lies among the slots of the same device, the previous or the next device in slot order (slots d * 1 to (d+1) - 1 belong to device d). Rows of inactive slots are all -1.
All inputs are finite; a program needn't handle non-finite values.
Results may differ from a plain program's by a relative error of at most 0.0018.
Values may be sent and summed in bfloat16 or wider, within the bound.
No kernel may reach another device: no remote copies, remote signals or barrier semaphores. Data moves between devices by JAX's collectives and lax.ppermute only.
A program may use at most 64 MiB of HBM per device.

v0:
```python
import jax
import jax.numpy as jnp
from jax import lax
from jax.sharding import PartitionSpec as P

C = 192


def extended(value, sides, width):
    for axis, dim in sides:
        size, length = (lax.axis_size(axis), value.shape[dim])
        up = [(i, (i + 1) % size) for i in range(size - 1)]
        down = [(j, i) for i, j in up]
        last = lax.slice_in_dim(value, length - width, length, axis=dim)
        leading = lax.slice_in_dim(value, 0, width, axis=dim)
        before = lax.ppermute(last, axis, up)
        after = lax.ppermute(leading, axis, down)
        value = jnp.concatenate([before, value, after], axis=dim)
    return value


def unpack_kernel(stored):
    quarter = stored.shape[3]
    width = C
    groups = stored.shape[4] // width
    grouped = stored.reshape(3, 3, 3, quarter, groups, width)
    return jnp.transpose(grouped, (0, 1, 2, 4, 3, 5)).reshape(3, 3, 3, groups * quarter, width)


def pad_blocks(source, index):
    ranges = ((7, 8), (0, 8), (0, 1))
    planes = []
    for first in range(3):
        rows = []
        for second in range(3):
            cols = []
            for third in range(3):
                tap = first * 9 + second * 3 + third
                which = index[:, tap]
                picked = jnp.take(source, jnp.maximum(which, 0), axis=0)
                lo_a, hi_a = ranges[first]
                lo_b, hi_b = ranges[second]
                lo_c, hi_c = ranges[third]
                piece = picked[:, lo_a:hi_a, lo_b:hi_b, lo_c:hi_c, :]
                valid = (which >= 0)[:, None, None, None, None]
                cols.append(jnp.where(valid, piece, jnp.zeros((), piece.dtype)))
            rows.append(jnp.concatenate(cols, axis=3))
        planes.append(jnp.concatenate(rows, axis=2))
    return jnp.concatenate(planes, axis=1)


def conv_taps(padded, kernel):
    return lax.conv_general_dilated(
        padded,
        kernel,
        (1, 1, 1),
        "VALID",
        dimension_numbers=("NDHWC", "DHWIO", "NDHWC"),
        preferred_element_type=jnp.float32,
    )


def padded_field(source, local_index):
    count = source.shape[0]
    beside_all = extended(source, ((("space", "wt"), 0),), count)
    return pad_blocks(beside_all, local_index)


def convolve(padded, kernel):
    gathered = lax.all_gather(kernel, "wt", axis=4, tiled=True)
    return conv_taps(padded, unpack_kernel(gathered))


def body(features, occupancy, neighbours, kernel_one, kernel_two):
    count = features.shape[0]
    device = lax.axis_index(("space", "wt"))
    local_index = jnp.where(neighbours >= 0, neighbours - (device - 1) * count, -1)
    active = occupancy.astype(jnp.float32)[:, None, None, None, None]
    hidden = (
        jax.nn.relu(convolve(padded_field(features, local_index), kernel_one)) * active
    ).astype(jnp.bfloat16)
    second = convolve(padded_field(hidden, local_index), kernel_two)
    return jax.nn.relu(features.astype(jnp.float32) + second) * active


def solution(mesh):
    return jax.shard_map(
        body,
        mesh=mesh,
        in_specs=(
            P(("space", "wt"), None, None, None, None),
            P(("space", "wt")),
            P(("space", "wt"), None),
            P(None, None, None, None, "wt"),
            P(None, None, None, None, "wt"),
        ),
        out_specs=P(("space", "wt"), None, None, None, None),
        check_vma=False,
    )
```

profile of v0, /device:TPU:8, one launch (start us, length us, event | category | flops | bytes accessed | tf_op | source)
XLA Modules:
  0.0 99.1 jit_solution(6766696011851365854)
XLA Ops:
  6.5 0.0 copy-start
  6.5 0.0 copy-start.2
  6.5 0.0 all-gather.3.cloned.1.call-start
  6.5 0.7 all-gather.3.cloned.1.call-update
  7.3 0.0 all-gather.5.cloned.1.call-start
  7.3 1.9 %collective-permute-start = (bf16[1,8,8,8,192]{4,3,2,1,0:T(8,128)(2,1)}, bf16[1,8,8,8,192]{4,3,2,1,0:T(8,128)(2,1)S(1)}, u32[]{:S(2)}, u32[]{:S(2)}) collective-permute-start(bf16[1,8,8,8,192]{4,3,2,1,0:T(8,128)(2,1)} %param.7), channel_id=1, source_target_pairs={{0,1},{1,2},{2,3},{3,4},{4,5},{5,6},{6,7},{7,8},{8,9},{9,10},{10,1... | collective-permute-start | bytes 589832 | tf_op jit(solution)/shard_map/ppermute | solution.py:16
  9.2 5.4 %collective-permute-start.1 = (bf16[1,8,8,8,192]{4,3,2,1,0:T(8,128)(2,1)}, bf16[1,8,8,8,192]{4,3,2,1,0:T(8,128)(2,1)S(1)}, u32[]{:S(2)}, u32[]{:S(2)}) collective-permute-start(bf16[1,8,8,8,192]{4,3,2,1,0:T(8,128)(2,1)} %param.7), channel_id=1, source_target_pairs={{1,0},{2,1},{3,2},{4,3},{5,4},{6,5},{7,6},{8,7},{9,8},{10,9},{11,1... | collective-permute-start | bytes 589832 | tf_op jit(solution)/shard_map/ppermute | solution.py:17
  14.7 0.0 all-gather.5.cloned.1.call-update
  14.7 0.0 copy-done.2
  14.7 0.7 fusion.32
  28.1 0.7 fusion.33
  50.9 0.0 collective-permute-done
  50.9 0.0 copy-done
  51.0 0.0 collective-permute-done.1
  51.0 0.1 broadcast_select_fusion.35
  51.1 0.1 broadcast_select_fusion.39
  51.3 0.2 broadcast_select_fusion.7
  51.5 1.5 %maximum_maximum_fusion = bf16[1,10,10,10,192]{4,3,2,1,0:T(8,128)(2,1)} fusion(bf16[1,1,1,1,192]{4,3,2,1,0:T(2,128)(2,1)S(1)} %get-tuple-element.44, bf16[1,1,1,8,192]{4,3,2,1,0:T(8,128)(2,1)S(1)} %get-tuple-element.49, bf16[1,1,1,1,192]{4,3,2,1,0:T(2,128)(2,1)S(1)} %get-tuple-element.45, bf16[1,1,8,1,192]{4,3,2,1,0:T(2,128)(2,1)S(1)} %get-tuple-element.56, ...), kind=kLoop, calls=%fused_computation.4 | loop fusion | flops 10368000 | bytes 768000 | tf_op jit(solution)/shard_map/concatenate | solution.py:49
  53.1 0.0 all-gather.3.cloned.1.call-done
  53.1 5.2 %reshape.242 = bf16[3,3,3,48,4,192]{5,4,3,2,1,0:T(4,128)(2,1)S(1)} reshape(bf16[3,3,3,48,768]{4,3,2,1,0:T(8,128)(2,1)} %all-gather.3.cloned.1.call-done) | data formatting | bytes 3981312 | tf_op jit(solution)/shard_map/reshape | solution.py:26
  58.3 0.0 copy-start.1
  58.3 0.5 copy.13
  58.8 0.7 copy-done.1
  59.4 8.0 %fusion.2 = f32[1,8,8,8,192]{4,0,3,2,1:T(1,128)S(1)} fusion(bf16[3,3,3,192,192]{4,3,2,1,0:T(8,128)(2,1)S(1)} %bitcast.122, bf16[1,10,10,10,192]{4,3,2,1,0:T(8,128)(2,1)S(1)} %copy-done.1), kind=kOutput, calls=%fused_computation.2 | convolution fusion | flops 1019215872 | bytes 2767872 | tf_op jit(solution)/shard_map/conv_general_dilated | solution.py:53
  67.4 0.1 fusion.7
  67.5 1.9 %collective-permute-start.2 = (bf16[1,8,8,8,192]{4,3,2,1,0:T(8,128)(2,1)S(1)}, bf16[1,8,8,8,192]{4,3,2,1,0:T(8,128)(2,1)S(1)}, u32[]{:S(2)}, u32[]{:S(2)}) collective-permute-start(bf16[1,8,8,8,192]{4,3,2,1,0:T(8,128)(2,1)S(1)} %fusion.7), channel_id=1, source_target_pairs={{0,1},{1,2},{2,3},{3,4},{4,5},{5,6},{6,7},{7,8},{8,9},{9,10},{10,1... | collective-permute-start | bytes 589832 | tf_op jit(solution)/shard_map/ppermute | solution.py:16
  69.4 5.6 %collective-permute-start.3 = (bf16[1,8,8,8,192]{4,3,2,1,0:T(8,128)(2,1)S(1)}, bf16[1,8,8,8,192]{4,3,2,1,0:T(8,128)(2,1)}, u32[]{:S(2)}, u32[]{:S(2)}) collective-permute-start(bf16[1,8,8,8,192]{4,3,2,1,0:T(8,128)(2,1)S(1)} %fusion.7), channel_id=1, source_target_pairs={{1,0},{2,1},{3,2},{4,3},{5,4},{6,5},{7,6},{8,7},{9,8},{10,9},{11,1... | collective-permute-start | bytes 589832 | tf_op jit(solution)/shard_map/ppermute | solution.py:17
  75.1 0.0 all-gather.5.cloned.1.call-done
  75.1 5.2 %reshape.244 = bf16[3,3,3,48,4,192]{5,4,3,2,1,0:T(4,128)(2,1)S(1)} reshape(bf16[3,3,3,48,768]{4,3,2,1,0:T(8,128)(2,1)} %all-gather.5.cloned.1.call-done) | data formatting | bytes 3981312 | tf_op jit(solution)/shard_map/reshape | solution.py:26
  80.3 0.5 copy.16
  80.8 0.0 collective-permute-done.2
  80.8 0.0 collective-permute-done.3
  80.8 1.1 %pad_maximum_fusion = bf16[3,8,8,8,192]{4,3,2,1,0:T(8,128)(2,1)S(1)} fusion(bf16[1,8,8,8,192]{4,3,2,1,0:T(8,128)(2,1)} %collective-permute-done.3, bf16[1,8,8,8,192]{4,3,2,1,0:T(8,128)(2,1)S(1)} %fusion.7, bf16[1,8,8,8,192]{4,3,2,1,0:T(8,128)(2,1)S(1)} %collective-permute-done.2), kind=kLoop, calls=%fused_computation.6 | loop fusion | flops 589824 | bytes 1179648 | tf_op jit(solution)/shard_map/concatenate | solution.py:18
  82.0 0.2 broadcast_select_fusion.6
  82.3 0.1 broadcast_select_fusion.34
  82.4 0.1 broadcast_select_fusion.38
  82.5 0.7 maximum_maximum_fusion.1
  83.3 8.1 %fusion = f32[1,8,8,8,192]{4,0,3,2,1:T(1,128)S(1)} fusion(bf16[3,3,3,192,192]{4,3,2,1,0:T(8,128)(2,1)S(1)} %bitcast.121, bf16[1,10,10,10,192]{4,3,2,1,0:T(8,128)(2,1)S(1)} %maximum_maximum_fusion.1), kind=kOutput, calls=%fused_computation | convolution fusion | flops 1019215872 | bytes 2767872 | tf_op jit(solution)/shard_map/conv_general_dilated | solution.py:53
  91.3 0.9 fusion.5
  (16 shorter events, 0.4 us)
Async XLA Ops:
  6.5 44.4 %copy-start = (bf16[1,8,8,8,192]{4,3,2,1,0:T(8,128)(2,1)S(1)}, bf16[1,8,8,8,192]{4,3,2,1,0:T(8,128)(2,1)}, u32[]{:S(2)}) copy-start(bf16[1,8,8,8,192]{4,3,2,1,0:T(8,128)(2,1)} %param.7) | copy-start | bytes 589828
  6.5 8.2 %copy-start.2 = (s32[1,27]{1,0:T(1,128)S(1)}, s32[1,27]{1,0:T(1,128)}, u32[]{:S(2)}) copy-start(s32[1,27]{1,0:T(1,128)} %param.9) | copy-start | bytes 328
  6.5 46.5 %all-gather.3.cloned.1.call-start = ((), (), s32[]{:S(2)}) async-start(), calls=%async_computation | async-start | bytes 2985984 | tf_op jit(solution)/shard_map/all_gather | solution.py:70
  7.3 67.8 %all-gather.5.cloned.1.call-start = ((), (), s32[]{:S(2)}) async-start(), calls=%async_computation.1 | async-start | bytes 2985984 | tf_op jit(solution)/shard_map/all_gather | solution.py:70
  7.3 43.6 %collective-permute-start = (bf16[1,8,8,8,192]{4,3,2,1,0:T(8,128)(2,1)}, bf16[1,8,8,8,192]{4,3,2,1,0:T(8,128)(2,1)S(1)}, u32[]{:S(2)}, u32[]{:S(2)}) collective-permute-start(bf16[1,8,8,8,192]{4,3,2,1,0:T(8,128)(2,1)} %param.7), channel_id=1, source_target_pairs={{0,1},{1,2},{2,3},{3,4},{4,5},{5,6},{6,7},{7,8},{8,9},{9,10},{10,1... | collective-permute-start | bytes 589832 | tf_op jit(solution)/shard_map/ppermute | solution.py:16
  9.2 41.7 %collective-permute-start.1 = (bf16[1,8,8,8,192]{4,3,2,1,0:T(8,128)(2,1)}, bf16[1,8,8,8,192]{4,3,2,1,0:T(8,128)(2,1)S(1)}, u32[]{:S(2)}, u32[]{:S(2)}) collective-permute-start(bf16[1,8,8,8,192]{4,3,2,1,0:T(8,128)(2,1)} %param.7), channel_id=1, source_target_pairs={{1,0},{2,1},{3,2},{4,3},{5,4},{6,5},{7,6},{8,7},{9,8},{10,9},{11,1... | collective-permute-start | bytes 589832 | tf_op jit(solution)/shard_map/ppermute | solution.py:17
  58.3 1.1 %copy-start.1 = (bf16[1,10,10,10,192]{4,3,2,1,0:T(8,128)(2,1)S(1)}, bf16[1,10,10,10,192]{4,3,2,1,0:T(8,128)(2,1)}, u32[]{:S(2)}) copy-start(bf16[1,10,10,10,192]{4,3,2,1,0:T(8,128)(2,1)} %maximum_maximum_fusion) | copy-start | bytes 1152004
  67.5 13.3 %collective-permute-start.2 = (bf16[1,8,8,8,192]{4,3,2,1,0:T(8,128)(2,1)S(1)}, bf16[1,8,8,8,192]{4,3,2,1,0:T(8,128)(2,1)S(1)}, u32[]{:S(2)}, u32[]{:S(2)}) collective-permute-start(bf16[1,8,8,8,192]{4,3,2,1,0:T(8,128)(2,1)S(1)} %fusion.7), channel_id=1, source_target_pairs={{0,1},{1,2},{2,3},{3,4},{4,5},{5,6},{6,7},{7,8},{8,9},{9,10},{10,1... | collective-permute-start | bytes 589832 | tf_op jit(solution)/shard_map/ppermute | solution.py:16
  69.4 11.4 %collective-permute-start.3 = (bf16[1,8,8,8,192]{4,3,2,1,0:T(8,128)(2,1)S(1)}, bf16[1,8,8,8,192]{4,3,2,1,0:T(8,128)(2,1)}, u32[]{:S(2)}, u32[]{:S(2)}) collective-permute-start(bf16[1,8,8,8,192]{4,3,2,1,0:T(8,128)(2,1)S(1)} %fusion.7), channel_id=1, source_target_pairs={{1,0},{2,1},{3,2},{4,3},{5,4},{6,5},{7,6},{8,7},{9,8},{10,9},{11,1... | collective-permute-start | bytes 589832 | tf_op jit(solution)/shard_map/ppermute | solution.py:17
Sparse Core Ops, SparseCore 0:
  8.9 11.7 all-gather.2
  22.3 11.5 all-gather.4
where the time goes:
time: 100 us; the launch traced here: 99.1 us
  between operations  48.5 us (48%)
  matrix products  16 us (16%)
  starting transfers between devices  14.9 us (15%)
  local copies, waits for them, and re-layouts  13.6 us (14%)
  other arithmetic  5.28 us (5%)
    conv_general_dilated x2, matrix products, conv_taps(): lax.conv_general_dilated(padded, kernel, (1, 1, 1), 'VALID', dimension_nu...  16 us
    reshape x4, local copies, waits for them, and re-layouts, unpack_kernel(): grouped = stored.reshape(3, 3, 3, quarter, groups, width)  11.4 us
    ppermute x2, starting transfers between devices, extended(): after = lax.ppermute(leading, axis, down)  11.1 us
    ppermute x2, starting transfers between devices, extended(): before = lax.ppermute(last, axis, up)  3.84 us
    concatenate x2, other arithmetic, pad_blocks(): return jnp.concatenate(planes, axis=1)  2.25 us
  transfers between devices with their start and end apart: 6, of which 0 were waited for; matrix products, arithmetic and copies ran while one was open for 23% of the time, Pallas kernels for 0%

commit v1 on v0

v1 whole, which is shorter than its diff:
```python
import functools

import jax
import jax.numpy as jnp
from jax import lax
from jax.experimental import pallas as pl
from jax.experimental.pallas import tpu as pltpu
from jax.sharding import PartitionSpec as P

AXES = ("space", "wt")
VMEM = pltpu.VMEM
SMEM = pltpu.SMEM


def surface_rows(side):
    plane = side * side
    inner = (side - 2) * side
    return 2 * plane + 4 * inner


LANES = 128


def pieces(width):
    return [(p, p * LANES, min(LANES, width - p * LANES)) for p in range(-(-width // LANES))]


def fill(wide, base, value):
    rows, width = value.shape
    for p, lane, lanes in pieces(width):
        wide[p, pl.ds(base, rows), 0:lanes] = value[:, lane : lane + lanes]


def pack_surface(wide, base, out_ref, side):
    plane = side * side
    inner = (side - 2) * side
    last = side - 1

    for p, lane, lanes in pieces(out_ref.shape[1]):
        ref = wide.at[p]

        def store(row, value):
            out_ref[pl.ds(row, value.shape[0]), lane : lane + lanes] = value[
                :, :lanes
            ].astype(jnp.bfloat16)

        store(0, ref[pl.ds(base, plane), :])
        store(plane, ref[pl.ds(base + last * plane, plane), :])
        row = 2 * plane
        for y in (0, last):
            parts = [
                ref[pl.ds(base + x * plane + y * side, side), :]
                for x in range(1, last)
            ]
            store(row, jnp.concatenate(parts, axis=0))
            row += inner
        for z in (0, last):
            store(row, ref[pl.ds(base + plane + z, inner, stride=side), :])
            row += inner


def unpack_surface(far_ref, wide, base, side):
    plane = side * side
    inner = (side - 2) * side
    last = side - 1
    far = far_ref[...].astype(jnp.float32)
    for p, lane, lanes in pieces(far.shape[1]):
        ref = wide.at[p]
        part = far[:, lane : lane + lanes]
        if lanes < LANES:
            pad = jnp.zeros((far.shape[0], LANES - lanes), jnp.float32)
            part = jnp.concatenate([part, pad], axis=1)
        ref[pl.ds(base, plane), :] = part[0:plane]
        ref[pl.ds(base + last * plane, plane), :] = part[plane : 2 * plane]
        row = 2 * plane
        for y in (0, last):
            for x in range(1, last):
                at = row + (x - 1) * side
                ref[pl.ds(base + x * plane + y * side, side), :] = part[at : at + side]
            row += inner
        for z in (0, last):
            ref[pl.ds(base + plane + z, inner, stride=side), :] = part[
                row : row + inner
            ]
            row += inner


def pack_kernel(x_ref, out_ref, wide, *, side):
    fill(wide, 0, x_ref[...].astype(jnp.float32))
    pack_surface(wide, 0, out_ref, side)


def weights_kernel(own_ref, other_ref, out_ref):
    core = lax.axis_index("wt")
    taps, depth, both = own_ref.shape
    width = out_ref.shape[2]
    half = depth * (both // width)
    for ref, place in ((own_ref, core), (other_ref, 1 - core)):
        for group in range(both // width):
            row = pl.multiple_of(place * half + group * depth, 16)
            out_ref[:, pl.ds(row, depth), :] = ref[
                :, :, group * width : (group + 1) * width
            ]


def conv(table, block, center, beside, far_ref, w_ref, src, even, odd, side):
    rows, width = center.shape
    plane = side * side
    last = side - 1
    fill(src, 0, jnp.zeros((rows, width), jnp.float32))
    fill(src, rows, beside[...].astype(jnp.float32))
    fill(src, 2 * rows, center[...].astype(jnp.float32))
    unpack_surface(far_ref, src, 3 * rows, side)

    def slot(a, b, c):
        if (a, b, c) == (0, 0, 0):
            return 2
        n = table[0, 9 * (a + 1) + 3 * (b + 1) + c + 1]
        near = jnp.where(n == block, 2, jnp.where(n == block + 1 - 2 * (block % 2), 1, 3))
        return jnp.where(n < 0, 0, near)

    slots = {
        (a, b, c): slot(a, b, c)
        for a in (-1, 0, 1)
        for b in (-1, 0, 1)
        for c in (-1, 0, 1)
    }

    def span(index):
        if index == 0:
            return -1, last
        if index == side + 1:
            return 1, 0
        return 0, index - 1

    z = lax.broadcasted_iota(jnp.int32, (side, side, LANES), 1)
    for xx in range(side + 2):
        a, x = span(xx)
        for b, y, count, to in ((-1, last, 1, 0), (0, 0, side, 1), (1, 0, 1, side + 1)):
            for p, lane, lanes in pieces(width):

                def chunk(c):
                    start = slots[a, b, c] * rows + x * plane + y * side
                    if not isinstance(start, int):
                        start = pl.multiple_of(start, side)
                    return src[p, pl.ds(start, count * side), :].reshape(
                        count, side, LANES
                    )

                middle = chunk(0)
                mask = z[:count]
                low = jnp.where(mask == last, chunk(-1), middle)
                high = jnp.where(mask == 0, chunk(1), middle)
                shifted = (
                    pltpu.roll(low, 1, axis=1),
                    middle,
                    pltpu.roll(high, side - 1, axis=1),
                )
                for k in range(3):
                    value = shifted[k].reshape(count * side, LANES)[:, :lanes]
                    even[
                        k, xx, pl.ds(to * side, count * side), lane : lane + lanes
                    ] = value
                    if b == 0:
                        odd[k, xx, :, lane : lane + lanes] = value.astype(jnp.bfloat16)


def conv_sum(even, evenb, odd, w_ref, rows, width, side):
    plane = side * side
    evenb[...] = even[...].astype(jnp.bfloat16)
    acc = jnp.zeros((rows, width), jnp.float32)
    for i in range(3):
        for j in range(3):
            for k in range(3):
                if j == 1:
                    part = odd[k, i : i + side]
                else:
                    part = evenb[k, i : i + side, j * side : j * side + plane]
                acc += jnp.dot(
                    part.reshape(rows, width),
                    w_ref[9 * i + 3 * j + k],
                    preferred_element_type=jnp.float32,
                )
    return acc


def first_kernel(
    table, occupancy, center, beside, far, w, out, surface, src, even, evenb, odd, *, side
):
    core = lax.axis_index("wt")
    block = 2 * lax.axis_index("space") + 1 - core
    rows, width = center.shape
    conv(table, block, center, beside, far, w, src, even, odd, side)
    acc = conv_sum(even, evenb, odd, w, rows, width, side)
    hidden = jnp.maximum(acc, 0.0) * occupancy[0, 0].astype(jnp.float32)
    out[...] = hidden.astype(jnp.bfloat16)
    fill(src, 0, hidden)
    pack_surface(src, 0, surface, side)


def second_kernel(
    table, occupancy, center, beside, far, w, features, out, src, even, evenb, odd, *, side
):
    block = 2 * lax.axis_index("space") + lax.axis_index("wt")
    rows, width = center.shape
    conv(table, block, center, beside, far, w, src, even, odd, side)
    acc = conv_sum(even, evenb, odd, w, rows, width, side)
    total = jnp.maximum(features[...].astype(jnp.float32) + acc, 0.0)
    out[...] = total * occupancy[0, 0].astype(jnp.float32)


def params(flops=0, moved=0):
    return dict(
        compiler_params=pltpu.CompilerParams(vmem_limit_bytes=40 * 2**20),
        cost_estimate=pl.CostEstimate(
            flops=flops, bytes_accessed=moved, transcendentals=0
        ),
    )


def vmem(count):
    return [pl.BlockSpec(memory_space=VMEM)] * count


def smem(count):
    return [pl.BlockSpec(memory_space=SMEM)] * count


def body(features, occupancy, neighbours, kernel_one, kernel_two):
    side, width = features.shape[1], features.shape[4]
    rows = side**3
    total = lax.axis_size(AXES)
    halves = [(i, i ^ 1) for i in range(total)]
    cycle = [(i, i - 2) if i % 2 == 0 else (i, i + 2) for i in range(total)]
    cycle[0], cycle[-1] = (0, 1), (total - 1, total - 2)
    back = [(j, i) for i, j in cycle]
    surface = surface_rows(side)

    own = features.reshape(rows, width)
    face = pl.pallas_call(
        functools.partial(pack_kernel, side=side),
        out_shape=jax.ShapeDtypeStruct((surface, width), jnp.bfloat16),
        in_specs=vmem(1),
        out_specs=vmem(1)[0],
        scratch_shapes=[VMEM((len(pieces(width)), rows, LANES), jnp.float32)],
        **params(),
    )(own)
    info = jnp.concatenate([neighbours, occupancy[:, None]], axis=1)
    info_other = lax.ppermute(info, AXES, halves)
    other = lax.ppermute(own, AXES, halves)
    far = lax.ppermute(face, AXES, cycle)

    def weights(kernel):
        flat = kernel.reshape((27,) + kernel.shape[3:])
        swapped = lax.ppermute(flat, AXES, halves)
        return pl.pallas_call(
            weights_kernel,
            out_shape=jax.ShapeDtypeStruct((27, width, width), jnp.bfloat16),
            in_specs=vmem(2),
            out_specs=vmem(1)[0],
            **params(),
        )(flat, swapped)

    w_one, w_two = weights(kernel_one), weights(kernel_two)
    scratch = [
        VMEM((len(pieces(width)), 4 * rows, LANES), jnp.float32),
        VMEM((3, side + 2, (side + 2) * side, width), jnp.float32),
        VMEM((3, side + 2, (side + 2) * side, width), jnp.bfloat16),
        VMEM((3, side + 2, side * side, width), jnp.bfloat16),
    ]
    flops = 2 * rows * 27 * width * width
    hidden, hidden_face = pl.pallas_call(
        functools.partial(first_kernel, side=side),
        out_shape=(
            jax.ShapeDtypeStruct((rows, width), jnp.bfloat16),
            jax.ShapeDtypeStruct((surface, width), jnp.bfloat16),
        ),
        in_specs=smem(2) + vmem(4),
        out_specs=tuple(vmem(2)),
        scratch_shapes=scratch,
        **params(flops),
    )(info_other[:, :27], info_other[:, 27:], other, own, far, w_one)
    hidden_own = lax.ppermute(hidden, AXES, halves)
    hidden_far = lax.ppermute(hidden_face, AXES, back)
    out = pl.pallas_call(
        functools.partial(second_kernel, side=side),
        out_shape=jax.ShapeDtypeStruct((rows, width), jnp.float32),
        in_specs=smem(2) + vmem(5),
        out_specs=vmem(1)[0],
        scratch_shapes=scratch,
        **params(flops),
    )(neighbours, occupancy[:, None], hidden_own, hidden, hidden_far, w_two, own)
    return out.reshape((1, side, side, side, width))


def solution(mesh):
    return jax.shard_map(
        body,
        mesh=mesh,
        in_specs=(
            P(AXES, None, None, None, None),
            P(AXES),
            P(AXES, None),
            P(None, None, None, None, "wt"),
            P(None, None, None, None, "wt"),
        ),
        out_specs=P(AXES, None, None, None, None),
        check_vma=False,
    )
```

time: 100 us -> 24.5 us (0.24)
  the two profiles are of different devices: /device:TPU:8 before, /device:TPU:0 now
where the time goes in v1:
time: 24.5 us; the launch traced here: 24.2 us
  Pallas kernels  8.38 us (34%)
  starting transfers between devices  6.67 us (27%)
  waiting for transfers between devices  4.99 us (20%)
  local copies, waits for them, and re-layouts  2.75 us (11%)
  other arithmetic  0.73 us (3%)
  between operations  0.72 us (3%)
    ppermute x1, waiting for transfers between devices, body(): hidden_far = lax.ppermute(hidden_face, AXES, back)  4.16 us
    pallas_call x1, Pallas kernels, body(): pl.pallas_call(functools.partial(second_kernel, side=side), out_shape=jax...  3.75 us
    pallas_call x1, Pallas kernels, body(): pl.pallas_call(functools.partial(first_kernel, side=side), out_shape=(jax...  3.72 us
    ppermute x1, starting transfers between devices, body(): info_other = lax.ppermute(info, AXES, halves)  2.66 us
    ppermute x1, starting transfers between devices, body(): hidden_far = lax.ppermute(hidden_face, AXES, back)  2.57 us
    unnamed x10, local copies, waits for them, and re-layouts  2.17 us
    pallas_call x2, Pallas kernels, weights(): pl.pallas_call(weights_kernel, out_shape=jax.ShapeDtypeStruct((27, width,...  0.85 us
    ppermute x1, waiting for transfers between devices, body(): info_other = lax.ppermute(info, AXES, halves)  0.82 us
  transfers between devices with their start and end apart: 7, of which 2 were waited for; matrix products, arithmetic and copies ran while one was open for 5% of the time, Pallas kernels for 19%

profile of v1, /device:TPU:0, one launch (start us, length us, event | category | flops | bytes accessed | tf_op | source)
XLA Modules:
  0.0 24.2 jit_solution(9398374786304060442)
XLA Ops:
  0.0 0.5 %collective-permute-start.3 = (bf16[27,48,384]{2,1,0:T(8,128)(2,1)}, bf16[27,48,384]{2,1,0:T(8,128)(2,1)S(1)}, u32[]{:S(2)}, u32[]{:S(2)}) collective-permute-start(bf16[27,48,384]{2,1,0:T(8,128)(2,1)} %bitcast.12), channel_id=1, source_target_pairs={{0,1},{1,0},{2,3},{3,2},{4,5},{5,4},{6,7},{7,6},{8,9},{9,8},{10,11... | collective-permute-start | bytes 2985992 | tf_op jit(solution)/shard_map/ppermute | solution.py:255
  0.5 0.1 collective-permute-start.6
  0.5 0.5 %collective-permute-start.1 = (bf16[512,192]{1,0:T(8,128)(2,1)}, bf16[512,192]{1,0:T(8,128)(2,1)S(1)}, u32[]{:S(2)}, u32[]{:S(2)}) collective-permute-start(bf16[512,192]{1,0:T(8,128)(2,1)} %bitcast.8), channel_id=1, source_target_pairs={{0,1},{1,0},{2,3},{3,2},{4,5},{5,4},{6,7},{7,6},{8,9},{9,8},{10,11... | collective-permute-start | bytes 589832 | tf_op jit(solution)/shard_map/ppermute | solution.py:250
  1.0 0.0 copy-start
  1.0 0.9 %copy-done = bf16[1,8,8,8,192]{4,3,2,1,0:T(8,128)(2,1)S(1)} copy-done((bf16[1,8,8,8,192]{4,3,2,1,0:T(8,128)(2,1)S(1)}, bf16[1,8,8,8,192]{4,3,2,1,0:T(8,128)(2,1)}, u32[]{:S(2)}) %copy-start) | copy-done | bytes 196632
  1.9 0.0 copy-start.1
  1.9 0.1 shard_map.55
  2.0 0.1 collective-permute-start.2
  2.7 0.7 %pad_add_fusion = s32[1,28]{1,0:T(1,128)S(1)} fusion(s32[1,1]{1,0:T(1,128)} %bitcast.6, s32[1,27]{1,0:T(1,128)} %table.1), kind=kLoop, calls=%fused_computation | loop fusion | flops 28 | bytes 224 | tf_op jit(solution)/shard_map/concatenate | solution.py:248
  3.5 2.7 %collective-permute-start = (s32[1,28]{1,0:T(1,128)S(1)}, s32[1,28]{1,0:T(1,128)S(1)}, u32[]{:S(2)}, u32[]{:S(2)}) collective-permute-start(s32[1,28]{1,0:T(1,128)S(1)} %pad_add_fusion), channel_id=1, source_target_pairs={{0,1},{1,0},{2,3},{3,2},{4,5},{5,4},{6,7},{7,6},{8,9},{9,8},{10,11... | collective-permute-start | bytes 344 | tf_op jit(solution)/shard_map/ppermute | solution.py:249
  6.1 0.8 %collective-permute-done = s32[1,28]{1,0:T(1,128)S(1)} collective-permute-done((s32[1,28]{1,0:T(1,128)S(1)}, s32[1,28]{1,0:T(1,128)S(1)}, u32[]{:S(2)}, u32[]{:S(2)}) %collective-permute-start) | collective-permute-done | bytes 144 | tf_op jit(solution)/shard_map/ppermute | solution.py:249
  7.0 0.6 %slice.7.occupancy = s32[1,1]{1,0:T(1,128)} slice(s32[1,28]{1,0:T(1,128)S(1)} %collective-permute-done), slice={[0:1], [27:28]} | slice | bytes 8 | tf_op jit(solution)/shard_map/slice | solution.py:282
  7.5 0.0 collective-permute-done.3.other_ref
  7.5 0.0 copy-start.2
  7.5 1.2 %copy-done.2 = bf16[3,3,3,48,384]{4,3,2,1,0:T(8,128)(2,1)S(1)} copy-done((bf16[3,3,3,48,384]{4,3,2,1,0:T(8,128)(2,1)S(1)}, bf16[3,3,3,48,384]{4,3,2,1,0:T(8,128)(2,1)}, u32[]{:S(2)}) %copy-start.2) | copy-done | bytes 995352
  8.8 0.4 %shard_map.56.w = bf16[27,192,192]{2,1,0:T(8,128)(2,1)S(1)} custom-call(bf16[27,48,384]{2,1,0:T(8,128)(2,1)S(1)} %bitcast.13, bf16[27,48,384]{2,1,0:T(8,128)(2,1)S(1)} %collective-permute-done.3.other_ref), custom_call_target="tpu_custom_call" | custom-call | tf_op jit(solution)/shard_map/pallas_call | solution.py:256
  9.2 0.0 copy-start.3
  9.2 0.0 collective-permute-done.2.far
  9.2 0.0 collective-permute-done.1.center
  9.2 0.0 copy-done.1
  9.2 3.7 %shard_map.57 = (bf16[512,192]{1,0:T(8,128)(2,1)S(1)}, bf16[320,192]{1,0:T(8,128)(2,1)S(1)}) custom-call(s32[1,27]{1,0:T(1,128)S(1)} %bitcast.16, s32[1,1]{1,0:T(1,128)} %slice.7.occupancy, bf16[512,192]{1,0:T(8,128)(2,1)S(1)} %collective-permute-done.1.center, bf16[512,192]{1,0:T(8,128)(2,1)S(1)} %bitcast.10, ...), custom_call_target="tpu_custom_call" | custom-call | flops 1019215872 | tf_op jit(solution)/shard_map/pallas_call | solution.py:272
  12.9 0.0 copy-start.4
  13.0 0.4 %collective-permute-start.4 = (bf16[512,192]{1,0:T(8,128)(2,1)S(1)}, bf16[512,192]{1,0:T(8,128)(2,1)S(1)}, u32[]{:S(2)}, u32[]{:S(2)}) collective-permute-start(bf16[512,192]{1,0:T(8,128)(2,1)S(1)} %get-tuple-element.7.beside), channel_id=1, source_target_pairs={{0,1},{1,0},{2,3},{3,2},{4,5},{5,4},{6,7},{7,6},{8,9},{9,8},{10,11... | collective-permute-start | bytes 589832 | tf_op jit(solution)/shard_map/ppermute | solution.py:283
  13.3 2.6 %collective-permute-start.5 = (bf16[320,192]{1,0:T(8,128)(2,1)S(1)}, bf16[320,192]{1,0:T(8,128)(2,1)S(1)}, u32[]{:S(2)}, u32[]{:S(2)}) collective-permute-start(bf16[320,192]{1,0:T(8,128)(2,1)S(1)} %get-tuple-element.8), channel_id=1, source_target_pairs={{1,0},{3,1},{0,2},{5,3},{2,4},{7,5},{4,6},{9,7},{6,8},{11,9},{8,10... | collective-permute-start | bytes 368648 | tf_op jit(solution)/shard_map/ppermute | solution.py:284
  15.9 0.0 collective-permute-done.6.other_ref
  15.9 0.0 copy-done.3
  15.9 0.4 %shard_map.58.w = bf16[27,192,192]{2,1,0:T(8,128)(2,1)S(1)} custom-call(bf16[27,48,384]{2,1,0:T(8,128)(2,1)S(1)} %bitcast.15, bf16[27,48,384]{2,1,0:T(8,128)(2,1)S(1)} %collective-permute-done.6.other_ref), custom_call_target="tpu_custom_call" | custom-call | tf_op jit(solution)/shard_map/pallas_call | solution.py:256
  16.3 4.2 %collective-permute-done.5.far = bf16[320,192]{1,0:T(8,128)(2,1)S(1)} collective-permute-done((bf16[320,192]{1,0:T(8,128)(2,1)S(1)}, bf16[320,192]{1,0:T(8,128)(2,1)S(1)}, u32[]{:S(2)}, u32[]{:S(2)}) %collective-permute-start.5) | collective-permute-done | bytes 122912 | tf_op jit(solution)/shard_map/ppermute | solution.py:284
  20.5 0.0 collective-permute-done.4.center
  20.5 0.0 copy-done.4
  20.5 3.7 %shard_map.59 = f32[512,192]{1,0:T(8,128)} custom-call(s32[1,27]{1,0:T(1,128)S(1)} %copy-done.4, s32[1,1]{1,0:T(1,128)} %bitcast.7.occupancy, bf16[512,192]{1,0:T(8,128)(2,1)S(1)} %collective-permute-done.4.center, bf16[512,192]{1,0:T(8,128)(2,1)S(1)} %get-tuple-element.7.beside, bf16[320,192]{1,0:T(8,128)(2,1)S(1)} %collective-permute-done.5.far, ...), custom_call_target="tpu_custom_call" | custom-call | flops 1019215872 | tf_op jit(solution)/shard_map/pallas_call | solution.py:285
Async XLA Ops:
  0.0 7.5 %collective-permute-start.3 = (bf16[27,48,384]{2,1,0:T(8,128)(2,1)}, bf16[27,48,384]{2,1,0:T(8,128)(2,1)S(1)}, u32[]{:S(2)}, u32[]{:S(2)}) collective-permute-start(bf16[27,48,384]{2,1,0:T(8,128)(2,1)} %bitcast.12), channel_id=1, source_target_pairs={{0,1},{1,0},{2,3},{3,2},{4,5},{5,4},{6,7},{7,6},{8,9},{9,8},{10,11... | collective-permute-start | bytes 2985992 | tf_op jit(solution)/shard_map/ppermute | solution.py:255
  0.5 15.4 %collective-permute-start.6 = (bf16[27,48,384]{2,1,0:T(8,128)(2,1)}, bf16[27,48,384]{2,1,0:T(8,128)(2,1)S(1)}, u32[]{:S(2)}, u32[]{:S(2)}) collective-permute-start(bf16[27,48,384]{2,1,0:T(8,128)(2,1)} %bitcast.14), channel_id=1, source_target_pairs={{0,1},{1,0},{2,3},{3,2},{4,5},{5,4},{6,7},{7,6},{8,9},{9,8},{10,11... | collective-permute-start | bytes 2985992 | tf_op jit(solution)/shard_map/ppermute | solution.py:255
  0.5 8.7 %collective-permute-start.1 = (bf16[512,192]{1,0:T(8,128)(2,1)}, bf16[512,192]{1,0:T(8,128)(2,1)S(1)}, u32[]{:S(2)}, u32[]{:S(2)}) collective-permute-start(bf16[512,192]{1,0:T(8,128)(2,1)} %bitcast.8), channel_id=1, source_target_pairs={{0,1},{1,0},{2,3},{3,2},{4,5},{5,4},{6,7},{7,6},{8,9},{9,8},{10,11... | collective-permute-start | bytes 589832 | tf_op jit(solution)/shard_map/ppermute | solution.py:250
  1.0 0.9 %copy-start = (bf16[1,8,8,8,192]{4,3,2,1,0:T(8,128)(2,1)S(1)}, bf16[1,8,8,8,192]{4,3,2,1,0:T(8,128)(2,1)}, u32[]{:S(2)}) copy-start(bf16[1,8,8,8,192]{4,3,2,1,0:T(8,128)(2,1)} %param.5) | copy-start | bytes 589828
  1.9 7.3 %copy-start.1 = (bf16[1,8,8,8,192]{4,3,2,1,0:T(8,128)(2,1)S(1)}, bf16[1,8,8,8,192]{4,3,2,1,0:T(8,128)(2,1)}, u32[]{:S(2)}) copy-start(bf16[1,8,8,8,192]{4,3,2,1,0:T(8,128)(2,1)} %param.5) | copy-start | bytes 589828
  2.0 7.2 %collective-permute-start.2 = (bf16[320,192]{1,0:T(8,128)(2,1)S(1)}, bf16[320,192]{1,0:T(8,128)(2,1)S(1)}, u32[]{:S(2)}, u32[]{:S(2)}) collective-permute-start(bf16[320,192]{1,0:T(8,128)(2,1)S(1)} %shard_map.55), channel_id=1, source_target_pairs={{0,1},{1,3},{2,0},{3,5},{4,2},{5,7},{6,4},{7,9},{8,6},{9,11},{10,8... | collective-permute-start | bytes 368648 | tf_op jit(solution)/shard_map/ppermute | solution.py:251
  3.5 3.5 %collective-permute-start = (s32[1,28]{1,0:T(1,128)S(1)}, s32[1,28]{1,0:T(1,128)S(1)}, u32[]{:S(2)}, u32[]{:S(2)}) collective-permute-start(s32[1,28]{1,0:T(1,128)S(1)} %pad_add_fusion), channel_id=1, source_target_pairs={{0,1},{1,0},{2,3},{3,2},{4,5},{5,4},{6,7},{7,6},{8,9},{9,8},{10,11... | collective-permute-start | bytes 344 | tf_op jit(solution)/shard_map/ppermute | solution.py:249
  7.5 1.2 %copy-start.2 = (bf16[3,3,3,48,384]{4,3,2,1,0:T(8,128)(2,1)S(1)}, bf16[3,3,3,48,384]{4,3,2,1,0:T(8,128)(2,1)}, u32[]{:S(2)}) copy-start(bf16[3,3,3,48,384]{4,3,2,1,0:T(8,128)(2,1)} %param.8) | copy-start | bytes 2985988
  9.2 6.7 %copy-start.3 = (bf16[3,3,3,48,384]{4,3,2,1,0:T(8,128)(2,1)S(1)}, bf16[3,3,3,48,384]{4,3,2,1,0:T(8,128)(2,1)}, u32[]{:S(2)}) copy-start(bf16[3,3,3,48,384]{4,3,2,1,0:T(8,128)(2,1)} %param.9) | copy-start | bytes 2985988
  12.9 7.5 %copy-start.4 = (s32[1,27]{1,0:T(1,128)S(1)}, s32[1,27]{1,0:T(1,128)}, u32[]{:S(2)}) copy-start(s32[1,27]{1,0:T(1,128)} %table.1) | copy-start | bytes 328
  13.0 7.5 %collective-permute-start.4 = (bf16[512,192]{1,0:T(8,128)(2,1)S(1)}, bf16[512,192]{1,0:T(8,128)(2,1)S(1)}, u32[]{:S(2)}, u32[]{:S(2)}) collective-permute-start(bf16[512,192]{1,0:T(8,128)(2,1)S(1)} %get-tuple-element.7.beside), channel_id=1, source_target_pairs={{0,1},{1,0},{2,3},{3,2},{4,5},{5,4},{6,7},{7,6},{8,9},{9,8},{10,11... | collective-permute-start | bytes 589832 | tf_op jit(solution)/shard_map/ppermute | solution.py:283
  13.3 7.2 %collective-permute-start.5 = (bf16[320,192]{1,0:T(8,128)(2,1)S(1)}, bf16[320,192]{1,0:T(8,128)(2,1)S(1)}, u32[]{:S(2)}, u32[]{:S(2)}) collective-permute-start(bf16[320,192]{1,0:T(8,128)(2,1)S(1)} %get-tuple-element.8), channel_id=1, source_target_pairs={{1,0},{3,1},{0,2},{5,3},{2,4},{7,5},{4,6},{9,7},{6,8},{11,9},{8,10... | collective-permute-start | bytes 368648 | tf_op jit(solution)/shard_map/ppermute | solution.py:284

commit v2 on v0

v2 whole, which is shorter than its diff:
```python
import functools

import jax
import jax.numpy as jnp
from jax import lax
from jax.experimental import pallas as pl
from jax.experimental.pallas import tpu as pltpu
from jax.sharding import PartitionSpec as P

AXES = ("space", "wt")
VMEM = pltpu.VMEM
SMEM = pltpu.SMEM
LANES = 128
F32 = jnp.float32
BF16 = jnp.bfloat16


def pieces(width):
    return [
        (p, p * LANES, min(LANES, width - p * LANES)) for p in range(-(-width // LANES))
    ]


def fill(wide, base, value):
    rows, width = value.shape
    for p, lane, lanes in pieces(width):
        wide[p, pl.ds(base, rows), 0:lanes] = value[:, lane : lane + lanes]


def whole(wide, width):
    return jnp.concatenate([wide[p, :, 0:lanes] for p, _, lanes in pieces(width)], axis=1)


def surface_rows(side):
    return 2 * side * side + 4 * (side - 2) * side


def pack_surface(wide, out_ref, side, change=lambda value: value):
    plane = side * side
    inner = (side - 2) * side
    last = side - 1
    for p, lane, lanes in pieces(out_ref.shape[1]):
        ref = wide.at[p]

        def store(row, value):
            value = change(value[:, :lanes]).astype(BF16)
            out_ref[pl.ds(row, value.shape[0]), lane : lane + lanes] = value

        store(0, ref[pl.ds(0, plane), :])
        store(plane, ref[pl.ds(last * plane, plane), :])
        row = 2 * plane
        for y in (0, last):
            parts = [
                ref[pl.ds(x * plane + y * side, side), :] for x in range(1, last)
            ]
            store(row, jnp.concatenate(parts, axis=0))
            row += inner
        for z in (0, last):
            store(row, ref[pl.ds(plane + z, inner, stride=side), :])
            row += inner


def spread_surface(packed_ref, faces, slot, side):
    plane = side * side
    inner = (side - 2) * side
    last = side - 1
    base = slot * 6 * plane
    packed = packed_ref[...].astype(F32)
    for p, lane, lanes in pieces(packed.shape[1]):
        ref = faces.at[p]
        part = packed[:, lane : lane + lanes]
        if lanes < LANES:
            pad = jnp.zeros((part.shape[0], LANES - lanes), F32)
            part = jnp.concatenate([part, pad], axis=1)
        ref[pl.ds(base, 2 * plane), :] = part[: 2 * plane]
        row = 2 * plane
        for f in range(2, 6):
            ref[pl.ds(base + f * plane + side, inner), :] = part[row : row + inner]
            row += inner
        for end, x in ((0, 0), (1, last)):
            for f, y in ((2, 0), (3, last)):
                ref[pl.ds(base + f * plane + x * side, side), :] = ref[
                    pl.ds(base + end * plane + y * side, side), :
                ]
            for f, z in ((4, 0), (5, last)):
                ref[pl.ds(base + f * plane + x * side, side), :] = ref[
                    pl.ds(base + end * plane + z, side, stride=side), :
                ]


def pack_kernel(x_ref, out_ref, wide, *, side):
    fill(wide, 0, x_ref[...].astype(F32))
    pack_surface(wide, out_ref, side)


def weights_kernel(own_ref, other_ref, out_ref):
    core = lax.axis_index("wt")
    taps, depth, both = own_ref.shape
    width = out_ref.shape[2]
    half = depth * (both // width)
    for ref, place in ((own_ref, core), (other_ref, 1 - core)):
        for group in range(both // width):
            row = pl.multiple_of(place * half + group * depth, 16)
            out_ref[:, pl.ds(row, depth), :] = ref[
                :, :, group * width : (group + 1) * width
            ]


def shifts(middle, low, high, mask):
    side = middle.shape[1]
    return (
        pltpu.roll(jnp.where(mask == side - 1, low, middle), 1, axis=1),
        middle,
        pltpu.roll(jnp.where(mask == 0, high, middle), side - 1, axis=1),
    )


def inside_kernel(center, w, out, surface, wide, even, odd, *, side):
    rows, width = center.shape
    plane = side * side
    fill(wide, 0, center[...].astype(F32))
    pack_surface(wide, surface, side)
    mask = lax.broadcasted_iota(jnp.int32, (side, side, LANES), 1)
    nothing = jnp.zeros((side, side, LANES), F32)
    edge = jnp.zeros((3, side, side, width), BF16)
    even[:, :, 0:side, :] = edge
    even[:, :, side + plane : plane + 2 * side, :] = edge
    for p, lane, lanes in pieces(width):
        for x in range(side):
            middle = wide[p, pl.ds(x * plane, plane), :].reshape(side, side, LANES)
            for k, value in enumerate(shifts(middle, nothing, nothing, mask)):
                value = value.reshape(plane, LANES)[:, :lanes].astype(BF16)
                even[k, x, side : side + plane, lane : lane + lanes] = value
                odd[k, x, :, lane : lane + lanes] = value
    for i in (1, 0, 2):
        first, count = (1, 0, 0)[i], side - (i != 1)
        source = (0, 0, 1)[i]
        acc = jnp.zeros((count * plane, width), F32)
        for j in range(3):
            for k in range(3):
                if j == 1:
                    part = odd[k, source : source + count]
                else:
                    part = even[
                        k, source : source + count, j * side : j * side + plane
                    ]
                acc += jnp.dot(
                    part.reshape(count * plane, width),
                    w[9 * i + 3 * j + k],
                    preferred_element_type=F32,
                )
        if i == 1:
            out[...] = acc
        else:
            out[pl.ds(first * plane, count * plane), :] += acc


def add_outside(table, block, sources, inside, w, total, faces, even, odd, side):
    rows, width = inside.shape
    plane = side * side
    last = side - 1
    fill(faces, 0, jnp.zeros((6 * plane, width), F32))
    for slot, source in enumerate(sources):
        spread_surface(source, faces, slot + 1, side)
    pair = block + 1 - 2 * lax.rem(block, 2)

    def start(face, a, b, c, row):
        n = table[0, 9 * (a + 1) + 3 * (b + 1) + c + 1]
        near = jnp.where(n == block, 2, jnp.where(n == pair, 1, 3))
        slot = jnp.where(n < 0, 0, near)
        return pl.multiple_of((slot * 6 + face) * plane + row, side)

    mask = lax.broadcasted_iota(jnp.int32, (side, side, LANES), 1)
    for group in range(6):
        axis, up = divmod(group, 2)
        face = 2 * axis + 1 - up
        sign = 2 * up - 1
        for to, count, row, b in (
            (0, 1, last * side, -1),
            (1, side, 0, 0),
            (side + 1, 1, 0, 1),
        ):
            for p, lane, lanes in pieces(width):
                place = pl.ds(to * side, count * side)
                if axis > 0 and b != 0:
                    blank = jnp.zeros((3, side, lanes), BF16)
                    even[group, :, place, lane : lane + lanes] = blank
                    continue

                def chunk(c):
                    if axis == 2:
                        if c != 0:
                            return jnp.zeros((count, side, LANES), F32)
                        at = start(face, 0, 0, sign, row)
                    elif axis == 1:
                        at = start(face, 0, sign, c, row)
                    else:
                        at = start(face, sign, b, c, row)
                    value = faces[p, pl.ds(at, count * side), :]
                    return value.reshape(count, side, LANES)

                moved = shifts(chunk(0), chunk(-1), chunk(1), mask[:count])
                for k, value in enumerate(moved):
                    value = value.reshape(count * side, LANES)[:, :lanes]
                    if b == 0:
                        odd[group, k, :, lane : lane + lanes] = value.astype(BF16)
                    even[group, k, place, lane : lane + lanes] = value.astype(BF16)

    sums = [None] * 6
    for i in range(3):
        for j in range(3):
            for k in range(3):
                parts, groups = [], []
                for axis, tap, chunk, shift in ((0, i, j, k), (1, j, i, k), (2, k, i, j)):
                    if tap == 1:
                        continue
                    group = 2 * axis + tap // 2
                    if chunk == 1:
                        parts.append(odd[group, shift])
                    else:
                        parts.append(
                            even[group, shift, chunk * side : chunk * side + plane]
                        )
                    groups.append(group)
                if not parts:
                    continue
                product = jnp.dot(
                    jnp.concatenate(parts, axis=0),
                    w[9 * i + 3 * j + k],
                    preferred_element_type=F32,
                )
                for n, group in enumerate(groups):
                    part = product[n * plane : (n + 1) * plane]
                    sums[group] = part if sums[group] is None else sums[group] + part

    for p, lane, lanes in pieces(width):
        ref = total.at[p]
        part = [value[:, lane : lane + lanes] for value in sums]
        if lanes < LANES:
            pad = jnp.zeros((plane, LANES - lanes), F32)
            part = [jnp.concatenate([value, pad], axis=1) for value in part]
        ref[:, 0:lanes] = inside[:, lane : lane + lanes]
        for up, x in ((0, 0), (1, last)):
            ref[pl.ds(x * plane, plane), :] += part[up]
        for up, y in ((0, 0), (1, last)):
            for x in range(side):
                ref[pl.ds(x * plane + y * side, side), :] += part[2 + up][
                    x * side : (x + 1) * side
                ]
        for up, z in ((0, 0), (1, last)):
            ref[pl.ds(z, plane, stride=side), :] += part[4 + up]


def first_kernel(
    table, beside, center, far, inside, w, out, surface, total, faces, even, odd, *, side
):
    block = 2 * lax.axis_index("space") + 1 - lax.axis_index("wt")
    add_outside(
        table, block, (beside, center, far), inside, w, total, faces, even, odd, side
    )
    active = (table[0, 13] >= 0).astype(F32)

    def change(value):
        return jnp.maximum(value, 0.0) * active

    pack_surface(total, surface, side, change)
    out[...] = change(whole(total, out.shape[1])).astype(BF16)


def second_kernel(
    table,
    occupancy,
    beside,
    center,
    far,
    inside,
    w,
    features,
    out,
    total,
    faces,
    even,
    odd,
    *,
    side,
):
    block = 2 * lax.axis_index("space") + lax.axis_index("wt")
    add_outside(
        table, block, (beside, center, far), inside, w, total, faces, even, odd, side
    )
    value = features[...].astype(F32) + whole(total, out.shape[1])
    out[...] = jnp.maximum(value, 0.0) * occupancy[0].astype(F32)


def call(kernel, operands, outs, scratch=(), scalars=0, flops=0):
    outs = [jax.ShapeDtypeStruct(shape, kind) for shape, kind in outs]
    moved = sum(o.size * o.dtype.itemsize for o in list(operands) + outs)
    result = pl.pallas_call(
        kernel,
        out_shape=outs,
        in_specs=[pl.BlockSpec(memory_space=SMEM)] * scalars
        + [pl.BlockSpec(memory_space=VMEM)] * (len(operands) - scalars),
        out_specs=[pl.BlockSpec(memory_space=VMEM)] * len(outs),
        scratch_shapes=list(scratch),
        compiler_params=pltpu.CompilerParams(vmem_limit_bytes=32 * 2**20),
        cost_estimate=pl.CostEstimate(
            flops=flops, bytes_accessed=moved, transcendentals=0
        ),
    )(*operands)
    return result[0] if len(outs) == 1 else result


def body(features, occupancy, neighbours, kernel_one, kernel_two):
    side, width = features.shape[1], features.shape[4]
    rows, plane = side**3, side * side
    total = lax.axis_size(AXES)
    halves = [(i, i ^ 1) for i in range(total)]
    cycle = [(i, i - 2) if i % 2 == 0 else (i, i + 2) for i in range(total)]
    cycle[0], cycle[-1] = (0, 1), (total - 1, total - 2)
    back = [(j, i) for i, j in cycle]
    face = ((surface_rows(side), width), BF16)
    block = ((rows, width), BF16)
    wide = ((rows, width), F32)
    count = len(pieces(width))
    flops = 2 * rows * 27 * width * width

    own = features.reshape(rows, width)
    own_face = call(
        functools.partial(pack_kernel, side=side),
        (own,),
        [face],
        [VMEM((count, rows, LANES), F32)],
    )
    table_other = lax.ppermute(neighbours, AXES, halves)
    other = lax.ppermute(own, AXES, halves)
    far = lax.ppermute(own_face, AXES, cycle)

    def weights(kernel):
        flat = kernel.reshape((27,) + kernel.shape[3:])
        swapped = lax.ppermute(flat, AXES, halves)
        return call(weights_kernel, (flat, swapped), [((27, width, width), BF16)])

    w_one, w_two = weights(kernel_one), weights(kernel_two)

    def inside(center, w):
        return call(
            functools.partial(inside_kernel, side=side),
            (center, w),
            [wide, face],
            [
                VMEM((count, rows, LANES), F32),
                VMEM((3, side, plane + 2 * side, width), BF16),
                VMEM((3, side, plane, width), BF16),
            ],
            flops=flops,
        )

    outside = [
        VMEM((count, rows, LANES), F32),
        VMEM((count, 4 * 6 * plane, LANES), F32),
        VMEM((6, 3, plane + 2 * side, width), BF16),
        VMEM((6, 3, plane, width), BF16),
    ]
    inside_one, other_face = inside(other, w_one)
    hidden, hidden_face = call(
        functools.partial(first_kernel, side=side),
        (table_other, own_face, other_face, far, inside_one, w_one),
        [block, face],
        outside,
        scalars=1,
        flops=flops // 4,
    )
    hidden_own = lax.ppermute(hidden, AXES, halves)
    hidden_far = lax.ppermute(hidden_face, AXES, back)
    inside_two, hidden_own_face = inside(hidden_own, w_two)
    out = call(
        functools.partial(second_kernel, side=side),
        (
            neighbours,
            occupancy,
            hidden_face,
            hidden_own_face,
            hidden_far,
            inside_two,
            w_two,
            own,
        ),
        [wide],
        outside,
        scalars=2,
        flops=flops // 4,
    )
    return out.reshape((1, side, side, side, width))


def solution(mesh):
    return jax.shard_map(
        body,
        mesh=mesh,
        in_specs=(
            P(AXES, None, None, None, None),
            P(AXES),
            P(AXES, None),
            P(None, None, None, None, "wt"),
            P(None, None, None, None, "wt"),
        ),
        out_specs=P(AXES, None, None, None, None),
        check_vma=False,
    )
```

time: 100 us -> 21.1 us (0.21)
  the two profiles are of different devices: /device:TPU:8 before, /device:TPU:0 now
where the time goes in v2:
time: 21.1 us; the launch traced here: 21 us
  Pallas kernels  8.96 us (42%)
  starting transfers between devices  7.4 us (35%)
  local copies, waits for them, and re-layouts  2.17 us (10%)
  waiting for transfers between devices  1.66 us (8%)
  between operations  0.77 us (4%)
    pallas_call x7, Pallas kernels, call(): pl.pallas_call(kernel, out_shape=outs, in_specs=[pl.BlockSpec(memory_spac...  8.96 us
    ppermute x1, starting transfers between devices, body(): hidden_far = lax.ppermute(hidden_face, AXES, back)  3.59 us
    ppermute x1, starting transfers between devices, body(): table_other = lax.ppermute(neighbours, AXES, halves)  2.66 us
    unnamed x10, local copies, waits for them, and re-layouts  2.17 us
    ppermute x1, waiting for transfers between devices, body(): hidden_far = lax.ppermute(hidden_face, AXES, back)  1.49 us
    ppermute x2, starting transfers between devices, weights(): swapped = lax.ppermute(flat, AXES, halves)  0.51 us
    ppermute x1, starting transfers between devices, body(): other = lax.ppermute(own, AXES, halves)  0.45 us
  transfers between devices with their start and end apart: 7, of which 2 were waited for; matrix products, arithmetic and copies ran while one was open for 0% of the time, Pallas kernels for 31%

profile of v2, /device:TPU:0, one launch (start us, length us, event | category | flops | bytes accessed | tf_op | source)
XLA Modules:
  0.0 21.0 jit_solution(11912495478428714730)
XLA Ops:
  0.0 0.5 %collective-permute-start.2 = (bf16[27,48,384]{2,1,0:T(8,128)(2,1)}, bf16[27,48,384]{2,1,0:T(8,128)(2,1)S(1)}, u32[]{:S(2)}, u32[]{:S(2)}) collective-permute-start(bf16[27,48,384]{2,1,0:T(8,128)(2,1)} %bitcast.7), channel_id=1, source_target_pairs={{0,1},{1,0},{2,3},{3,2},{4,5},{5,4},{6,7},{7,6},{8,9},{9,8},{10,11... | collective-permute-start | bytes 2985992 | tf_op jit(solution)/shard_map/ppermute | solution.py:340
  0.5 0.1 collective-permute-start.5
  0.5 0.5 %collective-permute-start.1 = (bf16[512,192]{1,0:T(8,128)(2,1)}, bf16[512,192]{1,0:T(8,128)(2,1)S(1)}, u32[]{:S(2)}, u32[]{:S(2)}) collective-permute-start(bf16[512,192]{1,0:T(8,128)(2,1)} %bitcast.4), channel_id=1, source_target_pairs={{0,1},{1,0},{2,3},{3,2},{4,5},{5,4},{6,7},{7,6},{8,9},{9,8},{10,11... | collective-permute-start | bytes 589832 | tf_op jit(solution)/shard_map/ppermute | solution.py:335
  1.0 0.0 copy-start
  1.0 0.9 %copy-done = bf16[1,8,8,8,192]{4,3,2,1,0:T(8,128)(2,1)S(1)} copy-done((bf16[1,8,8,8,192]{4,3,2,1,0:T(8,128)(2,1)S(1)}, bf16[1,8,8,8,192]{4,3,2,1,0:T(8,128)(2,1)}, u32[]{:S(2)}) %copy-start) | copy-done | bytes 196632
  1.9 0.1 shard_map.55.beside
  2.0 0.1 collective-permute-start.3
  2.1 2.7 %collective-permute-start = (s32[1,27]{1,0:T(1,128)}, s32[1,27]{1,0:T(1,128)S(1)}, u32[]{:S(2)}, u32[]{:S(2)}) collective-permute-start(s32[1,27]{1,0:T(1,128)} %table.1), channel_id=1, source_target_pairs={{0,1},{1,0},{2,3},{3,2},{4,5},{5,4},{6,7},{7,6},{8,9},{9,8},{10,11... | collective-permute-start | bytes 332 | tf_op jit(solution)/shard_map/ppermute | solution.py:334
  4.8 0.0 collective-permute-done.2.other_ref
  4.8 0.0 copy-start.2
  4.8 1.2 %copy-done.2 = bf16[3,3,3,48,384]{4,3,2,1,0:T(8,128)(2,1)S(1)} copy-done((bf16[3,3,3,48,384]{4,3,2,1,0:T(8,128)(2,1)S(1)}, bf16[3,3,3,48,384]{4,3,2,1,0:T(8,128)(2,1)}, u32[]{:S(2)}) %copy-start.2) | copy-done | bytes 995352
  6.0 0.4 %shard_map.56.w = bf16[27,192,192]{2,1,0:T(8,128)(2,1)S(1)} custom-call(bf16[27,48,384]{2,1,0:T(8,128)(2,1)S(1)} %bitcast.8, bf16[27,48,384]{2,1,0:T(8,128)(2,1)S(1)} %collective-permute-done.2.other_ref), custom_call_target="tpu_custom_call" | custom-call | bytes 3981312 | tf_op jit(solution)/shard_map/pallas_call | solution.py:298
  6.4 0.0 collective-permute-done.1.center
  6.4 2.0 %shard_map.57 = (f32[512,192]{1,0:T(8,128)S(1)}, bf16[320,192]{1,0:T(8,128)(2,1)S(1)}) custom-call(bf16[512,192]{1,0:T(8,128)(2,1)S(1)} %collective-permute-done.1.center, bf16[27,192,192]{2,1,0:T(8,128)(2,1)S(1)} %shard_map.56.w), custom_call_target="tpu_custom_call" | custom-call | flops 1019215872 | bytes 2703360 | tf_op jit(solution)/shard_map/pallas_call | solution.py:298
  8.4 0.0 copy-start.3
  8.4 0.0 collective-permute-done.table
  8.4 0.2 collective-permute-done.3.far
  8.6 1.7 %shard_map.58 = (bf16[512,192]{1,0:T(8,128)(2,1)S(1)}, bf16[320,192]{1,0:T(8,128)(2,1)S(1)}) custom-call(s32[1,27]{1,0:T(1,128)S(1)} %collective-permute-done.table, bf16[320,192]{1,0:T(8,128)(2,1)S(1)} %shard_map.55.beside, bf16[320,192]{1,0:T(8,128)(2,1)S(1)} %get-tuple-element.11.center, bf16[320,192]{1,0:T(8,128)(2,1)S(1)} %collective-permute-done.3.far, ...), custom_call_target="tpu_custom_call" | custom-call | flops 254803968 | bytes 3072108 | tf_op jit(solution)/shard_map/pallas_call | solution.py:298
  10.2 0.1 collective-permute-start.4
  10.3 3.6 %collective-permute-start.6 = (bf16[320,192]{1,0:T(8,128)(2,1)S(1)}, bf16[320,192]{1,0:T(8,128)(2,1)S(1)}, u32[]{:S(2)}, u32[]{:S(2)}) collective-permute-start(bf16[320,192]{1,0:T(8,128)(2,1)S(1)} %get-tuple-element.13.beside), channel_id=1, source_target_pairs={{1,0},{3,1},{0,2},{5,3},{2,4},{7,5},{4,6},{9,7},{6,8},{11,9},{8,10... | collective-permute-start | bytes 368648 | tf_op jit(solution)/shard_map/ppermute | solution.py:374
  14.6 0.0 collective-permute-done.5.other_ref
  14.6 0.0 copy-done.3
  14.6 0.4 %shard_map.59.w = bf16[27,192,192]{2,1,0:T(8,128)(2,1)S(1)} custom-call(bf16[27,48,384]{2,1,0:T(8,128)(2,1)S(1)} %bitcast.10, bf16[27,48,384]{2,1,0:T(8,128)(2,1)S(1)} %collective-permute-done.5.other_ref), custom_call_target="tpu_custom_call" | custom-call | bytes 3981312 | tf_op jit(solution)/shard_map/pallas_call | solution.py:298
  15.0 0.0 copy-start.1
  15.0 0.0 copy-start.4
  15.0 0.0 collective-permute-done.4.center
  15.0 2.0 %shard_map.60 = (f32[512,192]{1,0:T(8,128)S(1)}, bf16[320,192]{1,0:T(8,128)(2,1)S(1)}) custom-call(bf16[512,192]{1,0:T(8,128)(2,1)S(1)} %collective-permute-done.4.center, bf16[27,192,192]{2,1,0:T(8,128)(2,1)S(1)} %shard_map.59.w), custom_call_target="tpu_custom_call" | custom-call | flops 1019215872 | bytes 2703360 | tf_op jit(solution)/shard_map/pallas_call | solution.py:298
  17.0 1.5 %collective-permute-done.6.far = bf16[320,192]{1,0:T(8,128)(2,1)S(1)} collective-permute-done((bf16[320,192]{1,0:T(8,128)(2,1)S(1)}, bf16[320,192]{1,0:T(8,128)(2,1)S(1)}, u32[]{:S(2)}, u32[]{:S(2)}) %collective-permute-start.6) | collective-permute-done | bytes 122912 | tf_op jit(solution)/shard_map/ppermute | solution.py:374
  18.5 0.0 copy-done.1
  18.5 0.0 copy-done.4
  18.5 2.5 %shard_map.61 = f32[512,192]{1,0:T(8,128)} custom-call(s32[1,27]{1,0:T(1,128)S(1)} %copy-done.4, s32[1]{0:T(128)S(6)} %copy.6.occupancy, bf16[320,192]{1,0:T(8,128)(2,1)S(1)} %get-tuple-element.13.beside, bf16[320,192]{1,0:T(8,128)(2,1)S(1)} %get-tuple-element.15.center, bf16[320,192]{1,0:T(8,128)(2,1)S(1)} %collective-permute-done.6.far, ...), custom_call_target="tpu_custom_call" | custom-call | flops 254803968 | bytes 3342448 | tf_op jit(solution)/shard_map/pallas_call | solution.py:298
Async XLA Ops:
  0.0 4.8 %collective-permute-start.2 = (bf16[27,48,384]{2,1,0:T(8,128)(2,1)}, bf16[27,48,384]{2,1,0:T(8,128)(2,1)S(1)}, u32[]{:S(2)}, u32[]{:S(2)}) collective-permute-start(bf16[27,48,384]{2,1,0:T(8,128)(2,1)} %bitcast.7), channel_id=1, source_target_pairs={{0,1},{1,0},{2,3},{3,2},{4,5},{5,4},{6,7},{7,6},{8,9},{9,8},{10,11... | collective-permute-start | bytes 2985992 | tf_op jit(solution)/shard_map/ppermute | solution.py:340
  0.5 14.1 %collective-permute-start.5 = (bf16[27,48,384]{2,1,0:T(8,128)(2,1)}, bf16[27,48,384]{2,1,0:T(8,128)(2,1)S(1)}, u32[]{:S(2)}, u32[]{:S(2)}) collective-permute-start(bf16[27,48,384]{2,1,0:T(8,128)(2,1)} %bitcast.9), channel_id=1, source_target_pairs={{0,1},{1,0},{2,3},{3,2},{4,5},{5,4},{6,7},{7,6},{8,9},{9,8},{10,11... | collective-permute-start | bytes 2985992 | tf_op jit(solution)/shard_map/ppermute | solution.py:340
  0.5 5.9 %collective-permute-start.1 = (bf16[512,192]{1,0:T(8,128)(2,1)}, bf16[512,192]{1,0:T(8,128)(2,1)S(1)}, u32[]{:S(2)}, u32[]{:S(2)}) collective-permute-start(bf16[512,192]{1,0:T(8,128)(2,1)} %bitcast.4), channel_id=1, source_target_pairs={{0,1},{1,0},{2,3},{3,2},{4,5},{5,4},{6,7},{7,6},{8,9},{9,8},{10,11... | collective-permute-start | bytes 589832 | tf_op jit(solution)/shard_map/ppermute | solution.py:335
  1.0 0.9 %copy-start = (bf16[1,8,8,8,192]{4,3,2,1,0:T(8,128)(2,1)S(1)}, bf16[1,8,8,8,192]{4,3,2,1,0:T(8,128)(2,1)}, u32[]{:S(2)}) copy-start(bf16[1,8,8,8,192]{4,3,2,1,0:T(8,128)(2,1)} %param.5) | copy-start | bytes 589828
  2.0 6.6 %collective-permute-start.3 = (bf16[320,192]{1,0:T(8,128)(2,1)S(1)}, bf16[320,192]{1,0:T(8,128)(2,1)S(1)}, u32[]{:S(2)}, u32[]{:S(2)}) collective-permute-start(bf16[320,192]{1,0:T(8,128)(2,1)S(1)} %shard_map.55.beside), channel_id=1, source_target_pairs={{0,1},{1,3},{2,0},{3,5},{4,2},{5,7},{6,4},{7,9},{8,6},{9,11},{10,8... | collective-permute-start | bytes 368648 | tf_op jit(solution)/shard_map/ppermute | solution.py:336
  2.1 6.3 %collective-permute-start = (s32[1,27]{1,0:T(1,128)}, s32[1,27]{1,0:T(1,128)S(1)}, u32[]{:S(2)}, u32[]{:S(2)}) collective-permute-start(s32[1,27]{1,0:T(1,128)} %table.1), channel_id=1, source_target_pairs={{0,1},{1,0},{2,3},{3,2},{4,5},{5,4},{6,7},{7,6},{8,9},{9,8},{10,11... | collective-permute-start | bytes 332 | tf_op jit(solution)/shard_map/ppermute | solution.py:334
  4.8 1.2 %copy-start.2 = (bf16[3,3,3,48,384]{4,3,2,1,0:T(8,128)(2,1)S(1)}, bf16[3,3,3,48,384]{4,3,2,1,0:T(8,128)(2,1)}, u32[]{:S(2)}) copy-start(bf16[3,3,3,48,384]{4,3,2,1,0:T(8,128)(2,1)} %param.8) | copy-start | bytes 2985988
  8.4 6.2 %copy-start.3 = (bf16[3,3,3,48,384]{4,3,2,1,0:T(8,128)(2,1)S(1)}, bf16[3,3,3,48,384]{4,3,2,1,0:T(8,128)(2,1)}, u32[]{:S(2)}) copy-start(bf16[3,3,3,48,384]{4,3,2,1,0:T(8,128)(2,1)} %param.9) | copy-start | bytes 2985988
  10.2 4.8 %collective-permute-start.4 = (bf16[512,192]{1,0:T(8,128)(2,1)S(1)}, bf16[512,192]{1,0:T(8,128)(2,1)S(1)}, u32[]{:S(2)}, u32[]{:S(2)}) collective-permute-start(bf16[512,192]{1,0:T(8,128)(2,1)S(1)} %get-tuple-element.14), channel_id=1, source_target_pairs={{0,1},{1,0},{2,3},{3,2},{4,5},{5,4},{6,7},{7,6},{8,9},{9,8},{10,11... | collective-permute-start | bytes 589832 | tf_op jit(solution)/shard_map/ppermute | solution.py:373
  10.3 8.2 %collective-permute-start.6 = (bf16[320,192]{1,0:T(8,128)(2,1)S(1)}, bf16[320,192]{1,0:T(8,128)(2,1)S(1)}, u32[]{:S(2)}, u32[]{:S(2)}) collective-permute-start(bf16[320,192]{1,0:T(8,128)(2,1)S(1)} %get-tuple-element.13.beside), channel_id=1, source_target_pairs={{1,0},{3,1},{0,2},{5,3},{2,4},{7,5},{4,6},{9,7},{6,8},{11,9},{8,10... | collective-permute-start | bytes 368648 | tf_op jit(solution)/shard_map/ppermute | solution.py:374
  15.0 3.5 %copy-start.1 = (bf16[1,8,8,8,192]{4,3,2,1,0:T(8,128)(2,1)S(1)}, bf16[1,8,8,8,192]{4,3,2,1,0:T(8,128)(2,1)}, u32[]{:S(2)}) copy-start(bf16[1,8,8,8,192]{4,3,2,1,0:T(8,128)(2,1)} %param.5) | copy-start | bytes 589828
  15.0 3.5 %copy-start.4 = (s32[1,27]{1,0:T(1,128)S(1)}, s32[1,27]{1,0:T(1,128)}, u32[]{:S(2)}) copy-start(s32[1,27]{1,0:T(1,128)} %table.1) | copy-start | bytes 328

commit v3 on v2

--- a/solution.py
+++ b/solution.py
@@ -7,6 +7,8 @@
 from jax.experimental.pallas import tpu as pltpu
 from jax.sharding import PartitionSpec as P
 
+PARTS = 2
+PACK_COST = 4 * 10**9
 AXES = ("space", "wt")
 VMEM = pltpu.VMEM
 SMEM = pltpu.SMEM
@@ -25,10 +27,6 @@
     rows, width = value.shape
     for p, lane, lanes in pieces(width):
         wide[p, pl.ds(base, rows), 0:lanes] = value[:, lane : lane + lanes]
-
-
-def whole(wide, width):
-    return jnp.concatenate([wide[p, :, 0:lanes] for p, _, lanes in pieces(width)], axis=1)
 
 
 def surface_rows(side):
@@ -88,9 +86,37 @@
                 ]
 
 
-def pack_kernel(x_ref, out_ref, wide, *, side):
+def cut_surface(wide, faces, slot, side):
+    plane = side * side
+    last = side - 1
+    base = slot * 6 * plane
+    for p in range(wide.shape[0]):
+        for n, x in enumerate((0, last)):
+            faces[p, pl.ds(base + n * plane, plane), :] = wide[
+                p, pl.ds(x * plane, plane), :
+            ]
+        for n, y in ((2, 0), (3, last)):
+            for x in range(side):
+                faces[p, pl.ds(base + n * plane + x * side, side), :] = wide[
+                    p, pl.ds(x * plane + y * side, side), :
+                ]
+        for n, z in ((4, 0), (5, last)):
+            faces[p, pl.ds(base + n * plane, plane), :] = wide.at[p][
+                pl.ds(z, plane, stride=side), :
+            ]
+
+
+def pack_kernel(x_ref, out_ref, *refs, side):
+    *pieces_out, wide = refs
     fill(wide, 0, x_ref[...].astype(F32))
     pack_surface(wide, out_ref, side)
+    share(x_ref[...], pieces_out)
+
+
+def share(value, refs):
+    for n, ref in enumerate(refs):
+        count = ref.shape[0]
+        ref[...] = value[n * count : (n + 1) * count]
 
 
 def weights_kernel(own_ref, other_ref, out_ref):
@@ -115,11 +141,16 @@
     )
 
 
-def inside_kernel(center, w, out, surface, wide, even, odd, *, side):
-    rows, width = center.shape
-    plane = side * side
-    fill(wide, 0, center[...].astype(F32))
-    pack_surface(wide, surface, side)
+def inside_kernel(*refs, side, block_of):
+    table, beside, *centers, w, total, near, masks, wide, faces, even, odd = refs
+    width = w.shape[2]
+    rows, plane = total.shape[1], side * side
+    for n, part in enumerate(centers):
+        fill(wide, n * part.shape[0], part[...].astype(F32))
+    fill(faces, 0, jnp.zeros((6 * plane, width), F32))
+    spread_surface(beside, faces, 1, side)
+    cut_surface(wide, faces, 2, side)
+    choose_near(table, block_of(), faces, near, masks, side)
     mask = lax.broadcasted_iota(jnp.int32, (side, side, LANES), 1)
     nothing = jnp.zeros((side, side, LANES), F32)
     edge = jnp.zeros((3, side, side, width), BF16)
@@ -149,28 +180,17 @@
                     w[9 * i + 3 * j + k],
                     preferred_element_type=F32,
                 )
-        if i == 1:
-            out[...] = acc
-        else:
-            out[pl.ds(first * plane, count * plane), :] += acc
-
-
-def add_outside(table, block, sources, inside, w, total, faces, even, odd, side):
-    rows, width = inside.shape
-    plane = side * side
+        for p, lane, lanes in pieces(width):
+            part = acc[:, lane : lane + lanes]
+            place = pl.ds(first * plane, count * plane)
+            if i == 1:
+                total[p, place, 0:lanes] = part
+            else:
+                total[p, place, 0:lanes] += part
+
+
+def borders(side):
     last = side - 1
-    fill(faces, 0, jnp.zeros((6 * plane, width), F32))
-    for slot, source in enumerate(sources):
-        spread_surface(source, faces, slot + 1, side)
-    pair = block + 1 - 2 * lax.rem(block, 2)
-
-    def start(face, a, b, c, row):
-        n = table[0, 9 * (a + 1) + 3 * (b + 1) + c + 1]
-        near = jnp.where(n == block, 2, jnp.where(n == pair, 1, 3))
-        slot = jnp.where(n < 0, 0, near)
-        return pl.multiple_of((slot * 6 + face) * plane + row, side)
-
-    mask = lax.broadcasted_iota(jnp.int32, (side, side, LANES), 1)
     for group in range(6):
         axis, up = divmod(group, 2)
         face = 2 * axis + 1 - up
@@ -180,31 +200,77 @@
             (1, side, 0, 0),
             (side + 1, 1, 0, 1),
         ):
-            for p, lane, lanes in pieces(width):
-                place = pl.ds(to * side, count * side)
-                if axis > 0 and b != 0:
-                    blank = jnp.zeros((3, side, lanes), BF16)
-                    even[group, :, place, lane : lane + lanes] = blank
-                    continue
-
-                def chunk(c):
-                    if axis == 2:
-                        if c != 0:
-                            return jnp.zeros((count, side, LANES), F32)
-                        at = start(face, 0, 0, sign, row)
-                    elif axis == 1:
-                        at = start(face, 0, sign, c, row)
-                    else:
-                        at = start(face, sign, b, c, row)
-                    value = faces[p, pl.ds(at, count * side), :]
-                    return value.reshape(count, side, LANES)
-
-                moved = shifts(chunk(0), chunk(-1), chunk(1), mask[:count])
-                for k, value in enumerate(moved):
-                    value = value.reshape(count * side, LANES)[:, :lanes]
-                    if b == 0:
-                        odd[group, k, :, lane : lane + lanes] = value.astype(BF16)
-                    even[group, k, place, lane : lane + lanes] = value.astype(BF16)
+            offsets = {}
+            for c in (-1, 0, 1):
+                if axis == 0:
+                    offsets[c] = (sign, b, c)
+                elif axis == 1 and b == 0:
+                    offsets[c] = (0, sign, c)
+                elif axis == 2 and b == 0 and c == 0:
+                    offsets[c] = (0, 0, sign)
+            yield group, to, count, row, face, offsets
+
+
+def entry(offset):
+    a, b, c = offset
+    return 9 * (a + 1) + 3 * (b + 1) + c + 1
+
+
+def choose_near(table, block, faces, near, masks, side):
+    plane = side * side
+    pair = block + 1 - 2 * lax.rem(block, 2)
+
+    def slot(n):
+        return jnp.where(n < 0, 0, jnp.where(n == block, 2, jnp.where(n == pair, 1, 3)))
+
+    slots = [slot(table[0, t]) for t in range(27)]
+    for t, value in enumerate(slots):
+        flag = (value > 0 if t == 13 else value == 3).astype(F32)
+        masks[pl.ds(8 * t, 8), :] = jnp.full((8, LANES), flag, F32)
+    for group, to, count, row, face, offsets in borders(side):
+        for c, offset in offsets.items():
+            value = slots[entry(offset)]
+            source = jnp.where(value == 3, 0, value)
+            start = pl.multiple_of((source * 6 + face) * plane + row, side)
+            place = pl.ds(((3 * group + c + 1) * (side + 2) + to) * side, count * side)
+            for p in range(faces.shape[0]):
+                near[p, place, :] = faces[p, pl.ds(start, count * side), :]
+
+
+def add_outside(far, w, near, masks, total, faces, even, odd, side):
+    width = w.shape[2]
+    plane = side * side
+    last = side - 1
+    spread_surface(far, faces, 0, side)
+    mask = lax.broadcasted_iota(jnp.int32, (side, side, LANES), 1)
+    for group, to, count, row, face, offsets in borders(side):
+        for p, lane, lanes in pieces(width):
+            place = pl.ds(to * side, count * side)
+            if not offsets:
+                blank = jnp.zeros((3, side, lanes), BF16)
+                even[group, :, place, lane : lane + lanes] = blank
+                continue
+
+            def chunk(c):
+                if c not in offsets:
+                    return jnp.zeros((count, side, LANES), F32)
+                away = masks[pl.ds(8 * entry(offsets[c]), 8), :] > 0
+                at = ((3 * group + c + 1) * (side + 2) + to) * side
+                afar = faces[p, pl.ds(face * plane + row, count * side), :]
+                here = near[p, pl.ds(at, count * side), :]
+                shape = (count, side, LANES)
+                return jnp.where(
+                    jnp.broadcast_to(away[None], shape),
+                    afar.reshape(shape),
+                    here.reshape(shape),
+                )
+
+            moved = shifts(chunk(0), chunk(-1), chunk(1), mask[:count])
+            for k, value in enumerate(moved):
+                value = value.reshape(count * side, LANES)[:, :lanes]
+                if count == side:
+                    odd[group, k, :, lane : lane + lanes] = value.astype(BF16)
+                even[group, k, place, lane : lane + lanes] = value.astype(BF16)
 
     sums = [None] * 6
     for i in range(3):
@@ -239,7 +305,6 @@
         if lanes < LANES:
             pad = jnp.zeros((plane, LANES - lanes), F32)
             part = [jnp.concatenate([value, pad], axis=1) for value in part]
-        ref[:, 0:lanes] = inside[:, lane : lane + lanes]
         for up, x in ((0, 0), (1, last)):
             ref[pl.ds(x * plane, plane), :] += part[up]
         for up, y in ((0, 0), (1, last)):
@@ -251,50 +316,42 @@
             ref[pl.ds(z, plane, stride=side), :] += part[4 + up]
 
 
-def first_kernel(
-    table, beside, center, far, inside, w, out, surface, total, faces, even, odd, *, side
+def first_kernel(far, w, total_in, near, masks, surface, *refs, side):
+    *outs, total, faces, even, odd = refs
+    add_outside(far, w, near, masks, total, faces, even, odd, side)
+    active = masks[pl.ds(8 * 13, 1), :]
+
+    def change(value):
+        return jnp.maximum(value, 0.0) * active[:, : value.shape[1]]
+
+    pack_surface(total, surface, side, change)
+    for p, lane, lanes in pieces(w.shape[2]):
+        for n, out in enumerate(outs):
+            count = out.shape[0]
+            value = change(total[p, pl.ds(n * count, count), 0:lanes])
+            out[:, lane : lane + lanes] = value.astype(BF16)
+
+
+def second_kernel(
+    occupancy, far, w, features, total_in, near, masks, out, total, faces, even, odd, *, side
 ):
-    block = 2 * lax.axis_index("space") + 1 - lax.axis_index("wt")
-    add_outside(
-        table, block, (beside, center, far), inside, w, total, faces, even, odd, side
-    )
-    active = (table[0, 13] >= 0).astype(F32)
-
-    def change(value):
-        return jnp.maximum(value, 0.0) * active
-
-    pack_surface(total, surface, side, change)
-    out[...] = change(whole(total, out.shape[1])).astype(BF16)
-
-
-def second_kernel(
-    table,
-    occupancy,
-    beside,
-    center,
-    far,
-    inside,
-    w,
-    features,
-    out,
-    total,
-    faces,
-    even,
-    odd,
-    *,
-    side,
-):
-    block = 2 * lax.axis_index("space") + lax.axis_index("wt")
-    add_outside(
-        table, block, (beside, center, far), inside, w, total, faces, even, odd, side
-    )
-    value = features[...].astype(F32) + whole(total, out.shape[1])
-    out[...] = jnp.maximum(value, 0.0) * occupancy[0].astype(F32)
-
-
-def call(kernel, operands, outs, scratch=(), scalars=0, flops=0):
+    add_outside(far, w, near, masks, total, faces, even, odd, side)
+    active = occupancy[...].astype(F32)
+    for p, lane, lanes in pieces(w.shape[2]):
+        value = features[:, lane : lane + lanes].astype(F32) + total[p, :, 0:lanes]
+        out[:, lane : lane + lanes] = jnp.maximum(value, 0.0) * active
+
+
+def first_block():
+    return 2 * lax.axis_index("space") + 1 - lax.axis_index("wt")
+
+
+def second_block():
+    return 2 * lax.axis_index("space") + lax.axis_index("wt")
+
+
+def call(kernel, operands, outs, scratch=(), scalars=0, cost=0, aliases={}):
     outs = [jax.ShapeDtypeStruct(shape, kind) for shape, kind in outs]
-    moved = sum(o.size * o.dtype.itemsize for o in list(operands) + outs)
     result = pl.pallas_call(
         kernel,
         out_shape=outs,
@@ -302,10 +359,9 @@
         + [pl.BlockSpec(memory_space=VMEM)] * (len(operands) - scalars),
         out_specs=[pl.BlockSpec(memory_space=VMEM)] * len(outs),
         scratch_shapes=list(scratch),
+        input_output_aliases=aliases,
         compiler_params=pltpu.CompilerParams(vmem_limit_bytes=32 * 2**20),
-        cost_estimate=pl.CostEstimate(
-            flops=flops, bytes_accessed=moved, transcendentals=0
-        ),
+        cost_estimate=pl.CostEstimate(flops=cost, bytes_accessed=0, transcendentals=0),
     )(*operands)
     return result[0] if len(outs) == 1 else result
 
@@ -319,20 +375,20 @@
     cycle[0], cycle[-1] = (0, 1), (total - 1, total - 2)
     back = [(j, i) for i, j in cycle]
     face = ((surface_rows(side), width), BF16)
-    block = ((rows, width), BF16)
+    piece = ((rows // PARTS, width), BF16)
     wide = ((rows, width), F32)
     count = len(pieces(width))
-    flops = 2 * rows * 27 * width * width
 
     own = features.reshape(rows, width)
-    own_face = call(
+    own_face, *own_parts = call(
         functools.partial(pack_kernel, side=side),
         (own,),
-        [face],
+        [face] + [piece] * PARTS,
         [VMEM((count, rows, LANES), F32)],
+        cost=PACK_COST,
     )
     table_other = lax.ppermute(neighbours, AXES, halves)
-    other = lax.ppermute(own, AXES, halves)
+    other = [lax.ppermute(part, AXES, halves) for part in own_parts]
     far = lax.ppermute(own_face, AXES, cycle)
 
     def weights(kernel):
@@ -342,53 +398,50 @@
 
     w_one, w_two = weights(kernel_one), weights(kernel_two)
 
-    def inside(center, w):
+    sums = ((count, rows, LANES), F32)
+    near = ((count, 6 * 3 * (side + 2) * side, LANES), F32)
+    masks = ((27 * 8, LANES), F32)
+
+    def inside(block_of, table, beside, center, w):
         return call(
-            functools.partial(inside_kernel, side=side),
-            (center, w),
-            [wide, face],
+            functools.partial(inside_kernel, side=side, block_of=block_of),
+            (table, beside, *center, w),
+            [sums, near, masks],
             [
                 VMEM((count, rows, LANES), F32),
+                VMEM((count, 3 * 6 * plane, LANES), F32),
                 VMEM((3, side, plane + 2 * side, width), BF16),
                 VMEM((3, side, plane, width), BF16),
             ],
-            flops=flops,
+            scalars=1,
         )
 
-    outside = [
-        VMEM((count, rows, LANES), F32),
-        VMEM((count, 4 * 6 * plane, LANES), F32),
+    planes = [
+        VMEM((count, 6 * plane, LANES), F32),
         VMEM((6, 3, plane + 2 * side, width), BF16),
         VMEM((6, 3, plane, width), BF16),
     ]
-    inside_one, other_face = inside(other, w_one)
-    hidden, hidden_face = call(
+    hidden_face, *hidden, _ = call(
         functools.partial(first_kernel, side=side),
-        (table_other, own_face, other_face, far, inside_one, w_one),
-        [block, face],
-        outside,
-        scalars=1,
-        flops=flops // 4,
+        (far, w_one, *inside(first_block, table_other, own_face, other, w_one)),
+        [face] + [piece] * PARTS + [sums],
+        planes,
+        aliases={2: 1 + PARTS},
     )
-    hidden_own = lax.ppermute(hidden, AXES, halves)
+    hidden_own = [lax.ppermute(part, AXES, halves) for part in hidden]
     hidden_far = lax.ppermute(hidden_face, AXES, back)
-    inside_two, hidden_own_face = inside(hidden_own, w_two)
-    out = call(
+    out, _ = call(
         functools.partial(second_kernel, side=side),
         (
-            neighbours,
-            occupancy,
-            hidden_face,
-            hidden_own_face,
+            occupancy.reshape(1, 1),
             hidden_far,
-            inside_two,
             w_two,
             own,
+            *inside(second_block, neighbours, hidden_face, hidden_own, w_two),
         ),
-        [wide],
-        outside,
-        scalars=2,
-        flops=flops // 4,
+        [wide, sums],
+        planes,
+        aliases={4: 1},
     )
     return out.reshape((1, side, side, side, width))
 

time: 21.1 us -> 18.6 us (0.88)
  the two profiles are of different devices: /device:TPU:0 before, /device:TPU:8 now
where the time goes in v3:
time: 18.6 us; the launch traced here: 18.4 us
  Pallas kernels  8.71 us (47%)
  starting transfers between devices  5.54 us (30%)
  waiting for transfers between devices  2.41 us (13%)
  local copies, waits for them, and re-layouts  0.97 us (5%)
  between operations  0.75 us (4%)
    pallas_call x7, Pallas kernels, call(): pl.pallas_call(kernel, out_shape=outs, in_specs=[pl.BlockSpec(memory_spac...  8.71 us
    ppermute x1, starting transfers between devices, body(): far = lax.ppermute(own_face, AXES, cycle)  2.39 us
    ppermute x1, starting transfers between devices, body(): hidden_far = lax.ppermute(hidden_face, AXES, back)  1.55 us
    ppermute x1, waiting for transfers between devices, body(): hidden_far = lax.ppermute(hidden_face, AXES, back)  1.37 us
    unnamed x10, local copies, waits for them, and re-layouts  0.97 us
    ppermute x1, waiting for transfers between devices, body(): table_other = lax.ppermute(neighbours, AXES, halves)  0.62 us
    ppermute x2, starting transfers between devices, body(): other = [lax.ppermute(part, AXES, halves) for part in own_parts]  0.51 us
    ppermute x2, starting transfers between devices, weights(): swapped = lax.ppermute(flat, AXES, halves)  0.51 us
  transfers between devices with their start and end apart: 9, of which 3 were waited for; matrix products, arithmetic and copies ran while one was open for 0% of the time, Pallas kernels for 38%

profile of v3, /device:TPU:8, one launch (start us, length us, event | category | flops | bytes accessed | tf_op | source)
XLA Modules:
  0.0 18.4 jit_solution(12824888057242722899)
XLA Ops:
  0.0 0.0 collective-permute-start.1
  0.0 0.5 %collective-permute-start.6 = (bf16[27,48,384]{2,1,0:T(8,128)(2,1)}, bf16[27,48,384]{2,1,0:T(8,128)(2,1)S(1)}, u32[]{:S(2)}, u32[]{:S(2)}) collective-permute-start(bf16[27,48,384]{2,1,0:T(8,128)(2,1)} %bitcast.8), channel_id=1, source_target_pairs={{0,1},{1,0},{2,3},{3,2},{4,5},{5,4},{6,7},{7,6},{8,9},{9,8},{10,11... | collective-permute-start | bytes 2985992 | tf_op jit(solution)/shard_map/ppermute | solution.py:396
  0.5 0.0 copy-start.2
  0.5 0.9 %copy-done.2 = bf16[1,8,8,8,192]{4,3,2,1,0:T(8,128)(2,1)S(1)} copy-done((bf16[1,8,8,8,192]{4,3,2,1,0:T(8,128)(2,1)S(1)}, bf16[1,8,8,8,192]{4,3,2,1,0:T(8,128)(2,1)}, u32[]{:S(2)}) %copy-start.2) | copy-done | bytes 196632
  1.5 0.0 copy-start.4
  1.5 0.0 copy-start
  1.5 0.1 shard_map.55
  1.6 2.4 %collective-permute-start = (bf16[320,192]{1,0:T(8,128)(2,1)S(1)}, bf16[320,192]{1,0:T(8,128)(2,1)S(1)}, u32[]{:S(2)}, u32[]{:S(2)}) collective-permute-start(bf16[320,192]{1,0:T(8,128)(2,1)S(1)} %get-tuple-element.18.refs_1_), channel_id=1, source_target_pairs={{0,1},{1,3},{2,0},{3,5},{4,2},{5,7},{6,4},{7,9},{8,6},{9,11},{10,8... | collective-permute-start | bytes 368648 | tf_op jit(solution)/shard_map/ppermute | solution.py:392
  3.9 0.0 collective-permute-start.3
  3.9 0.5 %collective-permute-start.4 = (bf16[256,192]{1,0:T(8,128)(2,1)S(1)}, bf16[256,192]{1,0:T(8,128)(2,1)S(1)}, u32[]{:S(2)}, u32[]{:S(2)}) collective-permute-start(bf16[256,192]{1,0:T(8,128)(2,1)S(1)} %get-tuple-element.20), channel_id=1, source_target_pairs={{0,1},{1,0},{2,3},{3,2},{4,5},{5,4},{6,7},{7,6},{8,9},{9,8},{10,11... | collective-permute-start | bytes 294920 | tf_op jit(solution)/shard_map/ppermute | solution.py:391
  4.5 0.0 collective-permute-done.1.other_ref
  4.5 0.0 copy-done.4
  4.5 0.1 collective-permute-start.2
  4.5 0.0 copy-done
  4.5 0.4 %shard_map.56.refs_4_.w = bf16[27,192,192]{2,1,0:T(8,128)(2,1)S(1)} custom-call(bf16[27,48,384]{2,1,0:T(8,128)(2,1)S(1)} %bitcast.7, bf16[27,48,384]{2,1,0:T(8,128)(2,1)S(1)} %collective-permute-done.1.other_ref), custom_call_target="tpu_custom_call" | custom-call | tf_op jit(solution)/shard_map/pallas_call | solution.py:355
  5.0 0.6 %collective-permute-done.2.refs_0_ = s32[1,27]{1,0:T(1,128)S(1)} collective-permute-done((s32[1,27]{1,0:T(1,128)S(1)}, s32[1,27]{1,0:T(1,128)S(1)}, u32[]{:S(2)}, u32[]{:S(2)}) %collective-permute-start.2) | collective-permute-done | bytes 140 | tf_op jit(solution)/shard_map/ppermute | solution.py:390
  5.6 0.0 collective-permute-done.3.refs_2_
  5.6 0.0 collective-permute-done.4.refs_3_
  5.6 2.7 %shard_map.57 = (f32[2,512,128]{2,1,0:T(8,128)S(1)}, f32[2,1440,128]{2,1,0:T(8,128)S(1)}, f32[216,128]{1,0:T(8,128)S(1)}) custom-call(s32[1,27]{1,0:T(1,128)S(1)} %collective-permute-done.2.refs_0_, bf16[320,192]{1,0:T(8,128)(2,1)S(1)} %get-tuple-element.18.refs_1_, bf16[256,192]{1,0:T(8,128)(2,1)S(1)} %collective-permute-done.3.refs_2_, ...), custom_call_target="tpu_custom_call" | custom-call | tf_op jit(solution)/shard_map/pallas_call | solution.py:355
  8.3 0.0 copy-start.1
  8.3 0.4 %collective-permute-done.far = bf16[320,192]{1,0:T(8,128)(2,1)S(1)} collective-permute-done((bf16[320,192]{1,0:T(8,128)(2,1)S(1)}, bf16[320,192]{1,0:T(8,128)(2,1)S(1)}, u32[]{:S(2)}, u32[]{:S(2)}) %collective-permute-start) | collective-permute-done | bytes 122912 | tf_op jit(solution)/shard_map/ppermute | solution.py:392
  8.7 0.9 %shard_map.58 = (bf16[320,192]{1,0:T(8,128)(2,1)S(1)}, bf16[256,192]{1,0:T(8,128)(2,1)S(1)}, bf16[256,192]{1,0:T(8,128)(2,1)S(1)}, f32[2,512,128]{2,1,0:T(8,128)S(1)}) custom-call(bf16[320,192]{1,0:T(8,128)(2,1)S(1)} %collective-permute-done.far, bf16[27,192,192]{2,1,0:T(8,128)(2,1)S(1)} %shard_map.56.refs_4_.w, ...), custom_call_target="tpu_custom_call", output_to_operand_aliasing={{3}: (2, {})} | custom-call | tf_op jit(solution)/shard_map/pallas_call | solution.py:355
  9.6 1.5 %collective-permute-start.5 = (bf16[320,192]{1,0:T(8,128)(2,1)S(1)}, bf16[320,192]{1,0:T(8,128)(2,1)S(1)}, u32[]{:S(2)}, u32[]{:S(2)}) collective-permute-start(bf16[320,192]{1,0:T(8,128)(2,1)S(1)} %get-tuple-element.24.refs_1_), channel_id=1, source_target_pairs={{1,0},{3,1},{0,2},{5,3},{2,4},{7,5},{4,6},{9,7},{6,8},{11,9},{8,10... | collective-permute-start | bytes 368648 | tf_op jit(solution)/shard_map/ppermute | solution.py:432
  11.1 0.0 collective-permute-start.7
  11.1 0.5 %collective-permute-start.8 = (bf16[256,192]{1,0:T(8,128)(2,1)S(1)}, bf16[256,192]{1,0:T(8,128)(2,1)S(1)}, u32[]{:S(2)}, u32[]{:S(2)}) collective-permute-start(bf16[256,192]{1,0:T(8,128)(2,1)S(1)} %get-tuple-element.26), channel_id=1, source_target_pairs={{0,1},{1,0},{2,3},{3,2},{4,5},{5,4},{6,7},{7,6},{8,9},{9,8},{10,11... | collective-permute-start | bytes 294920 | tf_op jit(solution)/shard_map/ppermute | solution.py:431
  12.3 0.0 collective-permute-done.6.other_ref
  12.3 0.0 copy-done.1
  12.3 0.4 %shard_map.59.refs_4_.w = bf16[27,192,192]{2,1,0:T(8,128)(2,1)S(1)} custom-call(bf16[27,48,384]{2,1,0:T(8,128)(2,1)S(1)} %bitcast.9, bf16[27,48,384]{2,1,0:T(8,128)(2,1)S(1)} %collective-permute-done.6.other_ref), custom_call_target="tpu_custom_call" | custom-call | tf_op jit(solution)/shard_map/pallas_call | solution.py:355
  12.7 0.0 copy-start.3
  12.7 0.0 collective-permute-done.7.refs_2_
  12.7 0.0 collective-permute-done.8.refs_3_
  12.8 2.6 %shard_map.60 = (f32[2,512,128]{2,1,0:T(8,128)S(1)}, f32[2,1440,128]{2,1,0:T(8,128)S(1)}, f32[216,128]{1,0:T(8,128)S(1)}) custom-call(s32[1,27]{1,0:T(1,128)S(1)} %copy-done.4, bf16[320,192]{1,0:T(8,128)(2,1)S(1)} %get-tuple-element.24.refs_1_, bf16[256,192]{1,0:T(8,128)(2,1)S(1)} %collective-permute-done.7.refs_2_, ...), custom_call_target="tpu_custom_call" | custom-call | tf_op jit(solution)/shard_map/pallas_call | solution.py:355
  15.4 1.4 %collective-permute-done.5.far = bf16[320,192]{1,0:T(8,128)(2,1)S(1)} collective-permute-done((bf16[320,192]{1,0:T(8,128)(2,1)S(1)}, bf16[320,192]{1,0:T(8,128)(2,1)S(1)}, u32[]{:S(2)}, u32[]{:S(2)}) %collective-permute-start.5) | collective-permute-done | bytes 122912 | tf_op jit(solution)/shard_map/ppermute | solution.py:432
  16.7 0.0 copy-done.3
  16.7 1.6 %shard_map.61 = (f32[512,192]{1,0:T(8,128)}, f32[2,512,128]{2,1,0:T(8,128)S(1)}) custom-call(s32[1,1]{1,0:T(1,128)} %bitcast.5.occupancy, bf16[320,192]{1,0:T(8,128)(2,1)S(1)} %collective-permute-done.5.far, bf16[27,192,192]{2,1,0:T(8,128)(2,1)S(1)} %shard_map.59.refs_4_.w, bf16[512,192]{1,0:T(8,128)(2,1)S(1)} %bitcast.11, ...), custom_call_target="tpu_custom_call", output_to_operand_aliasing={{1}: (4, {})} | custom-call | tf_op jit(solution)/shard_map/pallas_call | solution.py:355
Async XLA Ops:
  0.0 4.5 %collective-permute-start.1 = (bf16[27,48,384]{2,1,0:T(8,128)(2,1)}, bf16[27,48,384]{2,1,0:T(8,128)(2,1)S(1)}, u32[]{:S(2)}, u32[]{:S(2)}) collective-permute-start(bf16[27,48,384]{2,1,0:T(8,128)(2,1)} %bitcast.6), channel_id=1, source_target_pairs={{0,1},{1,0},{2,3},{3,2},{4,5},{5,4},{6,7},{7,6},{8,9},{9,8},{10,11... | collective-permute-start | bytes 2985992 | tf_op jit(solution)/shard_map/ppermute | solution.py:396
  0.0 12.3 %collective-permute-start.6 = (bf16[27,48,384]{2,1,0:T(8,128)(2,1)}, bf16[27,48,384]{2,1,0:T(8,128)(2,1)S(1)}, u32[]{:S(2)}, u32[]{:S(2)}) collective-permute-start(bf16[27,48,384]{2,1,0:T(8,128)(2,1)} %bitcast.8), channel_id=1, source_target_pairs={{0,1},{1,0},{2,3},{3,2},{4,5},{5,4},{6,7},{7,6},{8,9},{9,8},{10,11... | collective-permute-start | bytes 2985992 | tf_op jit(solution)/shard_map/ppermute | solution.py:396
  0.5 0.9 %copy-start.2 = (bf16[1,8,8,8,192]{4,3,2,1,0:T(8,128)(2,1)S(1)}, bf16[1,8,8,8,192]{4,3,2,1,0:T(8,128)(2,1)}, u32[]{:S(2)}) copy-start(bf16[1,8,8,8,192]{4,3,2,1,0:T(8,128)(2,1)} %param.5) | copy-start | bytes 589828
  1.5 3.0 %copy-start.4 = (s32[1,27]{1,0:T(1,128)S(1)}, s32[1,27]{1,0:T(1,128)}, u32[]{:S(2)}) copy-start(s32[1,27]{1,0:T(1,128)} %refs_0_.1) | copy-start | bytes 328
  1.5 3.1 %copy-start = (bf16[3,3,3,48,384]{4,3,2,1,0:T(8,128)(2,1)S(1)}, bf16[3,3,3,48,384]{4,3,2,1,0:T(8,128)(2,1)}, u32[]{:S(2)}) copy-start(bf16[3,3,3,48,384]{4,3,2,1,0:T(8,128)(2,1)} %param.8) | copy-start | bytes 2985988
  1.6 7.1 %collective-permute-start = (bf16[320,192]{1,0:T(8,128)(2,1)S(1)}, bf16[320,192]{1,0:T(8,128)(2,1)S(1)}, u32[]{:S(2)}, u32[]{:S(2)}) collective-permute-start(bf16[320,192]{1,0:T(8,128)(2,1)S(1)} %get-tuple-element.18.refs_1_), channel_id=1, source_target_pairs={{0,1},{1,3},{2,0},{3,5},{4,2},{5,7},{6,4},{7,9},{8,6},{9,11},{10,8... | collective-permute-start | bytes 368648 | tf_op jit(solution)/shard_map/ppermute | solution.py:392
  3.9 1.6 %collective-permute-start.3 = (bf16[256,192]{1,0:T(8,128)(2,1)S(1)}, bf16[256,192]{1,0:T(8,128)(2,1)S(1)}, u32[]{:S(2)}, u32[]{:S(2)}) collective-permute-start(bf16[256,192]{1,0:T(8,128)(2,1)S(1)} %get-tuple-element.19), channel_id=1, source_target_pairs={{0,1},{1,0},{2,3},{3,2},{4,5},{5,4},{6,7},{7,6},{8,9},{9,8},{10,11... | collective-permute-start | bytes 294920 | tf_op jit(solution)/shard_map/ppermute | solution.py:391
  3.9 1.6 %collective-permute-start.4 = (bf16[256,192]{1,0:T(8,128)(2,1)S(1)}, bf16[256,192]{1,0:T(8,128)(2,1)S(1)}, u32[]{:S(2)}, u32[]{:S(2)}) collective-permute-start(bf16[256,192]{1,0:T(8,128)(2,1)S(1)} %get-tuple-element.20), channel_id=1, source_target_pairs={{0,1},{1,0},{2,3},{3,2},{4,5},{5,4},{6,7},{7,6},{8,9},{9,8},{10,11... | collective-permute-start | bytes 294920 | tf_op jit(solution)/shard_map/ppermute | solution.py:391
  4.5 1.1 %collective-permute-start.2 = (s32[1,27]{1,0:T(1,128)S(1)}, s32[1,27]{1,0:T(1,128)S(1)}, u32[]{:S(2)}, u32[]{:S(2)}) collective-permute-start(s32[1,27]{1,0:T(1,128)S(1)} %copy-done.4), channel_id=1, source_target_pairs={{0,1},{1,0},{2,3},{3,2},{4,5},{5,4},{6,7},{7,6},{8,9},{9,8},{10,11... | collective-permute-start | bytes 332 | tf_op jit(solution)/shard_map/ppermute | solution.py:390
  8.3 4.0 %copy-start.1 = (bf16[3,3,3,48,384]{4,3,2,1,0:T(8,128)(2,1)S(1)}, bf16[3,3,3,48,384]{4,3,2,1,0:T(8,128)(2,1)}, u32[]{:S(2)}) copy-start(bf16[3,3,3,48,384]{4,3,2,1,0:T(8,128)(2,1)} %param.9) | copy-start | bytes 2985988
  9.6 7.2 %collective-permute-start.5 = (bf16[320,192]{1,0:T(8,128)(2,1)S(1)}, bf16[320,192]{1,0:T(8,128)(2,1)S(1)}, u32[]{:S(2)}, u32[]{:S(2)}) collective-permute-start(bf16[320,192]{1,0:T(8,128)(2,1)S(1)} %get-tuple-element.24.refs_1_), channel_id=1, source_target_pairs={{1,0},{3,1},{0,2},{5,3},{2,4},{7,5},{4,6},{9,7},{6,8},{11,9},{8,10... | collective-permute-start | bytes 368648 | tf_op jit(solution)/shard_map/ppermute | solution.py:432
  11.1 1.6 %collective-permute-start.7 = (bf16[256,192]{1,0:T(8,128)(2,1)S(1)}, bf16[256,192]{1,0:T(8,128)(2,1)S(1)}, u32[]{:S(2)}, u32[]{:S(2)}) collective-permute-start(bf16[256,192]{1,0:T(8,128)(2,1)S(1)} %get-tuple-element.25), channel_id=1, source_target_pairs={{0,1},{1,0},{2,3},{3,2},{4,5},{5,4},{6,7},{7,6},{8,9},{9,8},{10,11... | collective-permute-start | bytes 294920 | tf_op jit(solution)/shard_map/ppermute | solution.py:431
  11.1 1.6 %collective-permute-start.8 = (bf16[256,192]{1,0:T(8,128)(2,1)S(1)}, bf16[256,192]{1,0:T(8,128)(2,1)S(1)}, u32[]{:S(2)}, u32[]{:S(2)}) collective-permute-start(bf16[256,192]{1,0:T(8,128)(2,1)S(1)} %get-tuple-element.26), channel_id=1, source_target_pairs={{0,1},{1,0},{2,3},{3,2},{4,5},{5,4},{6,7},{7,6},{8,9},{9,8},{10,11... | collective-permute-start | bytes 294920 | tf_op jit(solution)/shard_map/ppermute | solution.py:431
  12.7 4.0 %copy-start.3 = (bf16[1,8,8,8,192]{4,3,2,1,0:T(8,128)(2,1)S(1)}, bf16[1,8,8,8,192]{4,3,2,1,0:T(8,128)(2,1)}, u32[]{:S(2)}) copy-start(bf16[1,8,8,8,192]{4,3,2,1,0:T(8,128)(2,1)} %param.5) | copy-start | bytes 589828

commit v4 on v3

--- a/solution.py
+++ b/solution.py
@@ -33,43 +33,49 @@
     return 2 * side * side + 4 * (side - 2) * side
 
 
-def pack_surface(wide, out_ref, side, change=lambda value: value):
+def folded_rows(side, width):
+    return -(-surface_rows(side) * width // LANES)
+
+
+def pack_surface(wide, out_ref, side, width, change=lambda value: value):
     plane = side * side
     inner = (side - 2) * side
     last = side - 1
-    for p, lane, lanes in pieces(out_ref.shape[1]):
+    rows = surface_rows(side)
+    for p, lane, lanes in pieces(width):
         ref = wide.at[p]
-
-        def store(row, value):
-            value = change(value[:, :lanes]).astype(BF16)
-            out_ref[pl.ds(row, value.shape[0]), lane : lane + lanes] = value
-
-        store(0, ref[pl.ds(0, plane), :])
-        store(plane, ref[pl.ds(last * plane, plane), :])
-        row = 2 * plane
+        parts = [ref[pl.ds(0, plane), :], ref[pl.ds(last * plane, plane), :]]
         for y in (0, last):
-            parts = [
-                ref[pl.ds(x * plane + y * side, side), :] for x in range(1, last)
-            ]
-            store(row, jnp.concatenate(parts, axis=0))
-            row += inner
+            for x in range(1, last):
+                parts.append(ref[pl.ds(x * plane + y * side, side), :])
         for z in (0, last):
-            store(row, ref[pl.ds(plane + z, inner, stride=side), :])
-            row += inner
-
-
-def spread_surface(packed_ref, faces, slot, side):
+            parts.append(ref[pl.ds(plane + z, inner, stride=side), :])
+        value = change(jnp.concatenate(parts, axis=0))
+        folds = LANES // lanes
+        count = rows // folds
+        result = value[:count]
+        position = lax.broadcasted_iota(jnp.int32, (count, LANES), 1)
+        for n in range(1, folds):
+            part = pltpu.roll(value[n * count : (n + 1) * count], n * lanes, axis=1)
+            result = jnp.where(position >= n * lanes, part, result)
+        out_ref[pl.ds(p * rows, count), :] = result.astype(BF16)
+
+
+def spread_surface(packed_ref, faces, slot, side, width):
     plane = side * side
     inner = (side - 2) * side
     last = side - 1
     base = slot * 6 * plane
-    packed = packed_ref[...].astype(F32)
-    for p, lane, lanes in pieces(packed.shape[1]):
+    rows = surface_rows(side)
+    for p, lane, lanes in pieces(width):
         ref = faces.at[p]
-        part = packed[:, lane : lane + lanes]
-        if lanes < LANES:
-            pad = jnp.zeros((part.shape[0], LANES - lanes), F32)
-            part = jnp.concatenate([part, pad], axis=1)
+        folds = LANES // lanes
+        part = packed_ref[pl.ds(p * rows, rows // folds), :].astype(F32)
+        if folds > 1:
+            turned = [part] + [
+                pltpu.roll(part, LANES - n * lanes, axis=1) for n in range(1, folds)
+            ]
+            part = jnp.concatenate(turned, axis=0)
         ref[pl.ds(base, 2 * plane), :] = part[: 2 * plane]
         row = 2 * plane
         for f in range(2, 6):
@@ -109,7 +115,7 @@
 def pack_kernel(x_ref, out_ref, *refs, side):
     *pieces_out, wide = refs
     fill(wide, 0, x_ref[...].astype(F32))
-    pack_surface(wide, out_ref, side)
+    pack_surface(wide, out_ref, side, x_ref.shape[1])
     share(x_ref[...], pieces_out)
 
 
@@ -117,6 +123,12 @@
     for n, ref in enumerate(refs):
         count = ref.shape[0]
         ref[...] = value[n * count : (n + 1) * count]
+
+
+def weight_rows(width, tap):
+    return [
+        (lane, 9 * lane + tap * lanes, lanes) for _, lane, lanes in pieces(width)
+    ]
 
 
 def weights_kernel(own_ref, other_ref, out_ref):
@@ -124,12 +136,29 @@
     taps, depth, both = own_ref.shape
     width = out_ref.shape[2]
     half = depth * (both // width)
-    for ref, place in ((own_ref, core), (other_ref, 1 - core)):
-        for group in range(both // width):
-            row = pl.multiple_of(place * half + group * depth, 16)
-            out_ref[:, pl.ds(row, depth), :] = ref[
-                :, :, group * width : (group + 1) * width
-            ]
+    step = 16
+    for tap in range(taps):
+        rows = {}
+        for channel, row, count in weight_rows(width, tap % 9):
+            for n in range(0, count, step):
+                rows[channel + n] = row + n
+        for ref, place in ((own_ref, core), (other_ref, 1 - core)):
+            for group in range(both // width):
+                lane = group * width
+                value = ref[tap, :, lane : lane + width]
+                for n in range(0, depth, step):
+                    at = group * depth + n
+                    row = jnp.where(place == 0, rows[at], rows[at + half])
+                    row = pl.multiple_of(row, step)
+                    out_ref[tap // 9, pl.ds(row, step), :] = value[n : n + step]
+
+
+def tap_weights(w, tap):
+    third, tap = divmod(tap, 9)
+    return jnp.concatenate(
+        [w[third, pl.ds(row, count), :] for _, row, count in weight_rows(w.shape[2], tap)],
+        axis=0,
+    )
 
 
 def shifts(middle, low, high, mask):
@@ -142,44 +171,53 @@
 
 
 def inside_kernel(*refs, side, block_of):
-    table, beside, *centers, w, total, near, masks, wide, faces, even, odd = refs
+    table_ref, beside, *centers, w, total, near, masks = refs[:-5]
+    wide, faces, lhs, table, semaphore = refs[-5:]
+    copy = pltpu.make_async_copy(table_ref, table, semaphore)
+    copy.start()
     width = w.shape[2]
-    rows, plane = total.shape[1], side * side
+    plane = side * side
     for n, part in enumerate(centers):
         fill(wide, n * part.shape[0], part[...].astype(F32))
-    fill(faces, 0, jnp.zeros((6 * plane, width), F32))
-    spread_surface(beside, faces, 1, side)
-    cut_surface(wide, faces, 2, side)
-    choose_near(table, block_of(), faces, near, masks, side)
     mask = lax.broadcasted_iota(jnp.int32, (side, side, LANES), 1)
     nothing = jnp.zeros((side, side, LANES), F32)
-    edge = jnp.zeros((3, side, side, width), BF16)
-    even[:, :, 0:side, :] = edge
-    even[:, :, side + plane : plane + 2 * side, :] = edge
+    edge = jnp.zeros((1, side, LANES), F32)
     for p, lane, lanes in pieces(width):
+        folds = LANES // lanes
         for x in range(side):
             middle = wide[p, pl.ds(x * plane, plane), :].reshape(side, side, LANES)
-            for k, value in enumerate(shifts(middle, nothing, nothing, mask)):
-                value = value.reshape(plane, LANES)[:, :lanes].astype(BF16)
-                even[k, x, side : side + plane, lane : lane + lanes] = value
-                odd[k, x, :, lane : lane + lanes] = value
+            if folds > 1:
+                position = lax.broadcasted_iota(jnp.int32, middle.shape, 2)
+                for n in range(1, folds):
+                    turned = pltpu.roll(middle, n * lanes, axis=2)
+                    middle = jnp.where(position >= n * lanes, turned, middle)
+            moved = shifts(middle, nothing, nothing, mask)
+            taps = []
+            for j in range(3):
+                for k in range(3):
+                    value = moved[k]
+                    if j == 0:
+                        value = jnp.concatenate([edge, value[: side - 1]], axis=0)
+                    elif j == 2:
+                        value = jnp.concatenate([value[1:], edge], axis=0)
+                    taps.append(value.reshape(plane, LANES))
+            for t in range(0, 9, folds):
+                value = taps[t]
+                used = min(folds, 9 - t)
+                for n in range(1, used):
+                    position = lax.broadcasted_iota(jnp.int32, value.shape, 1)
+                    value = jnp.where(position >= n * lanes, taps[t + n], value)
+                at = 9 * lane + t * lanes
+                lhs[pl.ds(x * plane, plane), at : at + used * lanes] = value[
+                    :, : used * lanes
+                ].astype(BF16)
     for i in (1, 0, 2):
-        first, count = (1, 0, 0)[i], side - (i != 1)
-        source = (0, 0, 1)[i]
-        acc = jnp.zeros((count * plane, width), F32)
-        for j in range(3):
-            for k in range(3):
-                if j == 1:
-                    part = odd[k, source : source + count]
-                else:
-                    part = even[
-                        k, source : source + count, j * side : j * side + plane
-                    ]
-                acc += jnp.dot(
-                    part.reshape(count * plane, width),
-                    w[9 * i + 3 * j + k],
-                    preferred_element_type=F32,
-                )
+        first, source, count = (1, 0, 0)[i], (0, 0, 1)[i], side - (i != 1)
+        acc = jnp.dot(
+            lhs[pl.ds(source * plane, count * plane), :],
+            w[i],
+            preferred_element_type=F32,
+        )
         for p, lane, lanes in pieces(width):
             part = acc[:, lane : lane + lanes]
             place = pl.ds(first * plane, count * plane)
@@ -187,6 +225,11 @@
                 total[p, place, 0:lanes] = part
             else:
                 total[p, place, 0:lanes] += part
+    fill(faces, 0, jnp.zeros((6 * plane, width), F32))
+    spread_surface(beside, faces, 1, side, width)
+    cut_surface(wide, faces, 2, side)
+    copy.wait()
+    choose_near(table, block_of(), faces, near, masks, side)
 
 
 def borders(side):
@@ -241,7 +284,7 @@
     width = w.shape[2]
     plane = side * side
     last = side - 1
-    spread_surface(far, faces, 0, side)
+    spread_surface(far, faces, 0, side, width)
     mask = lax.broadcasted_iota(jnp.int32, (side, side, LANES), 1)
     for group, to, count, row, face, offsets in borders(side):
         for p, lane, lanes in pieces(width):
@@ -292,7 +335,7 @@
                     continue
                 product = jnp.dot(
                     jnp.concatenate(parts, axis=0),
-                    w[9 * i + 3 * j + k],
+                    tap_weights(w, 9 * i + 3 * j + k),
                     preferred_element_type=F32,
                 )
                 for n, group in enumerate(groups):
@@ -324,7 +367,7 @@
     def change(value):
         return jnp.maximum(value, 0.0) * active[:, : value.shape[1]]
 
-    pack_surface(total, surface, side, change)
+    pack_surface(total, surface, side, w.shape[2], change)
     for p, lane, lanes in pieces(w.shape[2]):
         for n, out in enumerate(outs):
             count = out.shape[0]
@@ -350,13 +393,13 @@
     return 2 * lax.axis_index("space") + lax.axis_index("wt")
 
 
-def call(kernel, operands, outs, scratch=(), scalars=0, cost=0, aliases={}):
+def call(kernel, operands, outs, scratch=(), anywhere=0, cost=0, aliases={}):
     outs = [jax.ShapeDtypeStruct(shape, kind) for shape, kind in outs]
     result = pl.pallas_call(
         kernel,
         out_shape=outs,
-        in_specs=[pl.BlockSpec(memory_space=SMEM)] * scalars
-        + [pl.BlockSpec(memory_space=VMEM)] * (len(operands) - scalars),
+        in_specs=[pl.BlockSpec(memory_space=pl.ANY)] * anywhere
+        + [pl.BlockSpec(memory_space=VMEM)] * (len(operands) - anywhere),
         out_specs=[pl.BlockSpec(memory_space=VMEM)] * len(outs),
         scratch_shapes=list(scratch),
         input_output_aliases=aliases,
@@ -374,7 +417,7 @@
     cycle = [(i, i - 2) if i % 2 == 0 else (i, i + 2) for i in range(total)]
     cycle[0], cycle[-1] = (0, 1), (total - 1, total - 2)
     back = [(j, i) for i, j in cycle]
-    face = ((surface_rows(side), width), BF16)
+    face = ((folded_rows(side, width), LANES), BF16)
     piece = ((rows // PARTS, width), BF16)
     wide = ((rows, width), F32)
     count = len(pieces(width))
@@ -394,7 +437,7 @@
     def weights(kernel):
         flat = kernel.reshape((27,) + kernel.shape[3:])
         swapped = lax.ppermute(flat, AXES, halves)
-        return call(weights_kernel, (flat, swapped), [((27, width, width), BF16)])
+        return call(weights_kernel, (flat, swapped), [((3, 9 * width, width), BF16)])
 
     w_one, w_two = weights(kernel_one), weights(kernel_two)
 
@@ -410,10 +453,11 @@
             [
                 VMEM((count, rows, LANES), F32),
                 VMEM((count, 3 * 6 * plane, LANES), F32),
-                VMEM((3, side, plane + 2 * side, width), BF16),
-                VMEM((3, side, plane, width), BF16),
+                VMEM((rows, 9 * width), BF16),
+                SMEM(table.shape, jnp.int32),
+                pltpu.SemaphoreType.DMA,
             ],
-            scalars=1,
+            anywhere=1,
         )
 
     planes = [

time: 18.6 us -> 17.4 us (0.935)
  Pallas kernels: 8.71 us -> 7.29 us
  waiting for transfers between devices: 2.41 us -> 2.7 us
    pallas_call x7, Pallas kernels: 8.71 us -> 7.29 us  [call(): pl.pallas_call(kernel, out_shape=outs, in_specs=[pl.BlockSpec(memory_spac...]
    ppermute x1, waiting for transfers between devices: 1.37 us -> 1.71 us  [body(): hidden_far = lax.ppermute(hidden_face, AXES, back)]
  transfers between devices with their start and end apart: 9 -> 9, of which waited for: 3 -> 3; matrix products, arithmetic and copies ran while one was open for 0% -> 0% of each run, Pallas kernels for 38% -> 32%
where the time goes in v4:
time: 17.4 us; the launch traced here: 17.3 us
  Pallas kernels  7.29 us (42%)
  starting transfers between devices  5.53 us (32%)
  waiting for transfers between devices  2.7 us (16%)
  local copies, waits for them, and re-layouts  0.97 us (6%)
  between operations  0.75 us (4%)
    pallas_call x7, Pallas kernels, call(): pl.pallas_call(kernel, out_shape=outs, in_specs=[pl.BlockSpec(memory_spac...  7.29 us
    ppermute x1, starting transfers between devices, body(): far = lax.ppermute(own_face, AXES, cycle)  2.39 us
    ppermute x1, waiting for transfers between devices, body(): hidden_far = lax.ppermute(hidden_face, AXES, back)  1.71 us
    ppermute x1, starting transfers between devices, body(): hidden_far = lax.ppermute(hidden_face, AXES, back)  1.54 us
    unnamed x10, local copies, waits for them, and re-layouts  0.97 us
    ppermute x1, waiting for transfers between devices, body(): table_other = lax.ppermute(neighbours, AXES, halves)  0.57 us
    ppermute x2, starting transfers between devices, body(): other = [lax.ppermute(part, AXES, halves) for part in own_parts]  0.51 us
    ppermute x2, starting transfers between devices, weights(): swapped = lax.ppermute(flat, AXES, halves)  0.51 us
  transfers between devices with their start and end apart: 9, of which 3 were waited for; matrix products, arithmetic and copies ran while one was open for 0% of the time, Pallas kernels for 32%

profile of v4, /device:TPU:8, one launch (start us, length us, event | category | flops | bytes accessed | tf_op | source)
XLA Modules:
  0.0 17.3 jit_solution(16089023229158036856)
XLA Ops:
  0.0 0.0 collective-permute-start.1
  0.0 0.5 %collective-permute-start.6 = (bf16[27,48,384]{2,1,0:T(8,128)(2,1)}, bf16[27,48,384]{2,1,0:T(8,128)(2,1)S(1)}, u32[]{:S(2)}, u32[]{:S(2)}) collective-permute-start(bf16[27,48,384]{2,1,0:T(8,128)(2,1)} %bitcast.8), channel_id=1, source_target_pairs={{0,1},{1,0},{2,3},{3,2},{4,5},{5,4},{6,7},{7,6},{8,9},{9,8},{10,11... | collective-permute-start | bytes 2985992 | tf_op jit(solution)/shard_map/ppermute | solution.py:439
  0.5 0.0 copy-start.2
  0.5 0.9 %copy-done.2 = bf16[1,8,8,8,192]{4,3,2,1,0:T(8,128)(2,1)S(1)} copy-done((bf16[1,8,8,8,192]{4,3,2,1,0:T(8,128)(2,1)S(1)}, bf16[1,8,8,8,192]{4,3,2,1,0:T(8,128)(2,1)}, u32[]{:S(2)}) %copy-start.2) | copy-done | bytes 196632
  1.5 0.0 copy-start.4
  1.5 0.0 copy-start
  1.5 0.1 shard_map.55
  1.6 2.4 %collective-permute-start = (bf16[480,128]{1,0:T(8,128)(2,1)S(1)}, bf16[480,128]{1,0:T(8,128)(2,1)S(1)}, u32[]{:S(2)}, u32[]{:S(2)}) collective-permute-start(bf16[480,128]{1,0:T(8,128)(2,1)S(1)} %get-tuple-element.18.refs_1_), channel_id=1, source_target_pairs={{0,1},{1,3},{2,0},{3,5},{4,2},{5,7},{6,4},{7,9},{8,6},{9,11},{10,8... | collective-permute-start | bytes 368648 | tf_op jit(solution)/shard_map/ppermute | solution.py:435
  4.0 0.0 collective-permute-start.3
  4.0 0.5 %collective-permute-start.4 = (bf16[256,192]{1,0:T(8,128)(2,1)S(1)}, bf16[256,192]{1,0:T(8,128)(2,1)S(1)}, u32[]{:S(2)}, u32[]{:S(2)}) collective-permute-start(bf16[256,192]{1,0:T(8,128)(2,1)S(1)} %get-tuple-element.20), channel_id=1, source_target_pairs={{0,1},{1,0},{2,3},{3,2},{4,5},{5,4},{6,7},{7,6},{8,9},{9,8},{10,11... | collective-permute-start | bytes 294920 | tf_op jit(solution)/shard_map/ppermute | solution.py:434
  4.5 0.0 collective-permute-done.1.other_ref
  4.5 0.0 copy-done.4
  4.5 0.1 collective-permute-start.2
  4.6 0.0 copy-done
  4.6 0.5 %shard_map.56.refs_4_.w = bf16[3,1728,192]{2,1,0:T(8,128)(2,1)S(1)} custom-call(bf16[27,48,384]{2,1,0:T(8,128)(2,1)S(1)} %bitcast.7, bf16[27,48,384]{2,1,0:T(8,128)(2,1)S(1)} %collective-permute-done.1.other_ref), custom_call_target="tpu_custom_call" | custom-call | tf_op jit(solution)/shard_map/pallas_call | solution.py:398
  5.0 0.6 %collective-permute-done.2.refs_0_ = s32[1,27]{1,0:T(1,128)S(1)} collective-permute-done((s32[1,27]{1,0:T(1,128)S(1)}, s32[1,27]{1,0:T(1,128)S(1)}, u32[]{:S(2)}, u32[]{:S(2)}) %collective-permute-start.2) | collective-permute-done | bytes 140 | tf_op jit(solution)/shard_map/ppermute | solution.py:433
  5.6 0.0 collective-permute-done.3.refs_2_
  5.6 0.0 collective-permute-done.4.refs_3_
  5.6 1.8 %shard_map.57 = (f32[2,512,128]{2,1,0:T(8,128)S(1)}, f32[2,1440,128]{2,1,0:T(8,128)S(1)}, f32[216,128]{1,0:T(8,128)S(1)}) custom-call(s32[1,27]{1,0:T(1,128)S(1)} %collective-permute-done.2.refs_0_, bf16[480,128]{1,0:T(8,128)(2,1)S(1)} %get-tuple-element.18.refs_1_, bf16[256,192]{1,0:T(8,128)(2,1)S(1)} %collective-permute-done.3.refs_2_, ...), custom_call_target="tpu_custom_call" | custom-call | tf_op jit(solution)/shard_map/pallas_call | solution.py:398
  7.4 0.0 copy-start.1
  7.4 0.4 %collective-permute-done.far = bf16[480,128]{1,0:T(8,128)(2,1)S(1)} collective-permute-done((bf16[480,128]{1,0:T(8,128)(2,1)S(1)}, bf16[480,128]{1,0:T(8,128)(2,1)S(1)}, u32[]{:S(2)}, u32[]{:S(2)}) %collective-permute-start) | collective-permute-done | bytes 122912 | tf_op jit(solution)/shard_map/ppermute | solution.py:435
  7.8 1.0 %shard_map.58 = (bf16[480,128]{1,0:T(8,128)(2,1)S(1)}, bf16[256,192]{1,0:T(8,128)(2,1)S(1)}, bf16[256,192]{1,0:T(8,128)(2,1)S(1)}, f32[2,512,128]{2,1,0:T(8,128)S(1)}) custom-call(bf16[480,128]{1,0:T(8,128)(2,1)S(1)} %collective-permute-done.far, bf16[3,1728,192]{2,1,0:T(8,128)(2,1)S(1)} %shard_map.56.refs_4_.w, ...), custom_call_target="tpu_custom_call", output_to_operand_aliasing={{3}: (2, {})} | custom-call | tf_op jit(solution)/shard_map/pallas_call | solution.py:398
  8.8 1.5 %collective-permute-start.5 = (bf16[480,128]{1,0:T(8,128)(2,1)S(1)}, bf16[480,128]{1,0:T(8,128)(2,1)S(1)}, u32[]{:S(2)}, u32[]{:S(2)}) collective-permute-start(bf16[480,128]{1,0:T(8,128)(2,1)S(1)} %get-tuple-element.24.refs_1_), channel_id=1, source_target_pairs={{1,0},{3,1},{0,2},{5,3},{2,4},{7,5},{4,6},{9,7},{6,8},{11,9},{8,10... | collective-permute-start | bytes 368648 | tf_op jit(solution)/shard_map/ppermute | solution.py:476
  10.4 0.0 collective-permute-start.7
  10.4 0.5 %collective-permute-start.8 = (bf16[256,192]{1,0:T(8,128)(2,1)S(1)}, bf16[256,192]{1,0:T(8,128)(2,1)S(1)}, u32[]{:S(2)}, u32[]{:S(2)}) collective-permute-start(bf16[256,192]{1,0:T(8,128)(2,1)S(1)} %get-tuple-element.26), channel_id=1, source_target_pairs={{0,1},{1,0},{2,3},{3,2},{4,5},{5,4},{6,7},{7,6},{8,9},{9,8},{10,11... | collective-permute-start | bytes 294920 | tf_op jit(solution)/shard_map/ppermute | solution.py:475
  11.5 0.0 collective-permute-done.6.other_ref
  11.5 0.0 copy-done.1
  11.5 0.5 %shard_map.59.refs_4_.w = bf16[3,1728,192]{2,1,0:T(8,128)(2,1)S(1)} custom-call(bf16[27,48,384]{2,1,0:T(8,128)(2,1)S(1)} %bitcast.9, bf16[27,48,384]{2,1,0:T(8,128)(2,1)S(1)} %collective-permute-done.6.other_ref), custom_call_target="tpu_custom_call" | custom-call | tf_op jit(solution)/shard_map/pallas_call | solution.py:398
  12.0 0.0 copy-start.3
  12.0 0.0 collective-permute-done.7.refs_2_
  12.0 0.0 collective-permute-done.8.refs_3_
  12.1 1.8 %shard_map.60 = (f32[2,512,128]{2,1,0:T(8,128)S(1)}, f32[2,1440,128]{2,1,0:T(8,128)S(1)}, f32[216,128]{1,0:T(8,128)S(1)}) custom-call(s32[1,27]{1,0:T(1,128)S(1)} %copy-done.4, bf16[480,128]{1,0:T(8,128)(2,1)S(1)} %get-tuple-element.24.refs_1_, bf16[256,192]{1,0:T(8,128)(2,1)S(1)} %collective-permute-done.7.refs_2_, ...), custom_call_target="tpu_custom_call" | custom-call | tf_op jit(solution)/shard_map/pallas_call | solution.py:398
  13.8 1.7 %collective-permute-done.5.far = bf16[480,128]{1,0:T(8,128)(2,1)S(1)} collective-permute-done((bf16[480,128]{1,0:T(8,128)(2,1)S(1)}, bf16[480,128]{1,0:T(8,128)(2,1)S(1)}, u32[]{:S(2)}, u32[]{:S(2)}) %collective-permute-start.5) | collective-permute-done | bytes 122912 | tf_op jit(solution)/shard_map/ppermute | solution.py:476
  15.6 0.0 copy-done.3
  15.6 1.7 %shard_map.61 = (f32[512,192]{1,0:T(8,128)}, f32[2,512,128]{2,1,0:T(8,128)S(1)}) custom-call(s32[1,1]{1,0:T(1,128)} %bitcast.5.occupancy, bf16[480,128]{1,0:T(8,128)(2,1)S(1)} %collective-permute-done.5.far, bf16[3,1728,192]{2,1,0:T(8,128)(2,1)S(1)} %shard_map.59.refs_4_.w, bf16[512,192]{1,0:T(8,128)(2,1)S(1)} %bitcast.11, ...), custom_call_target="tpu_custom_call", output_to_operand_aliasing={{1}: (4, {})} | custom-call | tf_op jit(solution)/shard_map/pallas_call | solution.py:398
Async XLA Ops:
  0.0 4.5 %collective-permute-start.1 = (bf16[27,48,384]{2,1,0:T(8,128)(2,1)}, bf16[27,48,384]{2,1,0:T(8,128)(2,1)S(1)}, u32[]{:S(2)}, u32[]{:S(2)}) collective-permute-start(bf16[27,48,384]{2,1,0:T(8,128)(2,1)} %bitcast.6), channel_id=1, source_target_pairs={{0,1},{1,0},{2,3},{3,2},{4,5},{5,4},{6,7},{7,6},{8,9},{9,8},{10,11... | collective-permute-start | bytes 2985992 | tf_op jit(solution)/shard_map/ppermute | solution.py:439
  0.0 11.5 %collective-permute-start.6 = (bf16[27,48,384]{2,1,0:T(8,128)(2,1)}, bf16[27,48,384]{2,1,0:T(8,128)(2,1)S(1)}, u32[]{:S(2)}, u32[]{:S(2)}) collective-permute-start(bf16[27,48,384]{2,1,0:T(8,128)(2,1)} %bitcast.8), channel_id=1, source_target_pairs={{0,1},{1,0},{2,3},{3,2},{4,5},{5,4},{6,7},{7,6},{8,9},{9,8},{10,11... | collective-permute-start | bytes 2985992 | tf_op jit(solution)/shard_map/ppermute | solution.py:439
  0.5 0.9 %copy-start.2 = (bf16[1,8,8,8,192]{4,3,2,1,0:T(8,128)(2,1)S(1)}, bf16[1,8,8,8,192]{4,3,2,1,0:T(8,128)(2,1)}, u32[]{:S(2)}) copy-start(bf16[1,8,8,8,192]{4,3,2,1,0:T(8,128)(2,1)} %param.5) | copy-start | bytes 589828
  1.5 3.0 %copy-start.4 = (s32[1,27]{1,0:T(1,128)S(1)}, s32[1,27]{1,0:T(1,128)}, u32[]{:S(2)}) copy-start(s32[1,27]{1,0:T(1,128)} %refs_0_.1) | copy-start | bytes 328
  1.5 3.1 %copy-start = (bf16[3,3,3,48,384]{4,3,2,1,0:T(8,128)(2,1)S(1)}, bf16[3,3,3,48,384]{4,3,2,1,0:T(8,128)(2,1)}, u32[]{:S(2)}) copy-start(bf16[3,3,3,48,384]{4,3,2,1,0:T(8,128)(2,1)} %param.8) | copy-start | bytes 2985988
  1.6 6.2 %collective-permute-start = (bf16[480,128]{1,0:T(8,128)(2,1)S(1)}, bf16[480,128]{1,0:T(8,128)(2,1)S(1)}, u32[]{:S(2)}, u32[]{:S(2)}) collective-permute-start(bf16[480,128]{1,0:T(8,128)(2,1)S(1)} %get-tuple-element.18.refs_1_), channel_id=1, source_target_pairs={{0,1},{1,3},{2,0},{3,5},{4,2},{5,7},{6,4},{7,9},{8,6},{9,11},{10,8... | collective-permute-start | bytes 368648 | tf_op jit(solution)/shard_map/ppermute | solution.py:435
  4.0 1.6 %collective-permute-start.3 = (bf16[256,192]{1,0:T(8,128)(2,1)S(1)}, bf16[256,192]{1,0:T(8,128)(2,1)S(1)}, u32[]{:S(2)}, u32[]{:S(2)}) collective-permute-start(bf16[256,192]{1,0:T(8,128)(2,1)S(1)} %get-tuple-element.19), channel_id=1, source_target_pairs={{0,1},{1,0},{2,3},{3,2},{4,5},{5,4},{6,7},{7,6},{8,9},{9,8},{10,11... | collective-permute-start | bytes 294920 | tf_op jit(solution)/shard_map/ppermute | solution.py:434
  4.0 1.6 %collective-permute-start.4 = (bf16[256,192]{1,0:T(8,128)(2,1)S(1)}, bf16[256,192]{1,0:T(8,128)(2,1)S(1)}, u32[]{:S(2)}, u32[]{:S(2)}) collective-permute-start(bf16[256,192]{1,0:T(8,128)(2,1)S(1)} %get-tuple-element.20), channel_id=1, source_target_pairs={{0,1},{1,0},{2,3},{3,2},{4,5},{5,4},{6,7},{7,6},{8,9},{9,8},{10,11... | collective-permute-start | bytes 294920 | tf_op jit(solution)/shard_map/ppermute | solution.py:434
  4.5 1.1 %collective-permute-start.2 = (s32[1,27]{1,0:T(1,128)S(1)}, s32[1,27]{1,0:T(1,128)S(1)}, u32[]{:S(2)}, u32[]{:S(2)}) collective-permute-start(s32[1,27]{1,0:T(1,128)S(1)} %copy-done.4), channel_id=1, source_target_pairs={{0,1},{1,0},{2,3},{3,2},{4,5},{5,4},{6,7},{7,6},{8,9},{9,8},{10,11... | collective-permute-start | bytes 332 | tf_op jit(solution)/shard_map/ppermute | solution.py:433
  7.4 4.1 %copy-start.1 = (bf16[3,3,3,48,384]{4,3,2,1,0:T(8,128)(2,1)S(1)}, bf16[3,3,3,48,384]{4,3,2,1,0:T(8,128)(2,1)}, u32[]{:S(2)}) copy-start(bf16[3,3,3,48,384]{4,3,2,1,0:T(8,128)(2,1)} %param.9) | copy-start | bytes 2985988
  8.8 6.7 %collective-permute-start.5 = (bf16[480,128]{1,0:T(8,128)(2,1)S(1)}, bf16[480,128]{1,0:T(8,128)(2,1)S(1)}, u32[]{:S(2)}, u32[]{:S(2)}) collective-permute-start(bf16[480,128]{1,0:T(8,128)(2,1)S(1)} %get-tuple-element.24.refs_1_), channel_id=1, source_target_pairs={{1,0},{3,1},{0,2},{5,3},{2,4},{7,5},{4,6},{9,7},{6,8},{11,9},{8,10... | collective-permute-start | bytes 368648 | tf_op jit(solution)/shard_map/ppermute | solution.py:476
  10.4 1.7 %collective-permute-start.7 = (bf16[256,192]{1,0:T(8,128)(2,1)S(1)}, bf16[256,192]{1,0:T(8,128)(2,1)S(1)}, u32[]{:S(2)}, u32[]{:S(2)}) collective-permute-start(bf16[256,192]{1,0:T(8,128)(2,1)S(1)} %get-tuple-element.25), channel_id=1, source_target_pairs={{0,1},{1,0},{2,3},{3,2},{4,5},{5,4},{6,7},{7,6},{8,9},{9,8},{10,11... | collective-permute-start | bytes 294920 | tf_op jit(solution)/shard_map/ppermute | solution.py:475
  10.4 1.7 %collective-permute-start.8 = (bf16[256,192]{1,0:T(8,128)(2,1)S(1)}, bf16[256,192]{1,0:T(8,128)(2,1)S(1)}, u32[]{:S(2)}, u32[]{:S(2)}) collective-permute-start(bf16[256,192]{1,0:T(8,128)(2,1)S(1)} %get-tuple-element.26), channel_id=1, source_target_pairs={{0,1},{1,0},{2,3},{3,2},{4,5},{5,4},{6,7},{7,6},{8,9},{9,8},{10,11... | collective-permute-start | bytes 294920 | tf_op jit(solution)/shard_map/ppermute | solution.py:475
  12.0 3.5 %copy-start.3 = (bf16[1,8,8,8,192]{4,3,2,1,0:T(8,128)(2,1)S(1)}, bf16[1,8,8,8,192]{4,3,2,1,0:T(8,128)(2,1)}, u32[]{:S(2)}) copy-start(bf16[1,8,8,8,192]{4,3,2,1,0:T(8,128)(2,1)} %param.5) | copy-start | bytes 589828

commit v5 on v4

--- a/solution.py
+++ b/solution.py
@@ -9,6 +9,7 @@
 
 PARTS = 2
 PACK_COST = 4 * 10**9
+FIRST_COST = 18 * 10**9
 AXES = ("space", "wt")
 VMEM = pltpu.VMEM
 SMEM = pltpu.SMEM
@@ -471,6 +472,7 @@
         [face] + [piece] * PARTS + [sums],
         planes,
         aliases={2: 1 + PARTS},
+        cost=FIRST_COST,
     )
     hidden_own = [lax.ppermute(part, AXES, halves) for part in hidden]
     hidden_far = lax.ppermute(hidden_face, AXES, back)

time: 17.4 us -> 17.1 us (0.983)
  the two profiles are of different devices: /device:TPU:8 before, /device:TPU:0 now
where the time goes in v5:
time: 17.1 us; the launch traced here: 17 us
  starting transfers between devices  7.68 us (45%)
  Pallas kernels  7.28 us (43%)
  local copies, waits for them, and re-layouts  0.97 us (6%)
  between operations  0.76 us (4%)
  waiting for transfers between devices  0.29 us (2%)
    pallas_call x7, Pallas kernels, call(): pl.pallas_call(kernel, out_shape=outs, in_specs=[pl.BlockSpec(memory_spac...  7.28 us
    ppermute x1, starting transfers between devices, body(): hidden_far = lax.ppermute(hidden_face, AXES, back)  3.36 us
    ppermute x2, starting transfers between devices, body(): other = [lax.ppermute(part, AXES, halves) for part in own_parts]  2.66 us
    unnamed x10, local copies, waits for them, and re-layouts  0.97 us
    ppermute x2, starting transfers between devices, weights(): swapped = lax.ppermute(flat, AXES, halves)  0.53 us
    ppermute x2, starting transfers between devices, body(): hidden_own = [lax.ppermute(part, AXES, halves) for part in hidden]  0.51 us
    ppermute x1, starting transfers between devices, body(): table_other = lax.ppermute(neighbours, AXES, halves)  0.51 us
  transfers between devices with their start and end apart: 9, of which 1 were waited for; matrix products, arithmetic and copies ran while one was open for 0% of the time, Pallas kernels for 33%

profile of v5, /device:TPU:0, one launch (start us, length us, event | category | flops | bytes accessed | tf_op | source)
XLA Modules:
  0.0 17.0 jit_solution(15378708969834715484)
XLA Ops:
  0.0 0.5 %collective-permute-start.1 = (bf16[27,48,384]{2,1,0:T(8,128)(2,1)}, bf16[27,48,384]{2,1,0:T(8,128)(2,1)S(1)}, u32[]{:S(2)}, u32[]{:S(2)}) collective-permute-start(bf16[27,48,384]{2,1,0:T(8,128)(2,1)} %bitcast.6), channel_id=1, source_target_pairs={{0,1},{1,0},{2,3},{3,2},{4,5},{5,4},{6,7},{7,6},{8,9},{9,8},{10,11... | collective-permute-start | bytes 2985992 | tf_op jit(solution)/shard_map/ppermute | solution.py:440
  0.5 0.0 copy-start.2
  0.5 0.9 %copy-done.2 = bf16[1,8,8,8,192]{4,3,2,1,0:T(8,128)(2,1)S(1)} copy-done((bf16[1,8,8,8,192]{4,3,2,1,0:T(8,128)(2,1)S(1)}, bf16[1,8,8,8,192]{4,3,2,1,0:T(8,128)(2,1)}, u32[]{:S(2)}) %copy-start.2) | copy-done | bytes 196632
  1.4 0.0 copy-start.4
  1.4 0.0 copy-start.1
  1.4 0.0 copy-start
  1.4 0.1 shard_map.55
  1.5 0.1 collective-permute-start
  1.6 2.7 %collective-permute-start.3 = (bf16[256,192]{1,0:T(8,128)(2,1)S(1)}, bf16[256,192]{1,0:T(8,128)(2,1)S(1)}, u32[]{:S(2)}, u32[]{:S(2)}) collective-permute-start(bf16[256,192]{1,0:T(8,128)(2,1)S(1)} %get-tuple-element.19), channel_id=1, source_target_pairs={{0,1},{1,0},{2,3},{3,2},{4,5},{5,4},{6,7},{7,6},{8,9},{9,8},{10,11... | collective-permute-start | bytes 294920 | tf_op jit(solution)/shard_map/ppermute | solution.py:435
  4.3 0.0 collective-permute-start.4
  4.3 0.0 copy-done.4
  4.3 0.5 %collective-permute-start.2 = (s32[1,27]{1,0:T(1,128)S(1)}, s32[1,27]{1,0:T(1,128)S(1)}, u32[]{:S(2)}, u32[]{:S(2)}) collective-permute-start(s32[1,27]{1,0:T(1,128)S(1)} %copy-done.4), channel_id=1, source_target_pairs={{0,1},{1,0},{2,3},{3,2},{4,5},{5,4},{6,7},{7,6},{8,9},{9,8},{10,11... | collective-permute-start | bytes 332 | tf_op jit(solution)/shard_map/ppermute | solution.py:434
  4.8 0.0 collective-permute-done.1.other_ref
  4.8 0.0 copy-done.1
  4.8 0.1 collective-permute-start.6
  4.9 0.0 copy-done
  4.9 0.5 %shard_map.56.refs_4_.w = bf16[3,1728,192]{2,1,0:T(8,128)(2,1)S(1)} custom-call(bf16[27,48,384]{2,1,0:T(8,128)(2,1)S(1)} %bitcast.7, bf16[27,48,384]{2,1,0:T(8,128)(2,1)S(1)} %collective-permute-done.1.other_ref), custom_call_target="tpu_custom_call" | custom-call | tf_op jit(solution)/shard_map/pallas_call | solution.py:399
  5.4 0.3 %collective-permute-done.2.refs_0_ = s32[1,27]{1,0:T(1,128)S(1)} collective-permute-done((s32[1,27]{1,0:T(1,128)S(1)}, s32[1,27]{1,0:T(1,128)S(1)}, u32[]{:S(2)}, u32[]{:S(2)}) %collective-permute-start.2) | collective-permute-done | bytes 140 | tf_op jit(solution)/shard_map/ppermute | solution.py:434
  5.7 0.0 collective-permute-done.3.refs_2_
  5.7 0.0 collective-permute-done.4.refs_3_
  5.7 1.8 %shard_map.57 = (f32[2,512,128]{2,1,0:T(8,128)S(1)}, f32[2,1440,128]{2,1,0:T(8,128)S(1)}, f32[216,128]{1,0:T(8,128)S(1)}) custom-call(s32[1,27]{1,0:T(1,128)S(1)} %collective-permute-done.2.refs_0_, bf16[480,128]{1,0:T(8,128)(2,1)S(1)} %get-tuple-element.18.refs_1_, bf16[256,192]{1,0:T(8,128)(2,1)S(1)} %collective-permute-done.3.refs_2_, ...), custom_call_target="tpu_custom_call" | custom-call | tf_op jit(solution)/shard_map/pallas_call | solution.py:399
  7.5 0.0 collective-permute-done.far
  7.5 1.0 %shard_map.58 = (bf16[480,128]{1,0:T(8,128)(2,1)S(1)}, bf16[256,192]{1,0:T(8,128)(2,1)S(1)}, bf16[256,192]{1,0:T(8,128)(2,1)S(1)}, f32[2,512,128]{2,1,0:T(8,128)S(1)}) custom-call(bf16[480,128]{1,0:T(8,128)(2,1)S(1)} %collective-permute-done.far, bf16[3,1728,192]{2,1,0:T(8,128)(2,1)S(1)} %shard_map.56.refs_4_.w, ...), custom_call_target="tpu_custom_call", output_to_operand_aliasing={{3}: (2, {})} | custom-call | flops 17999998976 | tf_op jit(solution)/shard_map/pallas_call | solution.py:399
  8.4 3.4 %collective-permute-start.5 = (bf16[480,128]{1,0:T(8,128)(2,1)S(1)}, bf16[480,128]{1,0:T(8,128)(2,1)S(1)}, u32[]{:S(2)}, u32[]{:S(2)}) collective-permute-start(bf16[480,128]{1,0:T(8,128)(2,1)S(1)} %get-tuple-element.24.refs_1_), channel_id=1, source_target_pairs={{1,0},{3,1},{0,2},{5,3},{2,4},{7,5},{4,6},{9,7},{6,8},{11,9},{8,10... | collective-permute-start | bytes 368648 | tf_op jit(solution)/shard_map/ppermute | solution.py:478
  11.8 0.0 collective-permute-start.7
  11.8 0.5 %collective-permute-start.8 = (bf16[256,192]{1,0:T(8,128)(2,1)S(1)}, bf16[256,192]{1,0:T(8,128)(2,1)S(1)}, u32[]{:S(2)}, u32[]{:S(2)}) collective-permute-start(bf16[256,192]{1,0:T(8,128)(2,1)S(1)} %get-tuple-element.26), channel_id=1, source_target_pairs={{0,1},{1,0},{2,3},{3,2},{4,5},{5,4},{6,7},{7,6},{8,9},{9,8},{10,11... | collective-permute-start | bytes 294920 | tf_op jit(solution)/shard_map/ppermute | solution.py:477
  13.0 0.0 collective-permute-done.6.other_ref
  13.0 0.5 %shard_map.59.refs_4_.w = bf16[3,1728,192]{2,1,0:T(8,128)(2,1)S(1)} custom-call(bf16[27,48,384]{2,1,0:T(8,128)(2,1)S(1)} %bitcast.9, bf16[27,48,384]{2,1,0:T(8,128)(2,1)S(1)} %collective-permute-done.6.other_ref), custom_call_target="tpu_custom_call" | custom-call | tf_op jit(solution)/shard_map/pallas_call | solution.py:399
  13.4 0.0 copy-start.3
  13.5 0.0 collective-permute-done.7.refs_2_
  13.5 0.0 collective-permute-done.8.refs_3_
  13.5 1.8 %shard_map.60 = (f32[2,512,128]{2,1,0:T(8,128)S(1)}, f32[2,1440,128]{2,1,0:T(8,128)S(1)}, f32[216,128]{1,0:T(8,128)S(1)}) custom-call(s32[1,27]{1,0:T(1,128)S(1)} %copy-done.4, bf16[480,128]{1,0:T(8,128)(2,1)S(1)} %get-tuple-element.24.refs_1_, bf16[256,192]{1,0:T(8,128)(2,1)S(1)} %collective-permute-done.7.refs_2_, ...), custom_call_target="tpu_custom_call" | custom-call | tf_op jit(solution)/shard_map/pallas_call | solution.py:399
  15.3 0.0 collective-permute-done.5.far
  15.3 0.0 copy-done.3
  15.3 1.7 %shard_map.61 = (f32[512,192]{1,0:T(8,128)}, f32[2,512,128]{2,1,0:T(8,128)S(1)}) custom-call(s32[1,1]{1,0:T(1,128)} %bitcast.5.occupancy, bf16[480,128]{1,0:T(8,128)(2,1)S(1)} %collective-permute-done.5.far, bf16[3,1728,192]{2,1,0:T(8,128)(2,1)S(1)} %shard_map.59.refs_4_.w, bf16[512,192]{1,0:T(8,128)(2,1)S(1)} %bitcast.11, ...), custom_call_target="tpu_custom_call", output_to_operand_aliasing={{1}: (4, {})} | custom-call | tf_op jit(solution)/shard_map/pallas_call | solution.py:399
Async XLA Ops:
  0.0 4.8 %collective-permute-start.1 = (bf16[27,48,384]{2,1,0:T(8,128)(2,1)}, bf16[27,48,384]{2,1,0:T(8,128)(2,1)S(1)}, u32[]{:S(2)}, u32[]{:S(2)}) collective-permute-start(bf16[27,48,384]{2,1,0:T(8,128)(2,1)} %bitcast.6), channel_id=1, source_target_pairs={{0,1},{1,0},{2,3},{3,2},{4,5},{5,4},{6,7},{7,6},{8,9},{9,8},{10,11... | collective-permute-start | bytes 2985992 | tf_op jit(solution)/shard_map/ppermute | solution.py:440
  0.5 0.9 %copy-start.2 = (bf16[1,8,8,8,192]{4,3,2,1,0:T(8,128)(2,1)S(1)}, bf16[1,8,8,8,192]{4,3,2,1,0:T(8,128)(2,1)}, u32[]{:S(2)}) copy-start(bf16[1,8,8,8,192]{4,3,2,1,0:T(8,128)(2,1)} %param.5) | copy-start | bytes 589828
  1.4 2.9 %copy-start.4 = (s32[1,27]{1,0:T(1,128)S(1)}, s32[1,27]{1,0:T(1,128)}, u32[]{:S(2)}) copy-start(s32[1,27]{1,0:T(1,128)} %refs_0_.1) | copy-start | bytes 328
  1.4 3.4 %copy-start.1 = (bf16[3,3,3,48,384]{4,3,2,1,0:T(8,128)(2,1)S(1)}, bf16[3,3,3,48,384]{4,3,2,1,0:T(8,128)(2,1)}, u32[]{:S(2)}) copy-start(bf16[3,3,3,48,384]{4,3,2,1,0:T(8,128)(2,1)} %param.9) | copy-start | bytes 2985988
  1.4 3.5 %copy-start = (bf16[3,3,3,48,384]{4,3,2,1,0:T(8,128)(2,1)S(1)}, bf16[3,3,3,48,384]{4,3,2,1,0:T(8,128)(2,1)}, u32[]{:S(2)}) copy-start(bf16[3,3,3,48,384]{4,3,2,1,0:T(8,128)(2,1)} %param.8) | copy-start | bytes 2985988
  1.5 5.9 %collective-permute-start = (bf16[480,128]{1,0:T(8,128)(2,1)S(1)}, bf16[480,128]{1,0:T(8,128)(2,1)S(1)}, u32[]{:S(2)}, u32[]{:S(2)}) collective-permute-start(bf16[480,128]{1,0:T(8,128)(2,1)S(1)} %get-tuple-element.18.refs_1_), channel_id=1, source_target_pairs={{0,1},{1,3},{2,0},{3,5},{4,2},{5,7},{6,4},{7,9},{8,6},{9,11},{10,8... | collective-permute-start | bytes 368648 | tf_op jit(solution)/shard_map/ppermute | solution.py:436
  1.6 4.0 %collective-permute-start.3 = (bf16[256,192]{1,0:T(8,128)(2,1)S(1)}, bf16[256,192]{1,0:T(8,128)(2,1)S(1)}, u32[]{:S(2)}, u32[]{:S(2)}) collective-permute-start(bf16[256,192]{1,0:T(8,128)(2,1)S(1)} %get-tuple-element.19), channel_id=1, source_target_pairs={{0,1},{1,0},{2,3},{3,2},{4,5},{5,4},{6,7},{7,6},{8,9},{9,8},{10,11... | collective-permute-start | bytes 294920 | tf_op jit(solution)/shard_map/ppermute | solution.py:435
  4.3 1.4 %collective-permute-start.4 = (bf16[256,192]{1,0:T(8,128)(2,1)S(1)}, bf16[256,192]{1,0:T(8,128)(2,1)S(1)}, u32[]{:S(2)}, u32[]{:S(2)}) collective-permute-start(bf16[256,192]{1,0:T(8,128)(2,1)S(1)} %get-tuple-element.20), channel_id=1, source_target_pairs={{0,1},{1,0},{2,3},{3,2},{4,5},{5,4},{6,7},{7,6},{8,9},{9,8},{10,11... | collective-permute-start | bytes 294920 | tf_op jit(solution)/shard_map/ppermute | solution.py:435
  4.3 1.3 %collective-permute-start.2 = (s32[1,27]{1,0:T(1,128)S(1)}, s32[1,27]{1,0:T(1,128)S(1)}, u32[]{:S(2)}, u32[]{:S(2)}) collective-permute-start(s32[1,27]{1,0:T(1,128)S(1)} %copy-done.4), channel_id=1, source_target_pairs={{0,1},{1,0},{2,3},{3,2},{4,5},{5,4},{6,7},{7,6},{8,9},{9,8},{10,11... | collective-permute-start | bytes 332 | tf_op jit(solution)/shard_map/ppermute | solution.py:434
  4.8 8.1 %collective-permute-start.6 = (bf16[27,48,384]{2,1,0:T(8,128)(2,1)S(1)}, bf16[27,48,384]{2,1,0:T(8,128)(2,1)S(1)}, u32[]{:S(2)}, u32[]{:S(2)}) collective-permute-start(bf16[27,48,384]{2,1,0:T(8,128)(2,1)S(1)} %bitcast.8), channel_id=1, source_target_pairs={{0,1},{1,0},{2,3},{3,2},{4,5},{5,4},{6,7},{7,6},{8,9},{9,8},{10,11... | collective-permute-start | bytes 2985992 | tf_op jit(solution)/shard_map/ppermute | solution.py:440
  8.4 6.8 %collective-permute-start.5 = (bf16[480,128]{1,0:T(8,128)(2,1)S(1)}, bf16[480,128]{1,0:T(8,128)(2,1)S(1)}, u32[]{:S(2)}, u32[]{:S(2)}) collective-permute-start(bf16[480,128]{1,0:T(8,128)(2,1)S(1)} %get-tuple-element.24.refs_1_), channel_id=1, source_target_pairs={{1,0},{3,1},{0,2},{5,3},{2,4},{7,5},{4,6},{9,7},{6,8},{11,9},{8,10... | collective-permute-start | bytes 368648 | tf_op jit(solution)/shard_map/ppermute | solution.py:478
  11.8 1.7 %collective-permute-start.7 = (bf16[256,192]{1,0:T(8,128)(2,1)S(1)}, bf16[256,192]{1,0:T(8,128)(2,1)S(1)}, u32[]{:S(2)}, u32[]{:S(2)}) collective-permute-start(bf16[256,192]{1,0:T(8,128)(2,1)S(1)} %get-tuple-element.25), channel_id=1, source_target_pairs={{0,1},{1,0},{2,3},{3,2},{4,5},{5,4},{6,7},{7,6},{8,9},{9,8},{10,11... | collective-permute-start | bytes 294920 | tf_op jit(solution)/shard_map/ppermute | solution.py:477
  11.8 1.7 %collective-permute-start.8 = (bf16[256,192]{1,0:T(8,128)(2,1)S(1)}, bf16[256,192]{1,0:T(8,128)(2,1)S(1)}, u32[]{:S(2)}, u32[]{:S(2)}) collective-permute-start(bf16[256,192]{1,0:T(8,128)(2,1)S(1)} %get-tuple-element.26), channel_id=1, source_target_pairs={{0,1},{1,0},{2,3},{3,2},{4,5},{5,4},{6,7},{7,6},{8,9},{9,8},{10,11... | collective-permute-start | bytes 294920 | tf_op jit(solution)/shard_map/ppermute | solution.py:477
  13.4 1.8 %copy-start.3 = (bf16[1,8,8,8,192]{4,3,2,1,0:T(8,128)(2,1)S(1)}, bf16[1,8,8,8,192]{4,3,2,1,0:T(8,128)(2,1)}, u32[]{:S(2)}) copy-start(bf16[1,8,8,8,192]{4,3,2,1,0:T(8,128)(2,1)} %param.5) | copy-start | bytes 589828

commit v6 on v5

--- a/solution.py
+++ b/solution.py
@@ -8,6 +8,8 @@
 from jax.sharding import PartitionSpec as P
 
 PARTS = 2
+MARK_COST = 65 * 10**7
+NEXT_COST = 30 * 10**7
 PACK_COST = 4 * 10**9
 FIRST_COST = 18 * 10**9
 AXES = ("space", "wt")
@@ -113,7 +115,11 @@
             ]
 
 
-def pack_kernel(x_ref, out_ref, *refs, side):
+def mark_kernel(out_ref):
+    out_ref[...] = jnp.zeros(out_ref.shape, out_ref.dtype)
+
+
+def pack_kernel(x_ref, mark, after, out_ref, *refs, side):
     *pieces_out, wide = refs
     fill(wide, 0, x_ref[...].astype(F32))
     pack_surface(wide, out_ref, side, x_ref.shape[1])
@@ -171,27 +177,44 @@
     )
 
 
-def inside_kernel(*refs, side, block_of):
-    table_ref, beside, *centers, w, total, near, masks = refs[:-5]
-    wide, faces, lhs, table, semaphore = refs[-5:]
-    copy = pltpu.make_async_copy(table_ref, table, semaphore)
-    copy.start()
+def turned_chip(chips):
+    chip = lax.axis_index("space")
+    return ((chip == 0) | (chip == chips - 1)).astype(jnp.int32)
+
+
+def inside_kernel(*refs, side, chips, counts, opening):
+    refs = list(refs)
+    table_refs, *sources = [[refs.pop(0) for _ in range(n)] for n in counts]
+    w, total, near, masks, wide, faces, lhs, tables, semaphores = refs
+    copies = [
+        pltpu.make_async_copy(ref, tables.at[n], semaphores.at[n])
+        for n, ref in enumerate(table_refs)
+    ]
+    for copy in copies:
+        copy.start()
     width = w.shape[2]
     plane = side * side
-    for n, part in enumerate(centers):
-        fill(wide, n * part.shape[0], part[...].astype(F32))
+    turned = turned_chip(chips)
+    home = 2 * lax.axis_index("space") + lax.axis_index("wt")
+    other = home + 1 - 2 * lax.axis_index("wt")
+    away = jnp.where(turned == 1, other, home)
+    ids = (home, other) if opening else (away, home + other - away)
+    for slot, parts in enumerate(sources):
+        for n, part in enumerate(parts):
+            fill(wide.at[slot], n * part.shape[0], part[...].astype(F32))
     mask = lax.broadcasted_iota(jnp.int32, (side, side, LANES), 1)
     nothing = jnp.zeros((side, side, LANES), F32)
     edge = jnp.zeros((1, side, LANES), F32)
     for p, lane, lanes in pieces(width):
         folds = LANES // lanes
         for x in range(side):
-            middle = wide[p, pl.ds(x * plane, plane), :].reshape(side, side, LANES)
+            middle = wide[turned, p, pl.ds(x * plane, plane), :]
+            middle = middle.reshape(side, side, LANES)
             if folds > 1:
                 position = lax.broadcasted_iota(jnp.int32, middle.shape, 2)
                 for n in range(1, folds):
-                    turned = pltpu.roll(middle, n * lanes, axis=2)
-                    middle = jnp.where(position >= n * lanes, turned, middle)
+                    moved = pltpu.roll(middle, n * lanes, axis=2)
+                    middle = jnp.where(position >= n * lanes, moved, middle)
             moved = shifts(middle, nothing, nothing, mask)
             taps = []
             for j in range(3):
@@ -227,10 +250,13 @@
             else:
                 total[p, place, 0:lanes] += part
     fill(faces, 0, jnp.zeros((6 * plane, width), F32))
-    spread_surface(beside, faces, 1, side, width)
-    cut_surface(wide, faces, 2, side)
-    copy.wait()
-    choose_near(table, block_of(), faces, near, masks, side)
+    for slot in range(2):
+        cut_surface(wide.at[slot], faces, slot + 1, side)
+    for copy in copies:
+        copy.wait()
+    row = turned if opening else 0
+    entries = [tables[row, 0, t] for t in range(27)]
+    choose_near(entries, ids, faces, near, masks, side)
 
 
 def borders(side):
@@ -260,14 +286,14 @@
     return 9 * (a + 1) + 3 * (b + 1) + c + 1
 
 
-def choose_near(table, block, faces, near, masks, side):
+def choose_near(entries, ids, faces, near, masks, side):
     plane = side * side
-    pair = block + 1 - 2 * lax.rem(block, 2)
 
     def slot(n):
-        return jnp.where(n < 0, 0, jnp.where(n == block, 2, jnp.where(n == pair, 1, 3)))
-
-    slots = [slot(table[0, t]) for t in range(27)]
+        here = jnp.where(n == ids[0], 1, jnp.where(n == ids[1], 2, 3))
+        return jnp.where(n < 0, 0, here)
+
+    slots = [slot(n) for n in entries]
     for t, value in enumerate(slots):
         flag = (value > 0 if t == 13 else value == 3).astype(F32)
         masks[pl.ds(8 * t, 8), :] = jnp.full((8, LANES), flag, F32)
@@ -386,12 +412,19 @@
         out[:, lane : lane + lanes] = jnp.maximum(value, 0.0) * active
 
 
-def first_block():
-    return 2 * lax.axis_index("space") + 1 - lax.axis_index("wt")
-
-
-def second_block():
-    return 2 * lax.axis_index("space") + lax.axis_index("wt")
+def chip_exchanges(chips):
+    def end(chip):
+        return int(chip in (0, chips - 1))
+
+    last = 2 * chips - 1
+    first, second = [(0, 1), (last, last - 1)], [(1, 0), (last - 1, last)]
+    for c in range(chips - 1):
+        up, down = 2 * c, 2 * (c + 1)
+        first.append((up + 1, down + end(c + 1)))
+        first.append((down, up + 1 - end(c)))
+        second.append((up + 1 - end(c), down))
+        second.append((down + end(c + 1), up + 1))
+    return first, second
 
 
 def call(kernel, operands, outs, scratch=(), anywhere=0, cost=0, aliases={}):
@@ -415,50 +448,55 @@
     rows, plane = side**3, side * side
     total = lax.axis_size(AXES)
     halves = [(i, i ^ 1) for i in range(total)]
-    cycle = [(i, i - 2) if i % 2 == 0 else (i, i + 2) for i in range(total)]
-    cycle[0], cycle[-1] = (0, 1), (total - 1, total - 2)
-    back = [(j, i) for i, j in cycle]
+    chips = total // 2
+    first, second = chip_exchanges(chips)
     face = ((folded_rows(side, width), LANES), BF16)
     piece = ((rows // PARTS, width), BF16)
     wide = ((rows, width), F32)
     count = len(pieces(width))
 
     own = features.reshape(rows, width)
+    mark = call(mark_kernel, (), [((8, LANES), F32)], cost=MARK_COST)
+    mark, one_late = lax.optimization_barrier((mark, kernel_one))
+    after = call(mark_kernel, (), [((8, LANES), F32)], cost=NEXT_COST)
     own_face, *own_parts = call(
         functools.partial(pack_kernel, side=side),
-        (own,),
+        (own, mark, after),
         [face] + [piece] * PARTS,
         [VMEM((count, rows, LANES), F32)],
         cost=PACK_COST,
     )
     table_other = lax.ppermute(neighbours, AXES, halves)
     other = [lax.ppermute(part, AXES, halves) for part in own_parts]
-    far = lax.ppermute(own_face, AXES, cycle)
-
-    def weights(kernel):
+    far = lax.ppermute(own_face, AXES, first)
+
+    def weights(kernel, late):
         flat = kernel.reshape((27,) + kernel.shape[3:])
-        swapped = lax.ppermute(flat, AXES, halves)
+        swapped = lax.ppermute(late.reshape(flat.shape), AXES, halves)
         return call(weights_kernel, (flat, swapped), [((3, 9 * width, width), BF16)])
 
-    w_one, w_two = weights(kernel_one), weights(kernel_two)
+    w_one, w_two = weights(kernel_one, one_late), weights(kernel_two, kernel_two)
 
     sums = ((count, rows, LANES), F32)
     near = ((count, 6 * 3 * (side + 2) * side, LANES), F32)
     masks = ((27 * 8, LANES), F32)
 
-    def inside(block_of, table, beside, center, w):
+    def inside(layer, tables, here, there, w):
+        counts = (len(tables), len(here), len(there))
         return call(
-            functools.partial(inside_kernel, side=side, block_of=block_of),
-            (table, beside, *center, w),
+            functools.partial(
+                inside_kernel, side=side, chips=chips, counts=counts, opening=layer == 0
+            ),
+            (*tables, *here, *there, w),
             [sums, near, masks],
             [
-                VMEM((count, rows, LANES), F32),
+                VMEM((2, count, rows, LANES), F32),
                 VMEM((count, 3 * 6 * plane, LANES), F32),
                 VMEM((rows, 9 * width), BF16),
-                SMEM(table.shape, jnp.int32),
-                pltpu.SemaphoreType.DMA,
+                SMEM((len(tables),) + neighbours.shape, jnp.int32),
+                pltpu.SemaphoreType.DMA((len(tables),)),
             ],
-            anywhere=1,
+            anywhere=len(tables),
         )
 
     planes = [
@@ -468,14 +506,14 @@
     ]
     hidden_face, *hidden, _ = call(
         functools.partial(first_kernel, side=side),
-        (far, w_one, *inside(first_block, table_other, own_face, other, w_one)),
+        (far, w_one, *inside(0, (neighbours, table_other), own_parts, other, w_one)),
         [face] + [piece] * PARTS + [sums],
         planes,
         aliases={2: 1 + PARTS},
         cost=FIRST_COST,
     )
-    hidden_own = [lax.ppermute(part, AXES, halves) for part in hidden]
-    hidden_far = lax.ppermute(hidden_face, AXES, back)
+    hidden_other = [lax.ppermute(part, AXES, halves) for part in hidden]
+    hidden_far = lax.ppermute(hidden_face, AXES, second)
     out, _ = call(
         functools.partial(second_kernel, side=side),
         (
@@ -483,7 +521,7 @@
             hidden_far,
             w_two,
             own,
-            *inside(second_block, neighbours, hidden_face, hidden_own, w_two),
+            *inside(1, (neighbours,), hidden, hidden_other, w_two),
         ),
         [wide, sums],
         planes,

time: 17.1 us -> 16.4 us (0.959)
  the two profiles are of different devices: /device:TPU:0 before, /device:TPU:8 now
where the time goes in v6:
time: 16.4 us; the launch traced here: 16.2 us
  Pallas kernels  7.57 us (46%)
  starting transfers between devices  5.06 us (31%)
  waiting for transfers between devices  1.91 us (12%)
  local copies, waits for them, and re-layouts  0.94 us (6%)
  between operations  0.76 us (5%)
    pallas_call x9, Pallas kernels, call(): pl.pallas_call(kernel, out_shape=outs, in_specs=[pl.BlockSpec(memory_spac...  7.57 us
    ppermute x1, starting transfers between devices, body(): far = lax.ppermute(own_face, AXES, first)  1.82 us
    ppermute x1, starting transfers between devices, body(): hidden_far = lax.ppermute(hidden_face, AXES, second)  1.71 us
    unnamed x8, local copies, waits for them, and re-layouts  0.94 us
    ppermute x1, waiting for transfers between devices, body(): hidden_far = lax.ppermute(hidden_face, AXES, second)  0.93 us
    ppermute x1, waiting for transfers between devices, body(): far = lax.ppermute(own_face, AXES, first)  0.83 us
    ppermute x2, starting transfers between devices, body(): other = [lax.ppermute(part, AXES, halves) for part in own_parts]  0.51 us
    ppermute x2, starting transfers between devices, body(): hidden_other = [lax.ppermute(part, AXES, halves) for part in hidden]  0.51 us
  transfers between devices with their start and end apart: 9, of which 3 were waited for; matrix products, arithmetic and copies ran while one was open for 0% of the time, Pallas kernels for 36%

profile of v6, /device:TPU:8, one launch (start us, length us, event | category | flops | bytes accessed | tf_op | source)
XLA Modules:
  0.0 16.2 jit_solution(4411785432245385630)
XLA Ops:
  0.0 0.0 copy-start.2
  0.0 0.0 collective-permute-start.1
  0.0 0.9 %copy-done.2 = bf16[1,8,8,8,192]{4,3,2,1,0:T(8,128)(2,1)S(1)} copy-done((bf16[1,8,8,8,192]{4,3,2,1,0:T(8,128)(2,1)S(1)}, bf16[1,8,8,8,192]{4,3,2,1,0:T(8,128)(2,1)}, u32[]{:S(2)}) %copy-start.2) | copy-done | bytes 196632
  1.0 0.0 copy-start.3
  1.0 0.0 copy-start.1
  1.0 0.0 copy-start
  1.0 0.1 shard_map.57
  1.1 1.8 %collective-permute-start = (bf16[480,128]{1,0:T(8,128)(2,1)S(1)}, bf16[480,128]{1,0:T(8,128)(2,1)S(1)}, u32[]{:S(2)}, u32[]{:S(2)}) collective-permute-start(bf16[480,128]{1,0:T(8,128)(2,1)S(1)} %get-tuple-element.21), channel_id=1, source_target_pairs={{0,1},{31,30},{1,2},{2,0},{3,4},{4,3},{5,6},{6,5},{7,8},{8,7},{9,1... | collective-permute-start | bytes 368648 | tf_op jit(solution)/shard_map/ppermute | solution.py:471
  2.9 0.0 collective-permute-start.3
  2.9 0.5 %collective-permute-start.4 = (bf16[256,192]{1,0:T(8,128)(2,1)S(1)}, bf16[256,192]{1,0:T(8,128)(2,1)S(1)}, u32[]{:S(2)}, u32[]{:S(2)}) collective-permute-start(bf16[256,192]{1,0:T(8,128)(2,1)S(1)} %get-tuple-element.24.refs_3_), channel_id=1, source_target_pairs={{0,1},{1,0},{2,3},{3,2},{4,5},{5,4},{6,7},{7,6},{8,9},{9,8},{10,11... | collective-permute-start | bytes 294920 | tf_op jit(solution)/shard_map/ppermute | solution.py:470
  3.4 0.0 copy-done.3
  3.4 0.0 collective-permute-start.2
  3.4 0.0 collective-permute-done.1.other_ref
  3.4 0.0 copy-done.1
  3.4 0.5 %collective-permute-start.6 = (bf16[27,48,384]{2,1,0:T(8,128)(2,1)S(1)}, bf16[27,48,384]{2,1,0:T(8,128)(2,1)S(1)}, u32[]{:S(2)}, u32[]{:S(2)}) collective-permute-start(bf16[27,48,384]{2,1,0:T(8,128)(2,1)S(1)} %bitcast.9), channel_id=1, source_target_pairs={{0,1},{1,0},{2,3},{3,2},{4,5},{5,4},{6,7},{7,6},{8,9},{9,8},{10,11... | collective-permute-start | bytes 2985992 | tf_op jit(solution)/shard_map/ppermute | solution.py:475
  3.9 0.0 copy-done
  3.9 0.5 %shard_map.58.refs_6_.w = bf16[3,1728,192]{2,1,0:T(8,128)(2,1)S(1)} custom-call(bf16[27,48,384]{2,1,0:T(8,128)(2,1)S(1)} %bitcast.8, bf16[27,48,384]{2,1,0:T(8,128)(2,1)S(1)} %collective-permute-done.1.other_ref), custom_call_target="tpu_custom_call" | custom-call | tf_op jit(solution)/shard_map/pallas_call | solution.py:432
  4.4 0.1 collective-permute-done.2.refs_1_
  4.5 0.0 collective-permute-done.3.refs_4_
  4.5 0.0 collective-permute-done.4.refs_5_
  4.5 2.0 %shard_map.59 = (f32[2,512,128]{2,1,0:T(8,128)S(1)}, f32[2,1440,128]{2,1,0:T(8,128)S(1)}, f32[216,128]{1,0:T(8,128)S(1)}) custom-call(s32[1,27]{1,0:T(1,128)S(1)} %copy-done.3, s32[1,27]{1,0:T(1,128)S(1)} %collective-permute-done.2.refs_1_, bf16[256,192]{1,0:T(8,128)(2,1)S(1)} %get-tuple-element.23.refs_2_, bf16[256,192]{1,0:T(8,128)(2,1)S(1)} %get-tuple-element.24.refs_3_, ...), custom_call_target="tpu_custom_call" | custom-call | tf_op jit(solution)/shard_map/pallas_call | solution.py:432
  6.5 0.8 %collective-permute-done.far = bf16[480,128]{1,0:T(8,128)(2,1)S(1)} collective-permute-done((bf16[480,128]{1,0:T(8,128)(2,1)S(1)}, bf16[480,128]{1,0:T(8,128)(2,1)S(1)}, u32[]{:S(2)}, u32[]{:S(2)}) %collective-permute-start) | collective-permute-done | bytes 122912 | tf_op jit(solution)/shard_map/ppermute | solution.py:471
  7.3 1.0 %shard_map.60 = (bf16[480,128]{1,0:T(8,128)(2,1)S(1)}, bf16[256,192]{1,0:T(8,128)(2,1)S(1)}, bf16[256,192]{1,0:T(8,128)(2,1)S(1)}, f32[2,512,128]{2,1,0:T(8,128)S(1)}) custom-call(bf16[480,128]{1,0:T(8,128)(2,1)S(1)} %collective-permute-done.far, bf16[3,1728,192]{2,1,0:T(8,128)(2,1)S(1)} %shard_map.58.refs_6_.w, ...), custom_call_target="tpu_custom_call", output_to_operand_aliasing={{3}: (2, {})} | custom-call | flops 17999998976 | tf_op jit(solution)/shard_map/pallas_call | solution.py:432
  8.3 1.7 %collective-permute-start.5 = (bf16[480,128]{1,0:T(8,128)(2,1)S(1)}, bf16[480,128]{1,0:T(8,128)(2,1)S(1)}, u32[]{:S(2)}, u32[]{:S(2)}) collective-permute-start(bf16[480,128]{1,0:T(8,128)(2,1)S(1)} %get-tuple-element.28), channel_id=1, source_target_pairs={{1,0},{30,31},{0,2},{2,1},{3,4},{4,3},{5,6},{6,5},{7,8},{8,7},{9,1... | collective-permute-start | bytes 368648 | tf_op jit(solution)/shard_map/ppermute | solution.py:516
  10.0 0.0 collective-permute-start.7
  10.0 0.5 %collective-permute-start.8 = (bf16[256,192]{1,0:T(8,128)(2,1)S(1)}, bf16[256,192]{1,0:T(8,128)(2,1)S(1)}, u32[]{:S(2)}, u32[]{:S(2)}) collective-permute-start(bf16[256,192]{1,0:T(8,128)(2,1)S(1)} %get-tuple-element.30.refs_2_), channel_id=1, source_target_pairs={{0,1},{1,0},{2,3},{3,2},{4,5},{5,4},{6,7},{7,6},{8,9},{9,8},{10,11... | collective-permute-start | bytes 294920 | tf_op jit(solution)/shard_map/ppermute | solution.py:515
  11.2 0.0 collective-permute-done.6.other_ref
  11.2 0.5 %shard_map.61.refs_5_.w = bf16[3,1728,192]{2,1,0:T(8,128)(2,1)S(1)} custom-call(bf16[27,48,384]{2,1,0:T(8,128)(2,1)S(1)} %bitcast.10, bf16[27,48,384]{2,1,0:T(8,128)(2,1)S(1)} %collective-permute-done.6.other_ref), custom_call_target="tpu_custom_call" | custom-call | tf_op jit(solution)/shard_map/pallas_call | solution.py:432
  11.7 0.0 collective-permute-done.7.refs_3_
  11.7 0.0 collective-permute-done.8.refs_4_
  11.7 1.9 %shard_map.62 = (f32[2,512,128]{2,1,0:T(8,128)S(1)}, f32[2,1440,128]{2,1,0:T(8,128)S(1)}, f32[216,128]{1,0:T(8,128)S(1)}) custom-call(s32[1,27]{1,0:T(1,128)S(1)} %copy-done.3, bf16[256,192]{1,0:T(8,128)(2,1)S(1)} %get-tuple-element.29.refs_1_, bf16[256,192]{1,0:T(8,128)(2,1)S(1)} %get-tuple-element.30.refs_2_, ...), custom_call_target="tpu_custom_call" | custom-call | tf_op jit(solution)/shard_map/pallas_call | solution.py:432
  13.6 0.9 %collective-permute-done.5.far = bf16[480,128]{1,0:T(8,128)(2,1)S(1)} collective-permute-done((bf16[480,128]{1,0:T(8,128)(2,1)S(1)}, bf16[480,128]{1,0:T(8,128)(2,1)S(1)}, u32[]{:S(2)}, u32[]{:S(2)}) %collective-permute-start.5) | collective-permute-done | bytes 122912 | tf_op jit(solution)/shard_map/ppermute | solution.py:516
  14.6 1.7 %shard_map.63 = (f32[512,192]{1,0:T(8,128)}, f32[2,512,128]{2,1,0:T(8,128)S(1)}) custom-call(s32[1,1]{1,0:T(1,128)} %bitcast.6.occupancy, bf16[480,128]{1,0:T(8,128)(2,1)S(1)} %collective-permute-done.5.far, bf16[3,1728,192]{2,1,0:T(8,128)(2,1)S(1)} %shard_map.61.refs_5_.w, bf16[512,192]{1,0:T(8,128)(2,1)S(1)} %bitcast.12, ...), custom_call_target="tpu_custom_call", output_to_operand_aliasing={{1}: (4, {})} | custom-call | tf_op jit(solution)/shard_map/pallas_call | solution.py:432
  (2 shorter events, 0.0 us)
Async XLA Ops:
  0.0 0.9 %copy-start.2 = (bf16[1,8,8,8,192]{4,3,2,1,0:T(8,128)(2,1)S(1)}, bf16[1,8,8,8,192]{4,3,2,1,0:T(8,128)(2,1)}, u32[]{:S(2)}) copy-start(bf16[1,8,8,8,192]{4,3,2,1,0:T(8,128)(2,1)} %param.5) | copy-start | bytes 589828
  0.0 3.4 %collective-permute-start.1 = (bf16[27,48,384]{2,1,0:T(8,128)(2,1)}, bf16[27,48,384]{2,1,0:T(8,128)(2,1)S(1)}, u32[]{:S(2)}, u32[]{:S(2)}) collective-permute-start(bf16[27,48,384]{2,1,0:T(8,128)(2,1)} %bitcast.7), channel_id=1, source_target_pairs={{0,1},{1,0},{2,3},{3,2},{4,5},{5,4},{6,7},{7,6},{8,9},{9,8},{10,11... | collective-permute-start | bytes 2985992 | tf_op jit(solution)/shard_map/ppermute | solution.py:475
  1.0 2.5 %copy-start.3 = (s32[1,27]{1,0:T(1,128)S(1)}, s32[1,27]{1,0:T(1,128)}, u32[]{:S(2)}) copy-start(s32[1,27]{1,0:T(1,128)} %refs_0_.3) | copy-start | bytes 328
  1.0 2.5 %copy-start.1 = (bf16[3,3,3,48,384]{4,3,2,1,0:T(8,128)(2,1)S(1)}, bf16[3,3,3,48,384]{4,3,2,1,0:T(8,128)(2,1)}, u32[]{:S(2)}) copy-start(bf16[3,3,3,48,384]{4,3,2,1,0:T(8,128)(2,1)} %param.9) | copy-start | bytes 2985988
  1.0 3.0 %copy-start = (bf16[3,3,3,48,384]{4,3,2,1,0:T(8,128)(2,1)S(1)}, bf16[3,3,3,48,384]{4,3,2,1,0:T(8,128)(2,1)}, u32[]{:S(2)}) copy-start(bf16[3,3,3,48,384]{4,3,2,1,0:T(8,128)(2,1)} %param.8) | copy-start | bytes 2985988
  1.1 6.3 %collective-permute-start = (bf16[480,128]{1,0:T(8,128)(2,1)S(1)}, bf16[480,128]{1,0:T(8,128)(2,1)S(1)}, u32[]{:S(2)}, u32[]{:S(2)}) collective-permute-start(bf16[480,128]{1,0:T(8,128)(2,1)S(1)} %get-tuple-element.21), channel_id=1, source_target_pairs={{0,1},{31,30},{1,2},{2,0},{3,4},{4,3},{5,6},{6,5},{7,8},{8,7},{9,1... | collective-permute-start | bytes 368648 | tf_op jit(solution)/shard_map/ppermute | solution.py:471
  2.9 1.6 %collective-permute-start.3 = (bf16[256,192]{1,0:T(8,128)(2,1)S(1)}, bf16[256,192]{1,0:T(8,128)(2,1)S(1)}, u32[]{:S(2)}, u32[]{:S(2)}) collective-permute-start(bf16[256,192]{1,0:T(8,128)(2,1)S(1)} %get-tuple-element.23.refs_2_), channel_id=1, source_target_pairs={{0,1},{1,0},{2,3},{3,2},{4,5},{5,4},{6,7},{7,6},{8,9},{9,8},{10,11... | collective-permute-start | bytes 294920 | tf_op jit(solution)/shard_map/ppermute | solution.py:470
  2.9 1.6 %collective-permute-start.4 = (bf16[256,192]{1,0:T(8,128)(2,1)S(1)}, bf16[256,192]{1,0:T(8,128)(2,1)S(1)}, u32[]{:S(2)}, u32[]{:S(2)}) collective-permute-start(bf16[256,192]{1,0:T(8,128)(2,1)S(1)} %get-tuple-element.24.refs_3_), channel_id=1, source_target_pairs={{0,1},{1,0},{2,3},{3,2},{4,5},{5,4},{6,7},{7,6},{8,9},{9,8},{10,11... | collective-permute-start | bytes 294920 | tf_op jit(solution)/shard_map/ppermute | solution.py:470
  3.4 1.1 %collective-permute-start.2 = (s32[1,27]{1,0:T(1,128)S(1)}, s32[1,27]{1,0:T(1,128)S(1)}, u32[]{:S(2)}, u32[]{:S(2)}) collective-permute-start(s32[1,27]{1,0:T(1,128)S(1)} %copy-done.3), channel_id=1, source_target_pairs={{0,1},{1,0},{2,3},{3,2},{4,5},{5,4},{6,7},{7,6},{8,9},{9,8},{10,11... | collective-permute-start | bytes 332 | tf_op jit(solution)/shard_map/ppermute | solution.py:469
  3.4 7.8 %collective-permute-start.6 = (bf16[27,48,384]{2,1,0:T(8,128)(2,1)S(1)}, bf16[27,48,384]{2,1,0:T(8,128)(2,1)S(1)}, u32[]{:S(2)}, u32[]{:S(2)}) collective-permute-start(bf16[27,48,384]{2,1,0:T(8,128)(2,1)S(1)} %bitcast.9), channel_id=1, source_target_pairs={{0,1},{1,0},{2,3},{3,2},{4,5},{5,4},{6,7},{7,6},{8,9},{9,8},{10,11... | collective-permute-start | bytes 2985992 | tf_op jit(solution)/shard_map/ppermute | solution.py:475
  8.3 6.3 %collective-permute-start.5 = (bf16[480,128]{1,0:T(8,128)(2,1)S(1)}, bf16[480,128]{1,0:T(8,128)(2,1)S(1)}, u32[]{:S(2)}, u32[]{:S(2)}) collective-permute-start(bf16[480,128]{1,0:T(8,128)(2,1)S(1)} %get-tuple-element.28), channel_id=1, source_target_pairs={{1,0},{30,31},{0,2},{2,1},{3,4},{4,3},{5,6},{6,5},{7,8},{8,7},{9,1... | collective-permute-start | bytes 368648 | tf_op jit(solution)/shard_map/ppermute | solution.py:516
  10.0 1.7 %collective-permute-start.7 = (bf16[256,192]{1,0:T(8,128)(2,1)S(1)}, bf16[256,192]{1,0:T(8,128)(2,1)S(1)}, u32[]{:S(2)}, u32[]{:S(2)}) collective-permute-start(bf16[256,192]{1,0:T(8,128)(2,1)S(1)} %get-tuple-element.29.refs_1_), channel_id=1, source_target_pairs={{0,1},{1,0},{2,3},{3,2},{4,5},{5,4},{6,7},{7,6},{8,9},{9,8},{10,11... | collective-permute-start | bytes 294920 | tf_op jit(solution)/shard_map/ppermute | solution.py:515
  10.0 1.7 %collective-permute-start.8 = (bf16[256,192]{1,0:T(8,128)(2,1)S(1)}, bf16[256,192]{1,0:T(8,128)(2,1)S(1)}, u32[]{:S(2)}, u32[]{:S(2)}) collective-permute-start(bf16[256,192]{1,0:T(8,128)(2,1)S(1)} %get-tuple-element.30.refs_2_), channel_id=1, source_target_pairs={{0,1},{1,0},{2,3},{3,2},{4,5},{5,4},{6,7},{7,6},{8,9},{9,8},{10,11... | collective-permute-start | bytes 294920 | tf_op jit(solution)/shard_map/ppermute | solution.py:515

commit v7 on v6

--- a/solution.py
+++ b/solution.py
@@ -33,18 +33,37 @@
 
 
 def surface_rows(side):
-    return 2 * side * side + 4 * (side - 2) * side
+    return side**3 - (side - 2) ** 3
+
+
+def folded_shape(side, lanes):
+    rows, folds = surface_rows(side), LANES // lanes
+    short = rows // folds // 16 * 16
+    return folds, short, rows - folds * short
 
 
 def folded_rows(side, width):
-    return -(-surface_rows(side) * width // LANES)
+    rows = 0
+    for p, lane, lanes in pieces(width):
+        folds, short, left = folded_shape(side, lanes)
+        rows += surface_rows(side) if folds == 1 else short + left
+    return -(-rows // 16) * 16
+
+
+def folded_start(side, width):
+    rows = surface_rows(side) * (width // LANES)
+    for p, lane, lanes in pieces(width):
+        if lanes < LANES:
+            rows += folded_shape(side, lanes)[2]
+    return -(-rows // 16) * 16
 
 
 def pack_surface(wide, out_ref, side, width, change=lambda value: value):
     plane = side * side
-    inner = (side - 2) * side
     last = side - 1
     rows = surface_rows(side)
+    start = folded_start(side, width)
+    whole = []
     for p, lane, lanes in pieces(width):
         ref = wide.at[p]
         parts = [ref[pl.ds(0, plane), :], ref[pl.ds(last * plane, plane), :]]
@@ -52,16 +71,26 @@
             for x in range(1, last):
                 parts.append(ref[pl.ds(x * plane + y * side, side), :])
         for z in (0, last):
-            parts.append(ref[pl.ds(plane + z, inner, stride=side), :])
+            for x in range(1, last):
+                at = x * plane + side + z
+                parts.append(ref[pl.ds(at, side - 2, stride=side), :])
         value = change(jnp.concatenate(parts, axis=0))
-        folds = LANES // lanes
-        count = rows // folds
+        folds, count, left = folded_shape(side, lanes)
+        if folds == 1:
+            whole.append(value)
+            continue
+        whole.append(value[folds * count :])
         result = value[:count]
         position = lax.broadcasted_iota(jnp.int32, (count, LANES), 1)
         for n in range(1, folds):
             part = pltpu.roll(value[n * count : (n + 1) * count], n * lanes, axis=1)
             result = jnp.where(position >= n * lanes, part, result)
-        out_ref[pl.ds(p * rows, count), :] = result.astype(BF16)
+        out_ref[pl.ds(start, count), :] = result.astype(BF16)
+    value = jnp.concatenate(whole, axis=0)
+    if value.shape[0] < start:
+        rest = jnp.zeros((start - value.shape[0], LANES), F32)
+        value = jnp.concatenate([value, rest], axis=0)
+    out_ref[pl.ds(0, start), :] = value.astype(BF16)
 
 
 def spread_surface(packed_ref, faces, slot, side, width):
@@ -70,20 +99,30 @@
     last = side - 1
     base = slot * 6 * plane
     rows = surface_rows(side)
+    start = folded_start(side, width)
+    whole = packed_ref[pl.ds(0, start), :].astype(F32)
     for p, lane, lanes in pieces(width):
         ref = faces.at[p]
-        folds = LANES // lanes
-        part = packed_ref[pl.ds(p * rows, rows // folds), :].astype(F32)
-        if folds > 1:
+        folds, count, left = folded_shape(side, lanes)
+        if folds == 1:
+            part = whole[p * rows : (p + 1) * rows]
+        else:
+            part = packed_ref[pl.ds(start, count), :].astype(F32)
             turned = [part] + [
                 pltpu.roll(part, LANES - n * lanes, axis=1) for n in range(1, folds)
             ]
+            turned.append(whole[p * rows : p * rows + left])
             part = jnp.concatenate(turned, axis=0)
         ref[pl.ds(base, 2 * plane), :] = part[: 2 * plane]
         row = 2 * plane
-        for f in range(2, 6):
+        for f in (2, 3):
             ref[pl.ds(base + f * plane + side, inner), :] = part[row : row + inner]
             row += inner
+        for f in (4, 5):
+            for x in range(1, last):
+                at = base + f * plane + x * side + 1
+                ref[pl.ds(at, side - 2), :] = part[row : row + side - 2]
+                row += side - 2
         for end, x in ((0, 0), (1, last)):
             for f, y in ((2, 0), (3, last)):
                 ref[pl.ds(base + f * plane + x * side, side), :] = ref[
@@ -92,6 +131,11 @@
             for f, z in ((4, 0), (5, last)):
                 ref[pl.ds(base + f * plane + x * side, side), :] = ref[
                     pl.ds(base + end * plane + z, side, stride=side), :
+                ]
+        for f, z in ((4, 0), (5, last)):
+            for g, y in ((2, 0), (3, last)):
+                ref[pl.ds(base + f * plane + y, side, stride=side), :] = ref[
+                    pl.ds(base + g * plane + z, side, stride=side), :
                 ]
 
 

time: 16.4 us -> 16.2 us (0.988)
  waiting for transfers between devices: 1.91 us -> 1.6 us
  Pallas kernels: 7.57 us -> 7.75 us
    ppermute x1, waiting for transfers between devices: 0.93 us -> 0.73 us  [body(): hidden_far = lax.ppermute(hidden_face, AXES, second)]
    pallas_call x9, Pallas kernels: 7.57 us -> 7.75 us  [call(): pl.pallas_call(kernel, out_shape=outs, in_specs=[pl.BlockSpec(memory_spac...]
  transfers between devices with their start and end apart: 9 -> 9, of which waited for: 3 -> 3; matrix products, arithmetic and copies ran while one was open for 0% -> 0% of each run, Pallas kernels for 36% -> 37%
where the time goes in v7:
time: 16.2 us; the launch traced here: 16.1 us
  Pallas kernels  7.75 us (48%)
  starting transfers between devices  5.05 us (31%)
  waiting for transfers between devices  1.6 us (10%)
  local copies, waits for them, and re-layouts  0.94 us (6%)
  between operations  0.75 us (5%)
    pallas_call x9, Pallas kernels, call(): pl.pallas_call(kernel, out_shape=outs, in_specs=[pl.BlockSpec(memory_spac...  7.75 us
    ppermute x1, starting transfers between devices, body(): far = lax.ppermute(own_face, AXES, first)  1.81 us
    ppermute x1, starting transfers between devices, body(): hidden_far = lax.ppermute(hidden_face, AXES, second)  1.71 us
    unnamed x8, local copies, waits for them, and re-layouts  0.94 us
    ppermute x1, waiting for transfers between devices, body(): hidden_far = lax.ppermute(hidden_face, AXES, second)  0.73 us
    ppermute x1, waiting for transfers between devices, body(): far = lax.ppermute(own_face, AXES, first)  0.73 us
    ppermute x2, starting transfers between devices, body(): hidden_other = [lax.ppermute(part, AXES, halves) for part in hidden]  0.51 us
    ppermute x2, starting transfers between devices, body(): other = [lax.ppermute(part, AXES, halves) for part in own_parts]  0.51 us
  transfers between devices with their start and end apart: 9, of which 3 were waited for; matrix products, arithmetic and copies ran while one was open for 0% of the time, Pallas kernels for 37%

profile of v7, /device:TPU:8, one launch (start us, length us, event | category | flops | bytes accessed | tf_op | source)
XLA Modules:
  0.0 16.1 jit_solution(14710750650408683358)
XLA Ops:
  0.0 0.0 copy-start.2
  0.0 0.0 collective-permute-start.1
  0.0 0.9 %copy-done.2 = bf16[1,8,8,8,192]{4,3,2,1,0:T(8,128)(2,1)S(1)} copy-done((bf16[1,8,8,8,192]{4,3,2,1,0:T(8,128)(2,1)S(1)}, bf16[1,8,8,8,192]{4,3,2,1,0:T(8,128)(2,1)}, u32[]{:S(2)}) %copy-start.2) | copy-done | bytes 196632
  1.0 0.0 copy-start.3
  1.0 0.0 copy-start.1
  1.0 0.0 copy-start
  1.0 0.1 shard_map.57
  1.1 1.8 %collective-permute-start = (bf16[448,128]{1,0:T(8,128)(2,1)S(1)}, bf16[448,128]{1,0:T(8,128)(2,1)S(1)}, u32[]{:S(2)}, u32[]{:S(2)}) collective-permute-start(bf16[448,128]{1,0:T(8,128)(2,1)S(1)} %get-tuple-element.21), channel_id=1, source_target_pairs={{0,1},{31,30},{1,2},{2,0},{3,4},{4,3},{5,6},{6,5},{7,8},{8,7},{9,1... | collective-permute-start | bytes 344072 | tf_op jit(solution)/shard_map/ppermute | solution.py:515
  2.9 0.0 collective-permute-start.3
  2.9 0.5 %collective-permute-start.4 = (bf16[256,192]{1,0:T(8,128)(2,1)S(1)}, bf16[256,192]{1,0:T(8,128)(2,1)S(1)}, u32[]{:S(2)}, u32[]{:S(2)}) collective-permute-start(bf16[256,192]{1,0:T(8,128)(2,1)S(1)} %get-tuple-element.24.refs_3_), channel_id=1, source_target_pairs={{0,1},{1,0},{2,3},{3,2},{4,5},{5,4},{6,7},{7,6},{8,9},{9,8},{10,11... | collective-permute-start | bytes 294920 | tf_op jit(solution)/shard_map/ppermute | solution.py:514
  3.4 0.0 copy-done.3
  3.4 0.0 collective-permute-start.2
  3.4 0.0 collective-permute-done.1.other_ref
  3.4 0.0 copy-done.1
  3.4 0.5 %collective-permute-start.6 = (bf16[27,48,384]{2,1,0:T(8,128)(2,1)S(1)}, bf16[27,48,384]{2,1,0:T(8,128)(2,1)S(1)}, u32[]{:S(2)}, u32[]{:S(2)}) collective-permute-start(bf16[27,48,384]{2,1,0:T(8,128)(2,1)S(1)} %bitcast.9), channel_id=1, source_target_pairs={{0,1},{1,0},{2,3},{3,2},{4,5},{5,4},{6,7},{7,6},{8,9},{9,8},{10,11... | collective-permute-start | bytes 2985992 | tf_op jit(solution)/shard_map/ppermute | solution.py:519
  3.9 0.0 copy-done
  3.9 0.5 %shard_map.58.refs_6_.w = bf16[3,1728,192]{2,1,0:T(8,128)(2,1)S(1)} custom-call(bf16[27,48,384]{2,1,0:T(8,128)(2,1)S(1)} %bitcast.8, bf16[27,48,384]{2,1,0:T(8,128)(2,1)S(1)} %collective-permute-done.1.other_ref), custom_call_target="tpu_custom_call" | custom-call | tf_op jit(solution)/shard_map/pallas_call | solution.py:476
  4.4 0.1 collective-permute-done.2.refs_1_
  4.5 0.0 collective-permute-done.3.refs_4_
  4.5 0.0 collective-permute-done.4.refs_5_
  4.5 2.0 %shard_map.59 = (f32[2,512,128]{2,1,0:T(8,128)S(1)}, f32[2,1440,128]{2,1,0:T(8,128)S(1)}, f32[216,128]{1,0:T(8,128)S(1)}) custom-call(s32[1,27]{1,0:T(1,128)S(1)} %copy-done.3, s32[1,27]{1,0:T(1,128)S(1)} %collective-permute-done.2.refs_1_, bf16[256,192]{1,0:T(8,128)(2,1)S(1)} %get-tuple-element.23.refs_2_, bf16[256,192]{1,0:T(8,128)(2,1)S(1)} %get-tuple-element.24.refs_3_, ...), custom_call_target="tpu_custom_call" | custom-call | tf_op jit(solution)/shard_map/pallas_call | solution.py:476
  6.5 0.7 %collective-permute-done.far = bf16[448,128]{1,0:T(8,128)(2,1)S(1)} collective-permute-done((bf16[448,128]{1,0:T(8,128)(2,1)S(1)}, bf16[448,128]{1,0:T(8,128)(2,1)S(1)}, u32[]{:S(2)}, u32[]{:S(2)}) %collective-permute-start) | collective-permute-done | bytes 114720 | tf_op jit(solution)/shard_map/ppermute | solution.py:515
  7.3 1.0 %shard_map.60 = (bf16[448,128]{1,0:T(8,128)(2,1)S(1)}, bf16[256,192]{1,0:T(8,128)(2,1)S(1)}, bf16[256,192]{1,0:T(8,128)(2,1)S(1)}, f32[2,512,128]{2,1,0:T(8,128)S(1)}) custom-call(bf16[448,128]{1,0:T(8,128)(2,1)S(1)} %collective-permute-done.far, bf16[3,1728,192]{2,1,0:T(8,128)(2,1)S(1)} %shard_map.58.refs_6_.w, ...), custom_call_target="tpu_custom_call", output_to_operand_aliasing={{3}: (2, {})} | custom-call | flops 17999998976 | tf_op jit(solution)/shard_map/pallas_call | solution.py:476
  8.3 1.7 %collective-permute-start.5 = (bf16[448,128]{1,0:T(8,128)(2,1)S(1)}, bf16[448,128]{1,0:T(8,128)(2,1)S(1)}, u32[]{:S(2)}, u32[]{:S(2)}) collective-permute-start(bf16[448,128]{1,0:T(8,128)(2,1)S(1)} %get-tuple-element.28), channel_id=1, source_target_pairs={{1,0},{30,31},{0,2},{2,1},{3,4},{4,3},{5,6},{6,5},{7,8},{8,7},{9,1... | collective-permute-start | bytes 344072 | tf_op jit(solution)/shard_map/ppermute | solution.py:560
  10.0 0.0 collective-permute-start.7
  10.0 0.5 %collective-permute-start.8 = (bf16[256,192]{1,0:T(8,128)(2,1)S(1)}, bf16[256,192]{1,0:T(8,128)(2,1)S(1)}, u32[]{:S(2)}, u32[]{:S(2)}) collective-permute-start(bf16[256,192]{1,0:T(8,128)(2,1)S(1)} %get-tuple-element.30.refs_2_), channel_id=1, source_target_pairs={{0,1},{1,0},{2,3},{3,2},{4,5},{5,4},{6,7},{7,6},{8,9},{9,8},{10,11... | collective-permute-start | bytes 294920 | tf_op jit(solution)/shard_map/ppermute | solution.py:559
  11.2 0.0 collective-permute-done.6.other_ref
  11.2 0.5 %shard_map.61.refs_5_.w = bf16[3,1728,192]{2,1,0:T(8,128)(2,1)S(1)} custom-call(bf16[27,48,384]{2,1,0:T(8,128)(2,1)S(1)} %bitcast.10, bf16[27,48,384]{2,1,0:T(8,128)(2,1)S(1)} %collective-permute-done.6.other_ref), custom_call_target="tpu_custom_call" | custom-call | tf_op jit(solution)/shard_map/pallas_call | solution.py:476
  11.7 0.0 collective-permute-done.7.refs_3_
  11.7 0.0 collective-permute-done.8.refs_4_
  11.7 1.9 %shard_map.62 = (f32[2,512,128]{2,1,0:T(8,128)S(1)}, f32[2,1440,128]{2,1,0:T(8,128)S(1)}, f32[216,128]{1,0:T(8,128)S(1)}) custom-call(s32[1,27]{1,0:T(1,128)S(1)} %copy-done.3, bf16[256,192]{1,0:T(8,128)(2,1)S(1)} %get-tuple-element.29.refs_1_, bf16[256,192]{1,0:T(8,128)(2,1)S(1)} %get-tuple-element.30.refs_2_, ...), custom_call_target="tpu_custom_call" | custom-call | tf_op jit(solution)/shard_map/pallas_call | solution.py:476
  13.6 0.7 %collective-permute-done.5.far = bf16[448,128]{1,0:T(8,128)(2,1)S(1)} collective-permute-done((bf16[448,128]{1,0:T(8,128)(2,1)S(1)}, bf16[448,128]{1,0:T(8,128)(2,1)S(1)}, u32[]{:S(2)}, u32[]{:S(2)}) %collective-permute-start.5) | collective-permute-done | bytes 114720 | tf_op jit(solution)/shard_map/ppermute | solution.py:560
  14.4 1.7 %shard_map.63 = (f32[512,192]{1,0:T(8,128)}, f32[2,512,128]{2,1,0:T(8,128)S(1)}) custom-call(s32[1,1]{1,0:T(1,128)} %bitcast.6.occupancy, bf16[448,128]{1,0:T(8,128)(2,1)S(1)} %collective-permute-done.5.far, bf16[3,1728,192]{2,1,0:T(8,128)(2,1)S(1)} %shard_map.61.refs_5_.w, bf16[512,192]{1,0:T(8,128)(2,1)S(1)} %bitcast.12, ...), custom_call_target="tpu_custom_call", output_to_operand_aliasing={{1}: (4, {})} | custom-call | tf_op jit(solution)/shard_map/pallas_call | solution.py:476
  (2 shorter events, 0.0 us)
Async XLA Ops:
  0.0 0.9 %copy-start.2 = (bf16[1,8,8,8,192]{4,3,2,1,0:T(8,128)(2,1)S(1)}, bf16[1,8,8,8,192]{4,3,2,1,0:T(8,128)(2,1)}, u32[]{:S(2)}) copy-start(bf16[1,8,8,8,192]{4,3,2,1,0:T(8,128)(2,1)} %param.5) | copy-start | bytes 589828
  0.0 3.4 %collective-permute-start.1 = (bf16[27,48,384]{2,1,0:T(8,128)(2,1)}, bf16[27,48,384]{2,1,0:T(8,128)(2,1)S(1)}, u32[]{:S(2)}, u32[]{:S(2)}) collective-permute-start(bf16[27,48,384]{2,1,0:T(8,128)(2,1)} %bitcast.7), channel_id=1, source_target_pairs={{0,1},{1,0},{2,3},{3,2},{4,5},{5,4},{6,7},{7,6},{8,9},{9,8},{10,11... | collective-permute-start | bytes 2985992 | tf_op jit(solution)/shard_map/ppermute | solution.py:519
  1.0 2.5 %copy-start.3 = (s32[1,27]{1,0:T(1,128)S(1)}, s32[1,27]{1,0:T(1,128)}, u32[]{:S(2)}) copy-start(s32[1,27]{1,0:T(1,128)} %refs_0_.3) | copy-start | bytes 328
  1.0 2.5 %copy-start.1 = (bf16[3,3,3,48,384]{4,3,2,1,0:T(8,128)(2,1)S(1)}, bf16[3,3,3,48,384]{4,3,2,1,0:T(8,128)(2,1)}, u32[]{:S(2)}) copy-start(bf16[3,3,3,48,384]{4,3,2,1,0:T(8,128)(2,1)} %param.9) | copy-start | bytes 2985988
  1.0 3.0 %copy-start = (bf16[3,3,3,48,384]{4,3,2,1,0:T(8,128)(2,1)S(1)}, bf16[3,3,3,48,384]{4,3,2,1,0:T(8,128)(2,1)}, u32[]{:S(2)}) copy-start(bf16[3,3,3,48,384]{4,3,2,1,0:T(8,128)(2,1)} %param.8) | copy-start | bytes 2985988
  1.1 6.2 %collective-permute-start = (bf16[448,128]{1,0:T(8,128)(2,1)S(1)}, bf16[448,128]{1,0:T(8,128)(2,1)S(1)}, u32[]{:S(2)}, u32[]{:S(2)}) collective-permute-start(bf16[448,128]{1,0:T(8,128)(2,1)S(1)} %get-tuple-element.21), channel_id=1, source_target_pairs={{0,1},{31,30},{1,2},{2,0},{3,4},{4,3},{5,6},{6,5},{7,8},{8,7},{9,1... | collective-permute-start | bytes 344072 | tf_op jit(solution)/shard_map/ppermute | solution.py:515
  2.9 1.6 %collective-permute-start.3 = (bf16[256,192]{1,0:T(8,128)(2,1)S(1)}, bf16[256,192]{1,0:T(8,128)(2,1)S(1)}, u32[]{:S(2)}, u32[]{:S(2)}) collective-permute-start(bf16[256,192]{1,0:T(8,128)(2,1)S(1)} %get-tuple-element.23.refs_2_), channel_id=1, source_target_pairs={{0,1},{1,0},{2,3},{3,2},{4,5},{5,4},{6,7},{7,6},{8,9},{9,8},{10,11... | collective-permute-start | bytes 294920 | tf_op jit(solution)/shard_map/ppermute | solution.py:514
  2.9 1.6 %collective-permute-start.4 = (bf16[256,192]{1,0:T(8,128)(2,1)S(1)}, bf16[256,192]{1,0:T(8,128)(2,1)S(1)}, u32[]{:S(2)}, u32[]{:S(2)}) collective-permute-start(bf16[256,192]{1,0:T(8,128)(2,1)S(1)} %get-tuple-element.24.refs_3_), channel_id=1, source_target_pairs={{0,1},{1,0},{2,3},{3,2},{4,5},{5,4},{6,7},{7,6},{8,9},{9,8},{10,11... | collective-permute-start | bytes 294920 | tf_op jit(solution)/shard_map/ppermute | solution.py:514
  3.4 1.1 %collective-permute-start.2 = (s32[1,27]{1,0:T(1,128)S(1)}, s32[1,27]{1,0:T(1,128)S(1)}, u32[]{:S(2)}, u32[]{:S(2)}) collective-permute-start(s32[1,27]{1,0:T(1,128)S(1)} %copy-done.3), channel_id=1, source_target_pairs={{0,1},{1,0},{2,3},{3,2},{4,5},{5,4},{6,7},{7,6},{8,9},{9,8},{10,11... | collective-permute-start | bytes 332 | tf_op jit(solution)/shard_map/ppermute | solution.py:513
  3.4 7.7 %collective-permute-start.6 = (bf16[27,48,384]{2,1,0:T(8,128)(2,1)S(1)}, bf16[27,48,384]{2,1,0:T(8,128)(2,1)S(1)}, u32[]{:S(2)}, u32[]{:S(2)}) collective-permute-start(bf16[27,48,384]{2,1,0:T(8,128)(2,1)S(1)} %bitcast.9), channel_id=1, source_target_pairs={{0,1},{1,0},{2,3},{3,2},{4,5},{5,4},{6,7},{7,6},{8,9},{9,8},{10,11... | collective-permute-start | bytes 2985992 | tf_op jit(solution)/shard_map/ppermute | solution.py:519
  8.3 6.1 %collective-permute-start.5 = (bf16[448,128]{1,0:T(8,128)(2,1)S(1)}, bf16[448,128]{1,0:T(8,128)(2,1)S(1)}, u32[]{:S(2)}, u32[]{:S(2)}) collective-permute-start(bf16[448,128]{1,0:T(8,128)(2,1)S(1)} %get-tuple-element.28), channel_id=1, source_target_pairs={{1,0},{30,31},{0,2},{2,1},{3,4},{4,3},{5,6},{6,5},{7,8},{8,7},{9,1... | collective-permute-start | bytes 344072 | tf_op jit(solution)/shard_map/ppermute | solution.py:560
  10.0 1.7 %collective-permute-start.7 = (bf16[256,192]{1,0:T(8,128)(2,1)S(1)}, bf16[256,192]{1,0:T(8,128)(2,1)S(1)}, u32[]{:S(2)}, u32[]{:S(2)}) collective-permute-start(bf16[256,192]{1,0:T(8,128)(2,1)S(1)} %get-tuple-element.29.refs_1_), channel_id=1, source_target_pairs={{0,1},{1,0},{2,3},{3,2},{4,5},{5,4},{6,7},{7,6},{8,9},{9,8},{10,11... | collective-permute-start | bytes 294920 | tf_op jit(solution)/shard_map/ppermute | solution.py:559
  10.0 1.7 %collective-permute-start.8 = (bf16[256,192]{1,0:T(8,128)(2,1)S(1)}, bf16[256,192]{1,0:T(8,128)(2,1)S(1)}, u32[]{:S(2)}, u32[]{:S(2)}) collective-permute-start(bf16[256,192]{1,0:T(8,128)(2,1)S(1)} %get-tuple-element.30.refs_2_), channel_id=1, source_target_pairs={{0,1},{1,0},{2,3},{3,2},{4,5},{5,4},{6,7},{7,6},{8,9},{9,8},{10,11... | collective-permute-start | bytes 294920 | tf_op jit(solution)/shard_map/ppermute | solution.py:559

commit v8 on v7

--- a/solution.py
+++ b/solution.py
@@ -228,8 +228,8 @@
 
 def inside_kernel(*refs, side, chips, counts, opening):
     refs = list(refs)
-    table_refs, *sources = [[refs.pop(0) for _ in range(n)] for n in counts]
-    w, total, near, masks, wide, faces, lhs, tables, semaphores = refs
+    table_refs, extra, *sources = [[refs.pop(0) for _ in range(n)] for n in counts]
+    w, total, near, masks, ends, wide, faces, lhs, tables, semaphores = refs
     copies = [
         pltpu.make_async_copy(ref, tables.at[n], semaphores.at[n])
         for n, ref in enumerate(table_refs)
@@ -290,9 +290,16 @@
             part = acc[:, lane : lane + lanes]
             place = pl.ds(first * plane, count * plane)
             if i == 1:
+                for ref in extra:
+                    part = part + ref[:, lane : lane + lanes].astype(F32)
                 total[p, place, 0:lanes] = part
             else:
                 total[p, place, 0:lanes] += part
+    for p in range(total.shape[0]):
+        for n, z in enumerate((0, side - 1)):
+            ends[p, pl.ds(n * plane, plane), :] = total.at[p][
+                pl.ds(z, plane, stride=side), :
+            ]
     fill(faces, 0, jnp.zeros((6 * plane, width), F32))
     for slot in range(2):
         cut_surface(wide.at[slot], faces, slot + 1, side)
@@ -351,7 +358,7 @@
                 near[p, place, :] = faces[p, pl.ds(start, count * side), :]
 
 
-def add_outside(far, w, near, masks, total, faces, even, odd, side):
+def add_outside(far, w, near, masks, ends, total, faces, even, odd, side):
     width = w.shape[2]
     plane = side * side
     last = side - 1
@@ -419,6 +426,9 @@
         if lanes < LANES:
             pad = jnp.zeros((plane, LANES - lanes), F32)
             part = [jnp.concatenate([value, pad], axis=1) for value in part]
+        for up, z in ((0, 0), (1, last)):
+            line = ends[p, pl.ds(up * plane, plane), :]
+            ref[pl.ds(z, plane, stride=side), :] = line + part[4 + up]
         for up, x in ((0, 0), (1, last)):
             ref[pl.ds(x * plane, plane), :] += part[up]
         for up, y in ((0, 0), (1, last)):
@@ -426,13 +436,11 @@
                 ref[pl.ds(x * plane + y * side, side), :] += part[2 + up][
                     x * side : (x + 1) * side
                 ]
-        for up, z in ((0, 0), (1, last)):
-            ref[pl.ds(z, plane, stride=side), :] += part[4 + up]
-
-
-def first_kernel(far, w, total_in, near, masks, surface, *refs, side):
+
+
+def first_kernel(far, w, total_in, near, masks, ends, surface, *refs, side):
     *outs, total, faces, even, odd = refs
-    add_outside(far, w, near, masks, total, faces, even, odd, side)
+    add_outside(far, w, near, masks, ends, total, faces, even, odd, side)
     active = masks[pl.ds(8 * 13, 1), :]
 
     def change(value):
@@ -447,13 +455,13 @@
 
 
 def second_kernel(
-    occupancy, far, w, features, total_in, near, masks, out, total, faces, even, odd, *, side
+    occupancy, far, w, total_in, near, masks, ends, out, total, faces, even, odd, *, side
 ):
-    add_outside(far, w, near, masks, total, faces, even, odd, side)
+    add_outside(far, w, near, masks, ends, total, faces, even, odd, side)
     active = occupancy[...].astype(F32)
     for p, lane, lanes in pieces(w.shape[2]):
-        value = features[:, lane : lane + lanes].astype(F32) + total[p, :, 0:lanes]
-        out[:, lane : lane + lanes] = jnp.maximum(value, 0.0) * active
+        value = jnp.maximum(total[p, :, 0:lanes], 0.0)
+        out[:, lane : lane + lanes] = value * active
 
 
 def chip_exchanges(chips):
@@ -524,15 +532,16 @@
     sums = ((count, rows, LANES), F32)
     near = ((count, 6 * 3 * (side + 2) * side, LANES), F32)
     masks = ((27 * 8, LANES), F32)
-
-    def inside(layer, tables, here, there, w):
-        counts = (len(tables), len(here), len(there))
+    ends = ((count, 2 * plane, LANES), F32)
+
+    def inside(layer, tables, extra, here, there, w):
+        counts = (len(tables), len(extra), len(here), len(there))
         return call(
             functools.partial(
                 inside_kernel, side=side, chips=chips, counts=counts, opening=layer == 0
             ),
-            (*tables, *here, *there, w),
-            [sums, near, masks],
+            (*tables, *extra, *here, *there, w),
+            [sums, near, masks, ends],
             [
                 VMEM((2, count, rows, LANES), F32),
                 VMEM((count, 3 * 6 * plane, LANES), F32),
@@ -550,7 +559,7 @@
     ]
     hidden_face, *hidden, _ = call(
         functools.partial(first_kernel, side=side),
-        (far, w_one, *inside(0, (neighbours, table_other), own_parts, other, w_one)),
+        (far, w_one, *inside(0, (neighbours, table_other), (), own_parts, other, w_one)),
         [face] + [piece] * PARTS + [sums],
         planes,
         aliases={2: 1 + PARTS},
@@ -564,12 +573,11 @@
             occupancy.reshape(1, 1),
             hidden_far,
             w_two,
-            own,
-            *inside(1, (neighbours,), hidden, hidden_other, w_two),
+            *inside(1, (neighbours,), (own,), hidden, hidden_other, w_two),
         ),
         [wide, sums],
         planes,
-        aliases={4: 1},
+        aliases={3: 1},
     )
     return out.reshape((1, side, side, side, width))
 

time: 16.2 us -> 16.1 us (level)
  transfers between devices with their start and end apart: 9 -> 9, of which waited for: 3 -> 3; matrix products, arithmetic and copies ran while one was open for 0% -> 0% of each run, Pallas kernels for 37% -> 38%
where the time goes in v8:
time: 16.1 us; the launch traced here: 16 us
  Pallas kernels  7.71 us (48%)
  starting transfers between devices  5.04 us (31%)
  waiting for transfers between devices  1.55 us (10%)
  local copies, waits for them, and re-layouts  0.94 us (6%)
  between operations  0.75 us (5%)
    pallas_call x9, Pallas kernels, call(): pl.pallas_call(kernel, out_shape=outs, in_specs=[pl.BlockSpec(memory_spac...  7.71 us
    ppermute x1, starting transfers between devices, body(): far = lax.ppermute(own_face, AXES, first)  1.81 us
    ppermute x1, starting transfers between devices, body(): hidden_far = lax.ppermute(hidden_face, AXES, second)  1.71 us
    unnamed x8, local copies, waits for them, and re-layouts  0.94 us
    ppermute x1, waiting for transfers between devices, body(): far = lax.ppermute(own_face, AXES, first)  0.71 us
    ppermute x1, waiting for transfers between devices, body(): hidden_far = lax.ppermute(hidden_face, AXES, second)  0.7 us
    ppermute x2, starting transfers between devices, body(): other = [lax.ppermute(part, AXES, halves) for part in own_parts]  0.51 us
    ppermute x2, starting transfers between devices, body(): hidden_other = [lax.ppermute(part, AXES, halves) for part in hidden]  0.51 us
  transfers between devices with their start and end apart: 9, of which 3 were waited for; matrix products, arithmetic and copies ran while one was open for 0% of the time, Pallas kernels for 38%

profile of v8, /device:TPU:8, one launch (start us, length us, event | category | flops | bytes accessed | tf_op | source)
XLA Modules:
  0.0 16.0 jit_solution(1215710877185353785)
XLA Ops:
  0.0 0.0 copy-start.2
  0.0 0.0 collective-permute-start.1
  0.0 0.9 %copy-done.2 = bf16[1,8,8,8,192]{4,3,2,1,0:T(8,128)(2,1)S(1)} copy-done((bf16[1,8,8,8,192]{4,3,2,1,0:T(8,128)(2,1)S(1)}, bf16[1,8,8,8,192]{4,3,2,1,0:T(8,128)(2,1)}, u32[]{:S(2)}) %copy-start.2) | copy-done | bytes 196632
  1.0 0.0 copy-start.3
  1.0 0.0 copy-start.1
  1.0 0.0 copy-start
  1.0 0.1 shard_map.57
  1.1 1.8 %collective-permute-start = (bf16[448,128]{1,0:T(8,128)(2,1)S(1)}, bf16[448,128]{1,0:T(8,128)(2,1)S(1)}, u32[]{:S(2)}, u32[]{:S(2)}) collective-permute-start(bf16[448,128]{1,0:T(8,128)(2,1)S(1)} %get-tuple-element.23), channel_id=1, source_target_pairs={{0,1},{31,30},{1,2},{2,0},{3,4},{4,3},{5,6},{6,5},{7,8},{8,7},{9,1... | collective-permute-start | bytes 344072 | tf_op jit(solution)/shard_map/ppermute | solution.py:523
  2.9 0.0 collective-permute-start.3
  2.9 0.5 %collective-permute-start.4 = (bf16[256,192]{1,0:T(8,128)(2,1)S(1)}, bf16[256,192]{1,0:T(8,128)(2,1)S(1)}, u32[]{:S(2)}, u32[]{:S(2)}) collective-permute-start(bf16[256,192]{1,0:T(8,128)(2,1)S(1)} %get-tuple-element.26.refs_3_), channel_id=1, source_target_pairs={{0,1},{1,0},{2,3},{3,2},{4,5},{5,4},{6,7},{7,6},{8,9},{9,8},{10,11... | collective-permute-start | bytes 294920 | tf_op jit(solution)/shard_map/ppermute | solution.py:522
  3.4 0.0 copy-done.3
  3.4 0.0 collective-permute-start.2
  3.4 0.0 collective-permute-done.1.other_ref
  3.4 0.0 copy-done.1
  3.4 0.5 %collective-permute-start.6 = (bf16[27,48,384]{2,1,0:T(8,128)(2,1)S(1)}, bf16[27,48,384]{2,1,0:T(8,128)(2,1)S(1)}, u32[]{:S(2)}, u32[]{:S(2)}) collective-permute-start(bf16[27,48,384]{2,1,0:T(8,128)(2,1)S(1)} %bitcast.9), channel_id=1, source_target_pairs={{0,1},{1,0},{2,3},{3,2},{4,5},{5,4},{6,7},{7,6},{8,9},{9,8},{10,11... | collective-permute-start | bytes 2985992 | tf_op jit(solution)/shard_map/ppermute | solution.py:527
  3.9 0.0 copy-done
  3.9 0.5 %shard_map.58.refs_6_.w = bf16[3,1728,192]{2,1,0:T(8,128)(2,1)S(1)} custom-call(bf16[27,48,384]{2,1,0:T(8,128)(2,1)S(1)} %bitcast.8, bf16[27,48,384]{2,1,0:T(8,128)(2,1)S(1)} %collective-permute-done.1.other_ref), custom_call_target="tpu_custom_call" | custom-call | tf_op jit(solution)/shard_map/pallas_call | solution.py:484
  4.4 0.1 collective-permute-done.2.refs_1_
  4.5 0.0 collective-permute-done.3.refs_4_
  4.5 0.0 collective-permute-done.4.refs_5_
  4.6 2.0 %shard_map.59 = (f32[2,512,128]{2,1,0:T(8,128)S(1)}, f32[2,1440,128]{2,1,0:T(8,128)S(1)}, f32[216,128]{1,0:T(8,128)S(1)}, f32[2,128,128]{2,1,0:T(8,128)S(1)}) custom-call(s32[1,27]{1,0:T(1,128)S(1)} %copy-done.3, s32[1,27]{1,0:T(1,128)S(1)} %collective-permute-done.2.refs_1_, bf16[256,192]{1,0:T(8,128)(2,1)S(1)} %get-tuple-element.25.refs_2_, ...), custom_call_target="tpu_custom_call" | custom-call | tf_op jit(solution)/shard_map/pallas_call | solution.py:484
  6.6 0.7 %collective-permute-done.far = bf16[448,128]{1,0:T(8,128)(2,1)S(1)} collective-permute-done((bf16[448,128]{1,0:T(8,128)(2,1)S(1)}, bf16[448,128]{1,0:T(8,128)(2,1)S(1)}, u32[]{:S(2)}, u32[]{:S(2)}) %collective-permute-start) | collective-permute-done | bytes 114720 | tf_op jit(solution)/shard_map/ppermute | solution.py:523
  7.3 1.0 %shard_map.60 = (bf16[448,128]{1,0:T(8,128)(2,1)S(1)}, bf16[256,192]{1,0:T(8,128)(2,1)S(1)}, bf16[256,192]{1,0:T(8,128)(2,1)S(1)}, f32[2,512,128]{2,1,0:T(8,128)S(1)}) custom-call(bf16[448,128]{1,0:T(8,128)(2,1)S(1)} %collective-permute-done.far, bf16[3,1728,192]{2,1,0:T(8,128)(2,1)S(1)} %shard_map.58.refs_6_.w, ...), custom_call_target="tpu_custom_call", output_to_operand_aliasing={{3}: (2, {})} | custom-call | flops 17999998976 | tf_op jit(solution)/shard_map/pallas_call | solution.py:484
  8.3 1.7 %collective-permute-start.5 = (bf16[448,128]{1,0:T(8,128)(2,1)S(1)}, bf16[448,128]{1,0:T(8,128)(2,1)S(1)}, u32[]{:S(2)}, u32[]{:S(2)}) collective-permute-start(bf16[448,128]{1,0:T(8,128)(2,1)S(1)} %get-tuple-element.31), channel_id=1, source_target_pairs={{1,0},{30,31},{0,2},{2,1},{3,4},{4,3},{5,6},{6,5},{7,8},{8,7},{9,1... | collective-permute-start | bytes 344072 | tf_op jit(solution)/shard_map/ppermute | solution.py:569
  10.0 0.0 collective-permute-start.7
  10.0 0.5 %collective-permute-start.8 = (bf16[256,192]{1,0:T(8,128)(2,1)S(1)}, bf16[256,192]{1,0:T(8,128)(2,1)S(1)}, u32[]{:S(2)}, u32[]{:S(2)}) collective-permute-start(bf16[256,192]{1,0:T(8,128)(2,1)S(1)} %get-tuple-element.33.refs_3_), channel_id=1, source_target_pairs={{0,1},{1,0},{2,3},{3,2},{4,5},{5,4},{6,7},{7,6},{8,9},{9,8},{10,11... | collective-permute-start | bytes 294920 | tf_op jit(solution)/shard_map/ppermute | solution.py:568
  11.1 0.0 collective-permute-done.6.other_ref
  11.1 0.5 %shard_map.61.refs_6_.w = bf16[3,1728,192]{2,1,0:T(8,128)(2,1)S(1)} custom-call(bf16[27,48,384]{2,1,0:T(8,128)(2,1)S(1)} %bitcast.10, bf16[27,48,384]{2,1,0:T(8,128)(2,1)S(1)} %collective-permute-done.6.other_ref), custom_call_target="tpu_custom_call" | custom-call | tf_op jit(solution)/shard_map/pallas_call | solution.py:484
  11.6 0.0 collective-permute-done.7.refs_4_
  11.6 0.0 collective-permute-done.8.refs_5_
  11.6 2.0 %shard_map.62 = (f32[2,512,128]{2,1,0:T(8,128)S(1)}, f32[2,1440,128]{2,1,0:T(8,128)S(1)}, f32[216,128]{1,0:T(8,128)S(1)}, f32[2,128,128]{2,1,0:T(8,128)S(1)}) custom-call(s32[1,27]{1,0:T(1,128)S(1)} %copy-done.3, bf16[512,192]{1,0:T(8,128)(2,1)S(1)} %bitcast.12, bf16[256,192]{1,0:T(8,128)(2,1)S(1)} %get-tuple-element.32.refs_2_, ...), custom_call_target="tpu_custom_call" | custom-call | tf_op jit(solution)/shard_map/pallas_call | solution.py:484
  13.6 0.7 %collective-permute-done.5.far = bf16[448,128]{1,0:T(8,128)(2,1)S(1)} collective-permute-done((bf16[448,128]{1,0:T(8,128)(2,1)S(1)}, bf16[448,128]{1,0:T(8,128)(2,1)S(1)}, u32[]{:S(2)}, u32[]{:S(2)}) %collective-permute-start.5) | collective-permute-done | bytes 114720 | tf_op jit(solution)/shard_map/ppermute | solution.py:569
  14.3 1.7 %shard_map.63 = (f32[512,192]{1,0:T(8,128)}, f32[2,512,128]{2,1,0:T(8,128)S(1)}) custom-call(s32[1,1]{1,0:T(1,128)} %bitcast.6.occupancy, bf16[448,128]{1,0:T(8,128)(2,1)S(1)} %collective-permute-done.5.far, bf16[3,1728,192]{2,1,0:T(8,128)(2,1)S(1)} %shard_map.61.refs_6_.w, ...), custom_call_target="tpu_custom_call", output_to_operand_aliasing={{1}: (3, {})} | custom-call | tf_op jit(solution)/shard_map/pallas_call | solution.py:484
  (2 shorter events, 0.0 us)
Async XLA Ops:
  0.0 0.9 %copy-start.2 = (bf16[1,8,8,8,192]{4,3,2,1,0:T(8,128)(2,1)S(1)}, bf16[1,8,8,8,192]{4,3,2,1,0:T(8,128)(2,1)}, u32[]{:S(2)}) copy-start(bf16[1,8,8,8,192]{4,3,2,1,0:T(8,128)(2,1)} %param.5) | copy-start | bytes 589828
  0.0 3.4 %collective-permute-start.1 = (bf16[27,48,384]{2,1,0:T(8,128)(2,1)}, bf16[27,48,384]{2,1,0:T(8,128)(2,1)S(1)}, u32[]{:S(2)}, u32[]{:S(2)}) collective-permute-start(bf16[27,48,384]{2,1,0:T(8,128)(2,1)} %bitcast.7), channel_id=1, source_target_pairs={{0,1},{1,0},{2,3},{3,2},{4,5},{5,4},{6,7},{7,6},{8,9},{9,8},{10,11... | collective-permute-start | bytes 2985992 | tf_op jit(solution)/shard_map/ppermute | solution.py:527
  1.0 2.5 %copy-start.3 = (s32[1,27]{1,0:T(1,128)S(1)}, s32[1,27]{1,0:T(1,128)}, u32[]{:S(2)}) copy-start(s32[1,27]{1,0:T(1,128)} %refs_0_.3) | copy-start | bytes 328
  1.0 2.5 %copy-start.1 = (bf16[3,3,3,48,384]{4,3,2,1,0:T(8,128)(2,1)S(1)}, bf16[3,3,3,48,384]{4,3,2,1,0:T(8,128)(2,1)}, u32[]{:S(2)}) copy-start(bf16[3,3,3,48,384]{4,3,2,1,0:T(8,128)(2,1)} %param.9) | copy-start | bytes 2985988
  1.0 3.0 %copy-start = (bf16[3,3,3,48,384]{4,3,2,1,0:T(8,128)(2,1)S(1)}, bf16[3,3,3,48,384]{4,3,2,1,0:T(8,128)(2,1)}, u32[]{:S(2)}) copy-start(bf16[3,3,3,48,384]{4,3,2,1,0:T(8,128)(2,1)} %param.8) | copy-start | bytes 2985988
  1.1 6.2 %collective-permute-start = (bf16[448,128]{1,0:T(8,128)(2,1)S(1)}, bf16[448,128]{1,0:T(8,128)(2,1)S(1)}, u32[]{:S(2)}, u32[]{:S(2)}) collective-permute-start(bf16[448,128]{1,0:T(8,128)(2,1)S(1)} %get-tuple-element.23), channel_id=1, source_target_pairs={{0,1},{31,30},{1,2},{2,0},{3,4},{4,3},{5,6},{6,5},{7,8},{8,7},{9,1... | collective-permute-start | bytes 344072 | tf_op jit(solution)/shard_map/ppermute | solution.py:523
  2.9 1.6 %collective-permute-start.3 = (bf16[256,192]{1,0:T(8,128)(2,1)S(1)}, bf16[256,192]{1,0:T(8,128)(2,1)S(1)}, u32[]{:S(2)}, u32[]{:S(2)}) collective-permute-start(bf16[256,192]{1,0:T(8,128)(2,1)S(1)} %get-tuple-element.25.refs_2_), channel_id=1, source_target_pairs={{0,1},{1,0},{2,3},{3,2},{4,5},{5,4},{6,7},{7,6},{8,9},{9,8},{10,11... | collective-permute-start | bytes 294920 | tf_op jit(solution)/shard_map/ppermute | solution.py:522
  2.9 1.6 %collective-permute-start.4 = (bf16[256,192]{1,0:T(8,128)(2,1)S(1)}, bf16[256,192]{1,0:T(8,128)(2,1)S(1)}, u32[]{:S(2)}, u32[]{:S(2)}) collective-permute-start(bf16[256,192]{1,0:T(8,128)(2,1)S(1)} %get-tuple-element.26.refs_3_), channel_id=1, source_target_pairs={{0,1},{1,0},{2,3},{3,2},{4,5},{5,4},{6,7},{7,6},{8,9},{9,8},{10,11... | collective-permute-start | bytes 294920 | tf_op jit(solution)/shard_map/ppermute | solution.py:522
  3.4 1.1 %collective-permute-start.2 = (s32[1,27]{1,0:T(1,128)S(1)}, s32[1,27]{1,0:T(1,128)S(1)}, u32[]{:S(2)}, u32[]{:S(2)}) collective-permute-start(s32[1,27]{1,0:T(1,128)S(1)} %copy-done.3), channel_id=1, source_target_pairs={{0,1},{1,0},{2,3},{3,2},{4,5},{5,4},{6,7},{7,6},{8,9},{9,8},{10,11... | collective-permute-start | bytes 332 | tf_op jit(solution)/shard_map/ppermute | solution.py:521
  3.4 7.7 %collective-permute-start.6 = (bf16[27,48,384]{2,1,0:T(8,128)(2,1)S(1)}, bf16[27,48,384]{2,1,0:T(8,128)(2,1)S(1)}, u32[]{:S(2)}, u32[]{:S(2)}) collective-permute-start(bf16[27,48,384]{2,1,0:T(8,128)(2,1)S(1)} %bitcast.9), channel_id=1, source_target_pairs={{0,1},{1,0},{2,3},{3,2},{4,5},{5,4},{6,7},{7,6},{8,9},{9,8},{10,11... | collective-permute-start | bytes 2985992 | tf_op jit(solution)/shard_map/ppermute | solution.py:527
  8.3 6.1 %collective-permute-start.5 = (bf16[448,128]{1,0:T(8,128)(2,1)S(1)}, bf16[448,128]{1,0:T(8,128)(2,1)S(1)}, u32[]{:S(2)}, u32[]{:S(2)}) collective-permute-start(bf16[448,128]{1,0:T(8,128)(2,1)S(1)} %get-tuple-element.31), channel_id=1, source_target_pairs={{1,0},{30,31},{0,2},{2,1},{3,4},{4,3},{5,6},{6,5},{7,8},{8,7},{9,1... | collective-permute-start | bytes 344072 | tf_op jit(solution)/shard_map/ppermute | solution.py:569
  10.0 1.7 %collective-permute-start.7 = (bf16[256,192]{1,0:T(8,128)(2,1)S(1)}, bf16[256,192]{1,0:T(8,128)(2,1)S(1)}, u32[]{:S(2)}, u32[]{:S(2)}) collective-permute-start(bf16[256,192]{1,0:T(8,128)(2,1)S(1)} %get-tuple-element.32.refs_2_), channel_id=1, source_target_pairs={{0,1},{1,0},{2,3},{3,2},{4,5},{5,4},{6,7},{7,6},{8,9},{9,8},{10,11... | collective-permute-start | bytes 294920 | tf_op jit(solution)/shard_map/ppermute | solution.py:568
  10.0 1.7 %collective-permute-start.8 = (bf16[256,192]{1,0:T(8,128)(2,1)S(1)}, bf16[256,192]{1,0:T(8,128)(2,1)S(1)}, u32[]{:S(2)}, u32[]{:S(2)}) collective-permute-start(bf16[256,192]{1,0:T(8,128)(2,1)S(1)} %get-tuple-element.33.refs_3_), channel_id=1, source_target_pairs={{0,1},{1,0},{2,3},{3,2},{4,5},{5,4},{6,7},{7,6},{8,9},{9,8},{10,11... | collective-permute-start | bytes 294920 | tf_op jit(solution)/shard_map/ppermute | solution.py:568

commit v9 on v8

--- a/solution.py
+++ b/solution.py
@@ -358,7 +358,7 @@
                 near[p, place, :] = faces[p, pl.ds(start, count * side), :]
 
 
-def add_outside(far, w, near, masks, ends, total, faces, even, odd, side):
+def add_outside(far, w, near, masks, ends, total, faces, even, odd, side, finish=None):
     width = w.shape[2]
     plane = side * side
     last = side - 1
@@ -436,6 +436,8 @@
                 ref[pl.ds(x * plane + y * side, side), :] += part[2 + up][
                     x * side : (x + 1) * side
                 ]
+        if finish is not None:
+            finish(p, lane, lanes)
 
 
 def first_kernel(far, w, total_in, near, masks, ends, surface, *refs, side):
@@ -455,13 +457,24 @@
 
 
 def second_kernel(
-    occupancy, far, w, total_in, near, masks, ends, out, total, faces, even, odd, *, side
+    occupancy, far, w, total_in, near, masks, ends, out, total, *refs, side
 ):
-    add_outside(far, w, near, masks, ends, total, faces, even, odd, side)
+    faces, even, odd, block, semaphores = refs
     active = occupancy[...].astype(F32)
-    for p, lane, lanes in pieces(w.shape[2]):
+    copies = []
+
+    def finish(p, lane, lanes):
         value = jnp.maximum(total[p, :, 0:lanes], 0.0)
-        out[:, lane : lane + lanes] = value * active
+        block[:, lane : lane + lanes] = value * active
+        place = (slice(None), pl.ds(lane, lanes))
+        copies.append(
+            pltpu.make_async_copy(block.at[place], out.at[place], semaphores.at[p])
+        )
+        copies[-1].start()
+
+    add_outside(far, w, near, masks, ends, total, faces, even, odd, side, finish)
+    for copy in copies:
+        copy.wait()
 
 
 def chip_exchanges(chips):
@@ -479,14 +492,15 @@
     return first, second
 
 
-def call(kernel, operands, outs, scratch=(), anywhere=0, cost=0, aliases={}):
+def call(kernel, operands, outs, scratch=(), anywhere=0, cost=0, aliases={}, result_space=VMEM):
     outs = [jax.ShapeDtypeStruct(shape, kind) for shape, kind in outs]
     result = pl.pallas_call(
         kernel,
         out_shape=outs,
         in_specs=[pl.BlockSpec(memory_space=pl.ANY)] * anywhere
         + [pl.BlockSpec(memory_space=VMEM)] * (len(operands) - anywhere),
-        out_specs=[pl.BlockSpec(memory_space=VMEM)] * len(outs),
+        out_specs=[pl.BlockSpec(memory_space=result_space)]
+        + [pl.BlockSpec(memory_space=VMEM)] * (len(outs) - 1),
         scratch_shapes=list(scratch),
         input_output_aliases=aliases,
         compiler_params=pltpu.CompilerParams(vmem_limit_bytes=32 * 2**20),
@@ -576,7 +590,8 @@
             *inside(1, (neighbours,), (own,), hidden, hidden_other, w_two),
         ),
         [wide, sums],
-        planes,
+        planes + [VMEM((rows, width), F32), pltpu.SemaphoreType.DMA((count,))],
+        result_space=pl.ANY,
         aliases={3: 1},
     )
     return out.reshape((1, side, side, side, width))

time: 16.1 us -> 16.1 us (level)
  no operation moved by 1% of the time
where the time goes in v9:
time: 16.1 us; the launch traced here: 16 us
  Pallas kernels  7.72 us (48%)
  starting transfers between devices  5.04 us (31%)
  waiting for transfers between devices  1.55 us (10%)
  local copies, waits for them, and re-layouts  0.94 us (6%)
  between operations  0.75 us (5%)
    pallas_call x9, Pallas kernels, call(): pl.pallas_call(kernel, out_shape=outs, in_specs=[pl.BlockSpec(memory_spac...  7.72 us
    ppermute x1, starting transfers between devices, body(): far = lax.ppermute(own_face, AXES, first)  1.81 us
    ppermute x1, starting transfers between devices, body(): hidden_far = lax.ppermute(hidden_face, AXES, second)  1.71 us
    unnamed x8, local copies, waits for them, and re-layouts  0.94 us
    ppermute x1, waiting for transfers between devices, body(): far = lax.ppermute(own_face, AXES, first)  0.71 us
    ppermute x1, waiting for transfers between devices, body(): hidden_far = lax.ppermute(hidden_face, AXES, second)  0.7 us
    ppermute x2, starting transfers between devices, body(): other = [lax.ppermute(part, AXES, halves) for part in own_parts]  0.51 us
    ppermute x2, starting transfers between devices, body(): hidden_other = [lax.ppermute(part, AXES, halves) for part in hidden]  0.51 us
  transfers between devices with their start and end apart: 9, of which 3 were waited for; matrix products, arithmetic and copies ran while one was open for 0% of the time, Pallas kernels for 38%

profile of v9, /device:TPU:8, one launch (start us, length us, event | category | flops | bytes accessed | tf_op | source)
XLA Modules:
  0.0 16.0 jit_solution(9255218210071652334)
XLA Ops:
  0.0 0.0 copy-start.2
  0.0 0.0 collective-permute-start.1
  0.0 0.9 %copy-done.2 = bf16[1,8,8,8,192]{4,3,2,1,0:T(8,128)(2,1)S(1)} copy-done((bf16[1,8,8,8,192]{4,3,2,1,0:T(8,128)(2,1)S(1)}, bf16[1,8,8,8,192]{4,3,2,1,0:T(8,128)(2,1)}, u32[]{:S(2)}) %copy-start.2) | copy-done | bytes 196632
  1.0 0.0 copy-start.3
  1.0 0.0 copy-start.1
  1.0 0.0 copy-start
  1.0 0.1 shard_map.57
  1.1 1.8 %collective-permute-start = (bf16[448,128]{1,0:T(8,128)(2,1)S(1)}, bf16[448,128]{1,0:T(8,128)(2,1)S(1)}, u32[]{:S(2)}, u32[]{:S(2)}) collective-permute-start(bf16[448,128]{1,0:T(8,128)(2,1)S(1)} %get-tuple-element.23), channel_id=1, source_target_pairs={{0,1},{31,30},{1,2},{2,0},{3,4},{4,3},{5,6},{6,5},{7,8},{8,7},{9,1... | collective-permute-start | bytes 344072 | tf_op jit(solution)/shard_map/ppermute | solution.py:537
  2.9 0.0 collective-permute-start.3
  2.9 0.5 %collective-permute-start.4 = (bf16[256,192]{1,0:T(8,128)(2,1)S(1)}, bf16[256,192]{1,0:T(8,128)(2,1)S(1)}, u32[]{:S(2)}, u32[]{:S(2)}) collective-permute-start(bf16[256,192]{1,0:T(8,128)(2,1)S(1)} %get-tuple-element.26.refs_3_), channel_id=1, source_target_pairs={{0,1},{1,0},{2,3},{3,2},{4,5},{5,4},{6,7},{7,6},{8,9},{9,8},{10,11... | collective-permute-start | bytes 294920 | tf_op jit(solution)/shard_map/ppermute | solution.py:536
  3.4 0.0 copy-done.3
  3.4 0.0 collective-permute-start.2
  3.4 0.0 collective-permute-done.1.other_ref
  3.4 0.0 copy-done.1
  3.4 0.5 %collective-permute-start.6 = (bf16[27,48,384]{2,1,0:T(8,128)(2,1)S(1)}, bf16[27,48,384]{2,1,0:T(8,128)(2,1)S(1)}, u32[]{:S(2)}, u32[]{:S(2)}) collective-permute-start(bf16[27,48,384]{2,1,0:T(8,128)(2,1)S(1)} %bitcast.9), channel_id=1, source_target_pairs={{0,1},{1,0},{2,3},{3,2},{4,5},{5,4},{6,7},{7,6},{8,9},{9,8},{10,11... | collective-permute-start | bytes 2985992 | tf_op jit(solution)/shard_map/ppermute | solution.py:541
  3.9 0.0 copy-done
  3.9 0.5 %shard_map.58.refs_6_.w = bf16[3,1728,192]{2,1,0:T(8,128)(2,1)S(1)} custom-call(bf16[27,48,384]{2,1,0:T(8,128)(2,1)S(1)} %bitcast.8, bf16[27,48,384]{2,1,0:T(8,128)(2,1)S(1)} %collective-permute-done.1.other_ref), custom_call_target="tpu_custom_call" | custom-call | tf_op jit(solution)/shard_map/pallas_call | solution.py:497
  4.4 0.1 collective-permute-done.2.refs_1_
  4.5 0.0 collective-permute-done.3.refs_4_
  4.5 0.0 collective-permute-done.4.refs_5_
  4.6 2.0 %shard_map.59 = (f32[2,512,128]{2,1,0:T(8,128)S(1)}, f32[2,1440,128]{2,1,0:T(8,128)S(1)}, f32[216,128]{1,0:T(8,128)S(1)}, f32[2,128,128]{2,1,0:T(8,128)S(1)}) custom-call(s32[1,27]{1,0:T(1,128)S(1)} %copy-done.3, s32[1,27]{1,0:T(1,128)S(1)} %collective-permute-done.2.refs_1_, bf16[256,192]{1,0:T(8,128)(2,1)S(1)} %get-tuple-element.25.refs_2_, ...), custom_call_target="tpu_custom_call" | custom-call | tf_op jit(solution)/shard_map/pallas_call | solution.py:497
  6.6 0.7 %collective-permute-done.far = bf16[448,128]{1,0:T(8,128)(2,1)S(1)} collective-permute-done((bf16[448,128]{1,0:T(8,128)(2,1)S(1)}, bf16[448,128]{1,0:T(8,128)(2,1)S(1)}, u32[]{:S(2)}, u32[]{:S(2)}) %collective-permute-start) | collective-permute-done | bytes 114720 | tf_op jit(solution)/shard_map/ppermute | solution.py:537
  7.3 1.0 %shard_map.60 = (bf16[448,128]{1,0:T(8,128)(2,1)S(1)}, bf16[256,192]{1,0:T(8,128)(2,1)S(1)}, bf16[256,192]{1,0:T(8,128)(2,1)S(1)}, f32[2,512,128]{2,1,0:T(8,128)S(1)}) custom-call(bf16[448,128]{1,0:T(8,128)(2,1)S(1)} %collective-permute-done.far, bf16[3,1728,192]{2,1,0:T(8,128)(2,1)S(1)} %shard_map.58.refs_6_.w, ...), custom_call_target="tpu_custom_call", output_to_operand_aliasing={{3}: (2, {})} | custom-call | flops 17999998976 | tf_op jit(solution)/shard_map/pallas_call | solution.py:497
  8.3 1.7 %collective-permute-start.5 = (bf16[448,128]{1,0:T(8,128)(2,1)S(1)}, bf16[448,128]{1,0:T(8,128)(2,1)S(1)}, u32[]{:S(2)}, u32[]{:S(2)}) collective-permute-start(bf16[448,128]{1,0:T(8,128)(2,1)S(1)} %get-tuple-element.31), channel_id=1, source_target_pairs={{1,0},{30,31},{0,2},{2,1},{3,4},{4,3},{5,6},{6,5},{7,8},{8,7},{9,1... | collective-permute-start | bytes 344072 | tf_op jit(solution)/shard_map/ppermute | solution.py:583
  10.0 0.0 collective-permute-start.7
  10.0 0.5 %collective-permute-start.8 = (bf16[256,192]{1,0:T(8,128)(2,1)S(1)}, bf16[256,192]{1,0:T(8,128)(2,1)S(1)}, u32[]{:S(2)}, u32[]{:S(2)}) collective-permute-start(bf16[256,192]{1,0:T(8,128)(2,1)S(1)} %get-tuple-element.33.refs_3_), channel_id=1, source_target_pairs={{0,1},{1,0},{2,3},{3,2},{4,5},{5,4},{6,7},{7,6},{8,9},{9,8},{10,11... | collective-permute-start | bytes 294920 | tf_op jit(solution)/shard_map/ppermute | solution.py:582
  11.1 0.0 collective-permute-done.6.other_ref
  11.1 0.5 %shard_map.61.refs_6_.w = bf16[3,1728,192]{2,1,0:T(8,128)(2,1)S(1)} custom-call(bf16[27,48,384]{2,1,0:T(8,128)(2,1)S(1)} %bitcast.10, bf16[27,48,384]{2,1,0:T(8,128)(2,1)S(1)} %collective-permute-done.6.other_ref), custom_call_target="tpu_custom_call" | custom-call | tf_op jit(solution)/shard_map/pallas_call | solution.py:497
  11.6 0.0 collective-permute-done.7.refs_4_
  11.6 0.0 collective-permute-done.8.refs_5_
  11.6 2.0 %shard_map.62 = (f32[2,512,128]{2,1,0:T(8,128)S(1)}, f32[2,1440,128]{2,1,0:T(8,128)S(1)}, f32[216,128]{1,0:T(8,128)S(1)}, f32[2,128,128]{2,1,0:T(8,128)S(1)}) custom-call(s32[1,27]{1,0:T(1,128)S(1)} %copy-done.3, bf16[512,192]{1,0:T(8,128)(2,1)S(1)} %bitcast.12, bf16[256,192]{1,0:T(8,128)(2,1)S(1)} %get-tuple-element.32.refs_2_, ...), custom_call_target="tpu_custom_call" | custom-call | tf_op jit(solution)/shard_map/pallas_call | solution.py:497
  13.6 0.7 %collective-permute-done.5.far = bf16[448,128]{1,0:T(8,128)(2,1)S(1)} collective-permute-done((bf16[448,128]{1,0:T(8,128)(2,1)S(1)}, bf16[448,128]{1,0:T(8,128)(2,1)S(1)}, u32[]{:S(2)}, u32[]{:S(2)}) %collective-permute-start.5) | collective-permute-done | bytes 114720 | tf_op jit(solution)/shard_map/ppermute | solution.py:583
  14.3 1.7 %shard_map.63 = (f32[512,192]{1,0:T(8,128)}, f32[2,512,128]{2,1,0:T(8,128)S(1)}) custom-call(s32[1,1]{1,0:T(1,128)} %bitcast.6.occupancy, bf16[448,128]{1,0:T(8,128)(2,1)S(1)} %collective-permute-done.5.far, bf16[3,1728,192]{2,1,0:T(8,128)(2,1)S(1)} %shard_map.61.refs_6_.w, ...), custom_call_target="tpu_custom_call", output_to_operand_aliasing={{1}: (3, {})} | custom-call | tf_op jit(solution)/shard_map/pallas_call | solution.py:497
  (2 shorter events, 0.0 us)
Async XLA Ops:
  0.0 0.9 %copy-start.2 = (bf16[1,8,8,8,192]{4,3,2,1,0:T(8,128)(2,1)S(1)}, bf16[1,8,8,8,192]{4,3,2,1,0:T(8,128)(2,1)}, u32[]{:S(2)}) copy-start(bf16[1,8,8,8,192]{4,3,2,1,0:T(8,128)(2,1)} %param.5) | copy-start | bytes 589828
  0.0 3.4 %collective-permute-start.1 = (bf16[27,48,384]{2,1,0:T(8,128)(2,1)}, bf16[27,48,384]{2,1,0:T(8,128)(2,1)S(1)}, u32[]{:S(2)}, u32[]{:S(2)}) collective-permute-start(bf16[27,48,384]{2,1,0:T(8,128)(2,1)} %bitcast.7), channel_id=1, source_target_pairs={{0,1},{1,0},{2,3},{3,2},{4,5},{5,4},{6,7},{7,6},{8,9},{9,8},{10,11... | collective-permute-start | bytes 2985992 | tf_op jit(solution)/shard_map/ppermute | solution.py:541
  1.0 2.5 %copy-start.3 = (s32[1,27]{1,0:T(1,128)S(1)}, s32[1,27]{1,0:T(1,128)}, u32[]{:S(2)}) copy-start(s32[1,27]{1,0:T(1,128)} %refs_0_.3) | copy-start | bytes 328
  1.0 2.5 %copy-start.1 = (bf16[3,3,3,48,384]{4,3,2,1,0:T(8,128)(2,1)S(1)}, bf16[3,3,3,48,384]{4,3,2,1,0:T(8,128)(2,1)}, u32[]{:S(2)}) copy-start(bf16[3,3,3,48,384]{4,3,2,1,0:T(8,128)(2,1)} %param.9) | copy-start | bytes 2985988
  1.0 3.0 %copy-start = (bf16[3,3,3,48,384]{4,3,2,1,0:T(8,128)(2,1)S(1)}, bf16[3,3,3,48,384]{4,3,2,1,0:T(8,128)(2,1)}, u32[]{:S(2)}) copy-start(bf16[3,3,3,48,384]{4,3,2,1,0:T(8,128)(2,1)} %param.8) | copy-start | bytes 2985988
  1.1 6.2 %collective-permute-start = (bf16[448,128]{1,0:T(8,128)(2,1)S(1)}, bf16[448,128]{1,0:T(8,128)(2,1)S(1)}, u32[]{:S(2)}, u32[]{:S(2)}) collective-permute-start(bf16[448,128]{1,0:T(8,128)(2,1)S(1)} %get-tuple-element.23), channel_id=1, source_target_pairs={{0,1},{31,30},{1,2},{2,0},{3,4},{4,3},{5,6},{6,5},{7,8},{8,7},{9,1... | collective-permute-start | bytes 344072 | tf_op jit(solution)/shard_map/ppermute | solution.py:537
  2.9 1.6 %collective-permute-start.3 = (bf16[256,192]{1,0:T(8,128)(2,1)S(1)}, bf16[256,192]{1,0:T(8,128)(2,1)S(1)}, u32[]{:S(2)}, u32[]{:S(2)}) collective-permute-start(bf16[256,192]{1,0:T(8,128)(2,1)S(1)} %get-tuple-element.25.refs_2_), channel_id=1, source_target_pairs={{0,1},{1,0},{2,3},{3,2},{4,5},{5,4},{6,7},{7,6},{8,9},{9,8},{10,11... | collective-permute-start | bytes 294920 | tf_op jit(solution)/shard_map/ppermute | solution.py:536
  2.9 1.6 %collective-permute-start.4 = (bf16[256,192]{1,0:T(8,128)(2,1)S(1)}, bf16[256,192]{1,0:T(8,128)(2,1)S(1)}, u32[]{:S(2)}, u32[]{:S(2)}) collective-permute-start(bf16[256,192]{1,0:T(8,128)(2,1)S(1)} %get-tuple-element.26.refs_3_), channel_id=1, source_target_pairs={{0,1},{1,0},{2,3},{3,2},{4,5},{5,4},{6,7},{7,6},{8,9},{9,8},{10,11... | collective-permute-start | bytes 294920 | tf_op jit(solution)/shard_map/ppermute | solution.py:536
  3.4 1.1 %collective-permute-start.2 = (s32[1,27]{1,0:T(1,128)S(1)}, s32[1,27]{1,0:T(1,128)S(1)}, u32[]{:S(2)}, u32[]{:S(2)}) collective-permute-start(s32[1,27]{1,0:T(1,128)S(1)} %copy-done.3), channel_id=1, source_target_pairs={{0,1},{1,0},{2,3},{3,2},{4,5},{5,4},{6,7},{7,6},{8,9},{9,8},{10,11... | collective-permute-start | bytes 332 | tf_op jit(solution)/shard_map/ppermute | solution.py:535
  3.4 7.7 %collective-permute-start.6 = (bf16[27,48,384]{2,1,0:T(8,128)(2,1)S(1)}, bf16[27,48,384]{2,1,0:T(8,128)(2,1)S(1)}, u32[]{:S(2)}, u32[]{:S(2)}) collective-permute-start(bf16[27,48,384]{2,1,0:T(8,128)(2,1)S(1)} %bitcast.9), channel_id=1, source_target_pairs={{0,1},{1,0},{2,3},{3,2},{4,5},{5,4},{6,7},{7,6},{8,9},{9,8},{10,11... | collective-permute-start | bytes 2985992 | tf_op jit(solution)/shard_map/ppermute | solution.py:541
  8.3 6.1 %collective-permute-start.5 = (bf16[448,128]{1,0:T(8,128)(2,1)S(1)}, bf16[448,128]{1,0:T(8,128)(2,1)S(1)}, u32[]{:S(2)}, u32[]{:S(2)}) collective-permute-start(bf16[448,128]{1,0:T(8,128)(2,1)S(1)} %get-tuple-element.31), channel_id=1, source_target_pairs={{1,0},{30,31},{0,2},{2,1},{3,4},{4,3},{5,6},{6,5},{7,8},{8,7},{9,1... | collective-permute-start | bytes 344072 | tf_op jit(solution)/shard_map/ppermute | solution.py:583
  10.0 1.7 %collective-permute-start.7 = (bf16[256,192]{1,0:T(8,128)(2,1)S(1)}, bf16[256,192]{1,0:T(8,128)(2,1)S(1)}, u32[]{:S(2)}, u32[]{:S(2)}) collective-permute-start(bf16[256,192]{1,0:T(8,128)(2,1)S(1)} %get-tuple-element.32.refs_2_), channel_id=1, source_target_pairs={{0,1},{1,0},{2,3},{3,2},{4,5},{5,4},{6,7},{7,6},{8,9},{9,8},{10,11... | collective-permute-start | bytes 294920 | tf_op jit(solution)/shard_map/ppermute | solution.py:582
  10.0 1.7 %collective-permute-start.8 = (bf16[256,192]{1,0:T(8,128)(2,1)S(1)}, bf16[256,192]{1,0:T(8,128)(2,1)S(1)}, u32[]{:S(2)}, u32[]{:S(2)}) collective-permute-start(bf16[256,192]{1,0:T(8,128)(2,1)S(1)} %get-tuple-element.33.refs_3_), channel_id=1, source_target_pairs={{0,1},{1,0},{2,3},{3,2},{4,5},{5,4},{6,7},{7,6},{8,9},{9,8},{10,11... | collective-permute-start | bytes 294920 | tf_op jit(solution)/shard_map/ppermute | solution.py:582

commit v10 on v8

--- a/solution.py
+++ b/solution.py
@@ -425,15 +425,15 @@
         part = [value[:, lane : lane + lanes] for value in sums]
         if lanes < LANES:
             pad = jnp.zeros((plane, LANES - lanes), F32)
-            part = [jnp.concatenate([value, pad], axis=1) for value in part]
+            part[4:] = [jnp.concatenate([value, pad], axis=1) for value in part[4:]]
         for up, z in ((0, 0), (1, last)):
             line = ends[p, pl.ds(up * plane, plane), :]
             ref[pl.ds(z, plane, stride=side), :] = line + part[4 + up]
         for up, x in ((0, 0), (1, last)):
-            ref[pl.ds(x * plane, plane), :] += part[up]
+            ref[pl.ds(x * plane, plane), 0:lanes] += part[up]
         for up, y in ((0, 0), (1, last)):
             for x in range(side):
-                ref[pl.ds(x * plane + y * side, side), :] += part[2 + up][
+                ref[pl.ds(x * plane + y * side, side), 0:lanes] += part[2 + up][
                     x * side : (x + 1) * side
                 ]
 

time: 16.1 us -> 16.2 us (level)
  no operation moved by 1% of the time
where the time goes in v10:
time: 16.2 us; the launch traced here: 16 us
  Pallas kernels  7.75 us (48%)
  starting transfers between devices  5.05 us (31%)
  waiting for transfers between devices  1.55 us (10%)
  local copies, waits for them, and re-layouts  0.94 us (6%)
  between operations  0.75 us (5%)
    pallas_call x9, Pallas kernels, call(): pl.pallas_call(kernel, out_shape=outs, in_specs=[pl.BlockSpec(memory_spac...  7.75 us
    ppermute x1, starting transfers between devices, body(): far = lax.ppermute(own_face, AXES, first)  1.81 us
    ppermute x1, starting transfers between devices, body(): hidden_far = lax.ppermute(hidden_face, AXES, second)  1.71 us
    unnamed x8, local copies, waits for them, and re-layouts  0.94 us
    ppermute x1, waiting for transfers between devices, body(): far = lax.ppermute(own_face, AXES, first)  0.71 us
    ppermute x1, waiting for transfers between devices, body(): hidden_far = lax.ppermute(hidden_face, AXES, second)  0.7 us
    ppermute x2, starting transfers between devices, body(): other = [lax.ppermute(part, AXES, halves) for part in own_parts]  0.51 us
    ppermute x2, starting transfers between devices, body(): hidden_other = [lax.ppermute(part, AXES, halves) for part in hidden]  0.51 us
  transfers between devices with their start and end apart: 9, of which 3 were waited for; matrix products, arithmetic and copies ran while one was open for 0% of the time, Pallas kernels for 38%

profile of v10, /device:TPU:8, one launch (start us, length us, event | category | flops | bytes accessed | tf_op | source)
XLA Modules:
  0.0 16.0 jit_solution(11877819138480185501)
XLA Ops:
  0.0 0.0 copy-start.2
  0.0 0.0 collective-permute-start.1
  0.0 0.9 %copy-done.2 = bf16[1,8,8,8,192]{4,3,2,1,0:T(8,128)(2,1)S(1)} copy-done((bf16[1,8,8,8,192]{4,3,2,1,0:T(8,128)(2,1)S(1)}, bf16[1,8,8,8,192]{4,3,2,1,0:T(8,128)(2,1)}, u32[]{:S(2)}) %copy-start.2) | copy-done | bytes 196632
  1.0 0.0 copy-start.3
  1.0 0.0 copy-start.1
  1.0 0.0 copy-start
  1.0 0.1 shard_map.57
  1.1 1.8 %collective-permute-start = (bf16[448,128]{1,0:T(8,128)(2,1)S(1)}, bf16[448,128]{1,0:T(8,128)(2,1)S(1)}, u32[]{:S(2)}, u32[]{:S(2)}) collective-permute-start(bf16[448,128]{1,0:T(8,128)(2,1)S(1)} %get-tuple-element.23), channel_id=1, source_target_pairs={{0,1},{31,30},{1,2},{2,0},{3,4},{4,3},{5,6},{6,5},{7,8},{8,7},{9,1... | collective-permute-start | bytes 344072 | tf_op jit(solution)/shard_map/ppermute | solution.py:523
  2.9 0.0 collective-permute-start.3
  2.9 0.5 %collective-permute-start.4 = (bf16[256,192]{1,0:T(8,128)(2,1)S(1)}, bf16[256,192]{1,0:T(8,128)(2,1)S(1)}, u32[]{:S(2)}, u32[]{:S(2)}) collective-permute-start(bf16[256,192]{1,0:T(8,128)(2,1)S(1)} %get-tuple-element.26.refs_3_), channel_id=1, source_target_pairs={{0,1},{1,0},{2,3},{3,2},{4,5},{5,4},{6,7},{7,6},{8,9},{9,8},{10,11... | collective-permute-start | bytes 294920 | tf_op jit(solution)/shard_map/ppermute | solution.py:522
  3.4 0.0 copy-done.3
  3.4 0.0 collective-permute-start.2
  3.4 0.0 collective-permute-done.1.other_ref
  3.4 0.0 copy-done.1
  3.4 0.5 %collective-permute-start.6 = (bf16[27,48,384]{2,1,0:T(8,128)(2,1)S(1)}, bf16[27,48,384]{2,1,0:T(8,128)(2,1)S(1)}, u32[]{:S(2)}, u32[]{:S(2)}) collective-permute-start(bf16[27,48,384]{2,1,0:T(8,128)(2,1)S(1)} %bitcast.9), channel_id=1, source_target_pairs={{0,1},{1,0},{2,3},{3,2},{4,5},{5,4},{6,7},{7,6},{8,9},{9,8},{10,11... | collective-permute-start | bytes 2985992 | tf_op jit(solution)/shard_map/ppermute | solution.py:527
  3.9 0.0 copy-done
  3.9 0.5 %shard_map.58.refs_6_.w = bf16[3,1728,192]{2,1,0:T(8,128)(2,1)S(1)} custom-call(bf16[27,48,384]{2,1,0:T(8,128)(2,1)S(1)} %bitcast.8, bf16[27,48,384]{2,1,0:T(8,128)(2,1)S(1)} %collective-permute-done.1.other_ref), custom_call_target="tpu_custom_call" | custom-call | tf_op jit(solution)/shard_map/pallas_call | solution.py:484
  4.4 0.1 collective-permute-done.2.refs_1_
  4.5 0.0 collective-permute-done.3.refs_4_
  4.5 0.0 collective-permute-done.4.refs_5_
  4.6 2.0 %shard_map.59 = (f32[2,512,128]{2,1,0:T(8,128)S(1)}, f32[2,1440,128]{2,1,0:T(8,128)S(1)}, f32[216,128]{1,0:T(8,128)S(1)}, f32[2,128,128]{2,1,0:T(8,128)S(1)}) custom-call(s32[1,27]{1,0:T(1,128)S(1)} %copy-done.3, s32[1,27]{1,0:T(1,128)S(1)} %collective-permute-done.2.refs_1_, bf16[256,192]{1,0:T(8,128)(2,1)S(1)} %get-tuple-element.25.refs_2_, ...), custom_call_target="tpu_custom_call" | custom-call | tf_op jit(solution)/shard_map/pallas_call | solution.py:484
  6.6 0.7 %collective-permute-done.far = bf16[448,128]{1,0:T(8,128)(2,1)S(1)} collective-permute-done((bf16[448,128]{1,0:T(8,128)(2,1)S(1)}, bf16[448,128]{1,0:T(8,128)(2,1)S(1)}, u32[]{:S(2)}, u32[]{:S(2)}) %collective-permute-start) | collective-permute-done | bytes 114720 | tf_op jit(solution)/shard_map/ppermute | solution.py:523
  7.3 1.0 %shard_map.60 = (bf16[448,128]{1,0:T(8,128)(2,1)S(1)}, bf16[256,192]{1,0:T(8,128)(2,1)S(1)}, bf16[256,192]{1,0:T(8,128)(2,1)S(1)}, f32[2,512,128]{2,1,0:T(8,128)S(1)}) custom-call(bf16[448,128]{1,0:T(8,128)(2,1)S(1)} %collective-permute-done.far, bf16[3,1728,192]{2,1,0:T(8,128)(2,1)S(1)} %shard_map.58.refs_6_.w, ...), custom_call_target="tpu_custom_call", output_to_operand_aliasing={{3}: (2, {})} | custom-call | flops 17999998976 | tf_op jit(solution)/shard_map/pallas_call | solution.py:484
  8.3 1.7 %collective-permute-start.5 = (bf16[448,128]{1,0:T(8,128)(2,1)S(1)}, bf16[448,128]{1,0:T(8,128)(2,1)S(1)}, u32[]{:S(2)}, u32[]{:S(2)}) collective-permute-start(bf16[448,128]{1,0:T(8,128)(2,1)S(1)} %get-tuple-element.31), channel_id=1, source_target_pairs={{1,0},{30,31},{0,2},{2,1},{3,4},{4,3},{5,6},{6,5},{7,8},{8,7},{9,1... | collective-permute-start | bytes 344072 | tf_op jit(solution)/shard_map/ppermute | solution.py:569
  10.0 0.0 collective-permute-start.7
  10.0 0.5 %collective-permute-start.8 = (bf16[256,192]{1,0:T(8,128)(2,1)S(1)}, bf16[256,192]{1,0:T(8,128)(2,1)S(1)}, u32[]{:S(2)}, u32[]{:S(2)}) collective-permute-start(bf16[256,192]{1,0:T(8,128)(2,1)S(1)} %get-tuple-element.33.refs_3_), channel_id=1, source_target_pairs={{0,1},{1,0},{2,3},{3,2},{4,5},{5,4},{6,7},{7,6},{8,9},{9,8},{10,11... | collective-permute-start | bytes 294920 | tf_op jit(solution)/shard_map/ppermute | solution.py:568
  11.2 0.0 collective-permute-done.6.other_ref
  11.2 0.5 %shard_map.61.refs_6_.w = bf16[3,1728,192]{2,1,0:T(8,128)(2,1)S(1)} custom-call(bf16[27,48,384]{2,1,0:T(8,128)(2,1)S(1)} %bitcast.10, bf16[27,48,384]{2,1,0:T(8,128)(2,1)S(1)} %collective-permute-done.6.other_ref), custom_call_target="tpu_custom_call" | custom-call | tf_op jit(solution)/shard_map/pallas_call | solution.py:484
  11.6 0.0 collective-permute-done.7.refs_4_
  11.7 0.0 collective-permute-done.8.refs_5_
  11.7 2.0 %shard_map.62 = (f32[2,512,128]{2,1,0:T(8,128)S(1)}, f32[2,1440,128]{2,1,0:T(8,128)S(1)}, f32[216,128]{1,0:T(8,128)S(1)}, f32[2,128,128]{2,1,0:T(8,128)S(1)}) custom-call(s32[1,27]{1,0:T(1,128)S(1)} %copy-done.3, bf16[512,192]{1,0:T(8,128)(2,1)S(1)} %bitcast.12, bf16[256,192]{1,0:T(8,128)(2,1)S(1)} %get-tuple-element.32.refs_2_, ...), custom_call_target="tpu_custom_call" | custom-call | tf_op jit(solution)/shard_map/pallas_call | solution.py:484
  13.6 0.7 %collective-permute-done.5.far = bf16[448,128]{1,0:T(8,128)(2,1)S(1)} collective-permute-done((bf16[448,128]{1,0:T(8,128)(2,1)S(1)}, bf16[448,128]{1,0:T(8,128)(2,1)S(1)}, u32[]{:S(2)}, u32[]{:S(2)}) %collective-permute-start.5) | collective-permute-done | bytes 114720 | tf_op jit(solution)/shard_map/ppermute | solution.py:569
  14.3 1.7 %shard_map.63 = (f32[512,192]{1,0:T(8,128)}, f32[2,512,128]{2,1,0:T(8,128)S(1)}) custom-call(s32[1,1]{1,0:T(1,128)} %bitcast.6.occupancy, bf16[448,128]{1,0:T(8,128)(2,1)S(1)} %collective-permute-done.5.far, bf16[3,1728,192]{2,1,0:T(8,128)(2,1)S(1)} %shard_map.61.refs_6_.w, ...), custom_call_target="tpu_custom_call", output_to_operand_aliasing={{1}: (3, {})} | custom-call | tf_op jit(solution)/shard_map/pallas_call | solution.py:484
  (2 shorter events, 0.0 us)
Async XLA Ops:
  0.0 0.9 %copy-start.2 = (bf16[1,8,8,8,192]{4,3,2,1,0:T(8,128)(2,1)S(1)}, bf16[1,8,8,8,192]{4,3,2,1,0:T(8,128)(2,1)}, u32[]{:S(2)}) copy-start(bf16[1,8,8,8,192]{4,3,2,1,0:T(8,128)(2,1)} %param.5) | copy-start | bytes 589828
  0.0 3.4 %collective-permute-start.1 = (bf16[27,48,384]{2,1,0:T(8,128)(2,1)}, bf16[27,48,384]{2,1,0:T(8,128)(2,1)S(1)}, u32[]{:S(2)}, u32[]{:S(2)}) collective-permute-start(bf16[27,48,384]{2,1,0:T(8,128)(2,1)} %bitcast.7), channel_id=1, source_target_pairs={{0,1},{1,0},{2,3},{3,2},{4,5},{5,4},{6,7},{7,6},{8,9},{9,8},{10,11... | collective-permute-start | bytes 2985992 | tf_op jit(solution)/shard_map/ppermute | solution.py:527
  1.0 2.5 %copy-start.3 = (s32[1,27]{1,0:T(1,128)S(1)}, s32[1,27]{1,0:T(1,128)}, u32[]{:S(2)}) copy-start(s32[1,27]{1,0:T(1,128)} %refs_0_.3) | copy-start | bytes 328
  1.0 2.5 %copy-start.1 = (bf16[3,3,3,48,384]{4,3,2,1,0:T(8,128)(2,1)S(1)}, bf16[3,3,3,48,384]{4,3,2,1,0:T(8,128)(2,1)}, u32[]{:S(2)}) copy-start(bf16[3,3,3,48,384]{4,3,2,1,0:T(8,128)(2,1)} %param.9) | copy-start | bytes 2985988
  1.0 3.0 %copy-start = (bf16[3,3,3,48,384]{4,3,2,1,0:T(8,128)(2,1)S(1)}, bf16[3,3,3,48,384]{4,3,2,1,0:T(8,128)(2,1)}, u32[]{:S(2)}) copy-start(bf16[3,3,3,48,384]{4,3,2,1,0:T(8,128)(2,1)} %param.8) | copy-start | bytes 2985988
  1.1 6.2 %collective-permute-start = (bf16[448,128]{1,0:T(8,128)(2,1)S(1)}, bf16[448,128]{1,0:T(8,128)(2,1)S(1)}, u32[]{:S(2)}, u32[]{:S(2)}) collective-permute-start(bf16[448,128]{1,0:T(8,128)(2,1)S(1)} %get-tuple-element.23), channel_id=1, source_target_pairs={{0,1},{31,30},{1,2},{2,0},{3,4},{4,3},{5,6},{6,5},{7,8},{8,7},{9,1... | collective-permute-start | bytes 344072 | tf_op jit(solution)/shard_map/ppermute | solution.py:523
  2.9 1.6 %collective-permute-start.3 = (bf16[256,192]{1,0:T(8,128)(2,1)S(1)}, bf16[256,192]{1,0:T(8,128)(2,1)S(1)}, u32[]{:S(2)}, u32[]{:S(2)}) collective-permute-start(bf16[256,192]{1,0:T(8,128)(2,1)S(1)} %get-tuple-element.25.refs_2_), channel_id=1, source_target_pairs={{0,1},{1,0},{2,3},{3,2},{4,5},{5,4},{6,7},{7,6},{8,9},{9,8},{10,11... | collective-permute-start | bytes 294920 | tf_op jit(solution)/shard_map/ppermute | solution.py:522
  2.9 1.6 %collective-permute-start.4 = (bf16[256,192]{1,0:T(8,128)(2,1)S(1)}, bf16[256,192]{1,0:T(8,128)(2,1)S(1)}, u32[]{:S(2)}, u32[]{:S(2)}) collective-permute-start(bf16[256,192]{1,0:T(8,128)(2,1)S(1)} %get-tuple-element.26.refs_3_), channel_id=1, source_target_pairs={{0,1},{1,0},{2,3},{3,2},{4,5},{5,4},{6,7},{7,6},{8,9},{9,8},{10,11... | collective-permute-start | bytes 294920 | tf_op jit(solution)/shard_map/ppermute | solution.py:522
  3.4 1.1 %collective-permute-start.2 = (s32[1,27]{1,0:T(1,128)S(1)}, s32[1,27]{1,0:T(1,128)S(1)}, u32[]{:S(2)}, u32[]{:S(2)}) collective-permute-start(s32[1,27]{1,0:T(1,128)S(1)} %copy-done.3), channel_id=1, source_target_pairs={{0,1},{1,0},{2,3},{3,2},{4,5},{5,4},{6,7},{7,6},{8,9},{9,8},{10,11... | collective-permute-start | bytes 332 | tf_op jit(solution)/shard_map/ppermute | solution.py:521
  3.4 7.7 %collective-permute-start.6 = (bf16[27,48,384]{2,1,0:T(8,128)(2,1)S(1)}, bf16[27,48,384]{2,1,0:T(8,128)(2,1)S(1)}, u32[]{:S(2)}, u32[]{:S(2)}) collective-permute-start(bf16[27,48,384]{2,1,0:T(8,128)(2,1)S(1)} %bitcast.9), channel_id=1, source_target_pairs={{0,1},{1,0},{2,3},{3,2},{4,5},{5,4},{6,7},{7,6},{8,9},{9,8},{10,11... | collective-permute-start | bytes 2985992 | tf_op jit(solution)/shard_map/ppermute | solution.py:527
  8.3 6.1 %collective-permute-start.5 = (bf16[448,128]{1,0:T(8,128)(2,1)S(1)}, bf16[448,128]{1,0:T(8,128)(2,1)S(1)}, u32[]{:S(2)}, u32[]{:S(2)}) collective-permute-start(bf16[448,128]{1,0:T(8,128)(2,1)S(1)} %get-tuple-element.31), channel_id=1, source_target_pairs={{1,0},{30,31},{0,2},{2,1},{3,4},{4,3},{5,6},{6,5},{7,8},{8,7},{9,1... | collective-permute-start | bytes 344072 | tf_op jit(solution)/shard_map/ppermute | solution.py:569
  10.0 1.7 %collective-permute-start.7 = (bf16[256,192]{1,0:T(8,128)(2,1)S(1)}, bf16[256,192]{1,0:T(8,128)(2,1)S(1)}, u32[]{:S(2)}, u32[]{:S(2)}) collective-permute-start(bf16[256,192]{1,0:T(8,128)(2,1)S(1)} %get-tuple-element.32.refs_2_), channel_id=1, source_target_pairs={{0,1},{1,0},{2,3},{3,2},{4,5},{5,4},{6,7},{7,6},{8,9},{9,8},{10,11... | collective-permute-start | bytes 294920 | tf_op jit(solution)/shard_map/ppermute | solution.py:568
  10.0 1.7 %collective-permute-start.8 = (bf16[256,192]{1,0:T(8,128)(2,1)S(1)}, bf16[256,192]{1,0:T(8,128)(2,1)S(1)}, u32[]{:S(2)}, u32[]{:S(2)}) collective-permute-start(bf16[256,192]{1,0:T(8,128)(2,1)S(1)} %get-tuple-element.33.refs_3_), channel_id=1, source_target_pairs={{0,1},{1,0},{2,3},{3,2},{4,5},{5,4},{6,7},{7,6},{8,9},{9,8},{10,11... | collective-permute-start | bytes 294920 | tf_op jit(solution)/shard_map/ppermute | solution.py:568
